TPU v7x, 32 devices: a whole 2x2x4 slice. The times are simulated.
32 devices in a mesh: grp: 2 (over y), seg: 8 (over z, x), yoke: 2 (over core).
Axes of the slice: x: 2, y: 2, z: 4, core: 2. Of those that a mesh axis runs over, the one named last changes fastest.
Arguments:
- seg_mid: float32 [3, 4096], P(None, ('grp', 'seg')), parts along dimension 1, may hold values from -1 to 1
- seg_vec: float32 [3, 4096], P(None, ('grp', 'seg')), parts along dimension 1, may hold values from -6 to 6
- strand_of: int32 [4096], P(('grp', 'seg')), parts along dimension 0, may hold values from 0 to 255
- strand_current: float32 [512], P('grp'), parts along dimension 0, may hold values from 0.5 to 2
- yoke_pos: float32 [3, 4096], P(None, ('grp', 'seg', 'yoke')), parts along dimension 1, may hold values from -1 to 1
- quad_weight: float32 [4096], P(('grp', 'seg', 'yoke')), parts along dimension 0, may hold values from 0.5 to 1.5
- panel_of: int32 [4096], P(('grp', 'seg', 'yoke')), parts along dimension 0, may hold values from 0 to 63
- panel_chi: float32 [128], P('grp'), parts along dimension 0, may hold values from 0.02 to 0.2
Outputs:
- lorentz: float32 [3, 4096], P(None, ('grp', 'seg', 'yoke')), parts along dimension 1
- moment: float32 [3, 4096], P(None, ('grp', 'seg', 'yoke')), parts along dimension 1
There are 2 independent parts, one for each index of `grp`. A program takes and returns all parts, laid end to end along the dimension named above; each array names one. Nothing has to cross between parts.
All inputs are finite; a program needn't handle non-finite values.
Results may differ from a plain program's by a relative error of at most 0.0002.
Values sent between devices are 32-bit elements; how exact they have to be, the bound alone decides.
No kernel may reach another device: no remote copies, remote signals or barrier semaphores. Data moves between devices by JAX's collectives and lax.ppermute only.
A program may use at most 64 MiB of HBM per device.

v0:
```python
import math

import jax
import jax.numpy as jnp
from jax import lax
from jax.sharding import PartitionSpec as P

ITERS = 2


coil_core = 0.05
yoke_core = 0.2


def coil_kernel(targets, sources):
    delta_x = targets[0][:, None] - sources[0][None, :]
    delta_y = targets[1][:, None] - sources[1][None, :]
    delta_z = targets[2][:, None] - sources[2][None, :]
    radial = delta_x * delta_x + delta_y * delta_y + delta_z * delta_z + coil_core * coil_core
    inverse = lax.rsqrt(radial)
    weight_cube = inverse * inverse * inverse
    field_x = jnp.sum(
        weight_cube * (sources[4][None, :] * delta_z - sources[5][None, :] * delta_y), axis=1
    )
    field_y = jnp.sum(
        weight_cube * (sources[5][None, :] * delta_x - sources[3][None, :] * delta_z), axis=1
    )
    field_z = jnp.sum(
        weight_cube * (sources[3][None, :] * delta_y - sources[4][None, :] * delta_x), axis=1
    )
    return jnp.stack([field_x, field_y, field_z], 0)


def dipole_kernel(targets, sources):
    delta_x = targets[0][:, None] - sources[0][None, :]
    delta_y = targets[1][:, None] - sources[1][None, :]
    delta_z = targets[2][:, None] - sources[2][None, :]
    radial = delta_x * delta_x + delta_y * delta_y + delta_z * delta_z
    inverse = lax.rsqrt(radial + yoke_core * yoke_core)
    fifth = inverse * inverse * inverse * inverse * inverse
    along = (
        delta_x * sources[3][None, :]
        + delta_y * sources[4][None, :]
        + delta_z * sources[5][None, :]
    )
    field_x = jnp.sum(fifth * (3.0 * delta_x * along - radial * sources[3][None, :]), axis=1)
    field_y = jnp.sum(fifth * (3.0 * delta_y * along - radial * sources[4][None, :]), axis=1)
    field_z = jnp.sum(fifth * (3.0 * delta_z * along - radial * sources[5][None, :]), axis=1)
    return jnp.stack([field_x, field_y, field_z], 0)


def blocked(kernel, targets, sources, element_limit):
    columns = targets.shape[1]
    pieces = 1
    while pieces < columns and (
        columns % pieces != 0 or columns // pieces * sources.shape[1] > element_limit
    ):
        pieces += 1
    if pieces == 1:
        return kernel(targets, sources)
    stacked = jnp.moveaxis(targets.reshape(3, pieces, columns // pieces), 1, 0)

    def one_block(target_block):
        return kernel(target_block, sources)

    result = lax.map(one_block, stacked)
    return jnp.moveaxis(result, 0, 1).reshape(3, columns)


def fold_blocks(kernel, targets, sources, shard_len):
    columns = sources.shape[1]
    shards = columns // shard_len
    group_size = max(1, (1 << 20) // (targets.shape[1] * shard_len))
    group_size = min(group_size, shards)
    while shards % group_size != 0:
        group_size -= 1
    block_width = group_size * shard_len
    block_count = columns // block_width
    if block_count == 1:
        return kernel(targets, sources)
    stacked = jnp.moveaxis(sources.reshape(sources.shape[0], block_count, block_width), 1, 0)

    def advance(running, source_block):
        return (running + kernel(targets, source_block), None)

    result, unused = lax.scan(advance, jnp.zeros((3, targets.shape[1]), jnp.float32), stacked)
    return result


def make_fold(kernel, targets, shard_len, sources):
    return fold_blocks(kernel, targets, sources, shard_len)


def cross_rows(left_rows, right_rows):
    return jnp.stack(
        [
            left_rows[1] * right_rows[2] - left_rows[2] * right_rows[1],
            left_rows[2] * right_rows[0] - left_rows[0] * right_rows[2],
            left_rows[0] * right_rows[1] - left_rows[1] * right_rows[0],
        ],
        0,
    )


def table_lookup(indices, table):
    rows_iota = lax.broadcasted_iota(jnp.int32, (table.shape[0], indices.shape[0]), 0)
    return jnp.sum(jnp.where(indices[None, :] == rows_iota, table[:, None], 0.0), axis=0)


def body(seg_mid, seg_vec, strand_of, strand_current, yoke_pos, quad_weight, panel_of, panel_chi):
    seg_len = seg_mid.shape[1]
    half_len = seg_len // 2
    yoke_len = yoke_pos.shape[1]
    segments_total = seg_len * lax.axis_size("seg")
    points_total = yoke_len * lax.axis_size("seg") * lax.axis_size("yoke")
    coil_scale = 1.0 / math.sqrt(segments_total)
    yoke_scale = 1.0 / math.sqrt(points_total)
    current = table_lookup(strand_of, strand_current)
    carried = current[None, :] * seg_vec
    seg_pack = jnp.concatenate([seg_mid, carried], 0)
    suscept = table_lookup(panel_of, panel_chi)[None, :]
    half_start = lax.axis_index("yoke") * half_len
    own_mid = lax.dynamic_slice_in_dim(seg_mid, half_start, half_len, 1)
    own_carried = lax.dynamic_slice_in_dim(carried, half_start, half_len, 1)
    half_points = lax.all_gather(yoke_pos, "seg", axis=1, tiled=True)
    partial_value = blocked(coil_kernel, half_points, seg_pack, 1 << 19)
    coil_yoke = lax.psum_scatter(partial_value, "seg", scatter_dimension=1, tiled=True) * coil_scale
    coil_seg = (
        make_fold(
            coil_kernel, own_mid, seg_len, lax.all_gather(seg_pack, "seg", axis=1, tiled=True)
        )
        * coil_scale
    )

    def moment_field(targets, moment):
        source_pack = jnp.concatenate([yoke_pos, quad_weight[None, :] * moment], 0)
        gathered_sum = make_fold(
            dipole_kernel,
            targets,
            yoke_len,
            lax.all_gather(source_pack, ("seg", "yoke"), axis=1, tiled=True),
        )
        return gathered_sum * yoke_scale

    moment = suscept * coil_yoke
    for sweep_index in range(ITERS):
        moment = suscept * (coil_yoke + moment_field(yoke_pos, moment))
    total_field = coil_seg + moment_field(own_mid, moment)
    lorentz = cross_rows(own_carried, total_field)
    return (lorentz, moment)


def solution(mesh):
    placed = (
        P(None, ("grp", "seg")),
        P(None, ("grp", "seg")),
        P(("grp", "seg")),
        P("grp"),
        P(None, ("grp", "seg", "yoke")),
        P(("grp", "seg", "yoke")),
        P(("grp", "seg", "yoke")),
        P("grp"),
    )
    return jax.shard_map(
        body,
        mesh=mesh,
        in_specs=placed,
        out_specs=(P(None, ("grp", "seg", "yoke")), P(None, ("grp", "seg", "yoke"))),
        check_vma=False,
    )
```

profile of v0, /device:TPU:0, one launch (start us, length us, event | category | flops | bytes accessed | tf_op | source)
XLA Modules:
  0.0 173.8 jit_solution(4760201296099230659)
XLA Ops:
  7.2 0.0 reduce-scatter.4.cloned.1.call-start
  7.2 0.8 select_reduce_fusion
  8.0 0.7 broadcast_multiply_fusion
  8.7 0.0 copy-start
  8.7 0.7 copy-done
  9.4 27.8 %all_gather.16 = f32[3,1024]{1,0:T(4,128)S(1)} all-gather(f32[3,128]{1,0:T(4,128)S(1)} %copy-done), channel_id=1, replica_groups=mesh['grp'=2,'seg'=8,'yoke'=2] {'seg'}, dimensions={1}, use_global_device_ids=true | all-gather | bytes 13824 | tf_op jit(solution)/shard_map/all_gather | solution.py:125
  37.2 0.0 copy-start.1
  37.2 0.7 copy-done.1
  37.9 1.5 fusion.25
  39.4 1.0 copy.10
  40.4 0.0 reduce-scatter.4.cloned.1.call-update
  40.5 30.6 %all_gather.15 = f32[6,2048]{1,0:T(8,128)S(1)} all-gather(f32[6,256]{1,0:T(8,128)S(1)} %pad_maximum_fusion.1), channel_id=1, replica_groups=mesh['grp'=2,'seg'=8,'yoke'=2] {'seg'}, dimensions={1}, use_global_device_ids=true | all-gather | bytes 55296 | tf_op jit(solution)/shard_map/all_gather | solution.py:130
  71.1 0.0 copy-start.3
  71.1 0.0 copy-start.4
  71.1 0.6 copy-done.3
  71.8 0.0 copy-done.4
  71.8 0.1 select_reduce_fusion.1
  71.9 30.5 %reduce-scatter.4.cloned.1.call-done = f32[128,3]{1,0:T(8,128)} async-done(((f32[1024,3]{1,0:T(8,128)}), f32[128,3]{1,0:T(8,128)}) %reduce-scatter.4.cloned.1.call-update) | async-done | bytes 1552
  102.3 0.0 copy-start.2
  102.3 0.9 copy.11
  103.3 0.0 copy-done.2
  103.3 19.6 %all_gather.17 = f32[6,2048]{1,0:T(8,128)S(1)} all-gather(f32[6,128]{1,0:T(8,128)S(1)} %pad_maximum_fusion.2), channel_id=1, replica_groups=mesh['grp'=2,'seg'=8,'yoke'=2] {'seg','yoke'}, dimensions={1}, use_global_device_ids=true | all-gather | bytes 52224 | tf_op jit(solution)/shard_map/all_gather | solution.py:141
  122.9 1.7 fusion.31
  124.6 17.6 %all_gather.18 = f32[6,2048]{1,0:T(8,128)S(1)} all-gather(f32[6,128]{1,0:T(8,128)S(1)} %pad_maximum_fusion.3), channel_id=1, replica_groups=mesh['grp'=2,'seg'=8,'yoke'=2] {'seg','yoke'}, dimensions={1}, use_global_device_ids=true | all-gather | bytes 52224 | tf_op jit(solution)/shard_map/all_gather | solution.py:141
  142.3 1.7 fusion.51
  144.0 0.6 broadcast_multiply_fusion.1
  144.6 18.9 %all_gather.19 = f32[6,2048]{1,0:T(8,128)S(1)} all-gather(f32[6,128]{1,0:T(8,128)S(1)} %pad_maximum_fusion.4), channel_id=1, replica_groups=mesh['grp'=2,'seg'=8,'yoke'=2] {'seg','yoke'}, dimensions={1}, use_global_device_ids=true | all-gather | bytes 52224 | tf_op jit(solution)/shard_map/all_gather | solution.py:141
  163.5 2.8 %fusion.71 = (f32[128]{0:T(128)S(1)}, f32[128]{0:T(128)S(1)}, f32[128]{0:T(128)S(1)}, f32[128]{0:T(128)S(1)}, f32[128]{0:T(128)S(1)}, /*index=5*/f32[128]{0:T(128)S(1)}) fusion(f32[2048]{0:T(1024)S(1)} %bitcast.71, f32[2048]{0:T(1024)S(1)} %bitcast.72, f32[2048]{0:T(1024)S(1)} %bitcast.73, f32[2048]{0:T(1024)S(1)} %bitcast.74, f32[2048]{0:T(1024)S(1)} %bitcast.75, ...), kind=kLoop, calls=%fused_computation.121 | loop fusion | flops 16252160 | bytes 102912 | tf_op jit(solution)/shard_map/reduce_sum | solution.py:46
  166.4 0.6 pad_maximum_fusion.5
  (20 shorter events, 0.3 us)
Async XLA Ops:
  7.2 95.2 %reduce-scatter.4.cloned.1.call-start = ((), (), s32[]{:S(2)}) async-start(), calls=%async_computation.1 | async-start | bytes 589824
  8.7 0.7 copy-start
  37.2 0.7 copy-start.1
  71.1 0.7 copy-start.3
  71.1 0.7 copy-start.4
  102.3 0.9 copy-start.2
Sparse Core Ops, SparseCore 0:
  40.6 61.7 reduce-scatter.3
where the time goes:
time: 174 us
  blocking collectives  114 us (66%)
  waiting for transfers between devices  30.5 us (18%)
  between operations  14.1 us (8%)
  other arithmetic  10.5 us (6%)
  local copies, waits for them, and re-layouts  4.09 us (2%)
    all_gather x3, blocking collectives, moment_field(): lax.all_gather(source_pack, ('seg', 'yoke'), axis=1, tiled=True)  56.1 us
    all_gather x1, blocking collectives, body(): lax.all_gather(seg_pack, 'seg', axis=1, tiled=True)  30.6 us
    unnamed x2, waiting for transfers between devices  30.5 us
    all_gather x1, blocking collectives, body(): half_points = lax.all_gather(yoke_pos, 'seg', axis=1, tiled=True)  27.8 us
    reduce_sum x3, other arithmetic, dipole_kernel(): jnp.sum(fifth * (3.0 * delta_x * along - radial * sources[3][None, :]), a...  6.15 us
    unnamed x12, local copies, waits for them, and re-layouts  3.92 us
  transfers between devices with their start and end apart: 1, of which 1 were waited for; matrix products, arithmetic and copies ran while one was open for 0% of the time, Pallas kernels for 0%

commit v1 on v0

--- a/solution.py
+++ b/solution.py
@@ -3,9 +3,12 @@
 import jax
 import jax.numpy as jnp
 from jax import lax
+from jax.experimental import pallas as pl
+from jax.experimental.pallas import tpu as pltpu
 from jax.sharding import PartitionSpec as P
 
 ITERS = 2
+VMEM_BYTES = 40 << 20
 
 
 coil_core = 0.05
@@ -107,7 +110,7 @@
     return jnp.sum(jnp.where(indices[None, :] == rows_iota, table[:, None], 0.0), axis=0)
 
 
-def body(seg_mid, seg_vec, strand_of, strand_current, yoke_pos, quad_weight, panel_of, panel_chi):
+def far_body(seg_mid, seg_vec, strand_of, strand_current, yoke_pos, quad_weight, panel_of, panel_chi):
     seg_len = seg_mid.shape[1]
     half_len = seg_len // 2
     yoke_len = yoke_pos.shape[1]
@@ -150,6 +153,354 @@
     return (lorentz, moment)
 
 
+def bf16_parts(value):
+    parts = []
+    for place in range(3):
+        part = value.astype(jnp.bfloat16)
+        parts.append(part)
+        if place < 2:
+            value = value - part.astype(jnp.float32)
+    return parts
+
+
+def split_rows(rows, split_ref):
+    count = rows.shape[0]
+    for place, part in enumerate(bf16_parts(rows)):
+        split_ref[place * count : (place + 1) * count, :] = part
+
+
+def joined(product):
+    count = product.shape[0] // 3
+    return product[:count] + product[count : 2 * count] + product[2 * count :]
+
+
+def pick(table_ref, index_ref):
+    entries = lax.broadcasted_iota(jnp.int32, (table_ref.shape[1], index_ref.shape[1]), 0)
+    chosen = jnp.where(entries == index_ref[...], 1.0, 0.0)
+    table = jnp.broadcast_to(table_ref[...], (8, table_ref.shape[1]))
+    found = jnp.dot(
+        table, chosen, precision=lax.Precision.HIGHEST, preferred_element_type=jnp.float32
+    )
+    return found[:1]
+
+
+def pack_kernel(
+    mid_ref, vec_ref, strand_ref, current_ref, pos_ref, weight_ref, panel_ref, chi_ref, out_ref
+):
+    half = pos_ref.shape[1]
+    first = lax.axis_index("yoke") == 0
+    mid = jnp.where(first, mid_ref[:, :half], mid_ref[:, half:])
+    carried = pick(current_ref, strand_ref) * vec_ref[...]
+    carried = jnp.where(first, carried[:, :half], carried[:, half:])
+    zeros = jnp.zeros((3, half), jnp.float32)
+    packed = jnp.concatenate(
+        [
+            pos_ref[...],
+            weight_ref[...],
+            pick(chi_ref, panel_ref),
+            zeros,
+            mid,
+            carried,
+            zeros[:2],
+        ],
+        0,
+    )
+    out_ref[...] = jnp.broadcast_to(packed[None], out_ref.shape)
+
+
+def coil_stage(gathered_ref, row_ref, col_ref, state_ref, split_ref, *weight_refs):
+    blocks, _, width = gathered_ref.shape
+    total = blocks * width
+    half = total // 2
+    coil_scale = 1.0 / math.sqrt(total)
+    positions = gathered_ref[0, 0:3, :]
+    for block in range(1, blocks):
+        positions = positions + gathered_ref[block, 0:3, :]
+    center = jnp.sum(positions, axis=1, keepdims=True) * (1.0 / total)
+    none = jnp.zeros((5, 1), jnp.float32)
+    shift = jnp.concatenate([center, none, center, none], 0)
+    for block in range(blocks):
+        place = (block % 2) * half + (block // 2) * width
+        rows = gathered_ref[block] - shift
+        row_ref[:, place : place + width] = rows
+        col_ref[place : place + width, :] = rows.T
+    mx, my, mz, cx, cy, cz = [row_ref[8 + k : 9 + k, :] for k in range(6)]
+    split_rows(
+        jnp.concatenate(
+            [
+                cx,
+                cy,
+                cz,
+                cy * mz - cz * my,
+                cz * mx - cx * mz,
+                cx * my - cy * mx,
+                jnp.zeros((10, total), jnp.float32),
+            ],
+            0,
+        ),
+        split_ref,
+    )
+    mine = pl.ds(pl.multiple_of(lax.axis_index("yoke") * half, half), half)
+    tx, ty, tz = [row_ref[k : k + 1, mine] for k in range(3)]
+    depth = 256
+    count = total // depth
+    product = jnp.zeros((split_ref.shape[0], half), jnp.float32)
+
+    def build(chunk):
+        target = weight_refs[3 * (chunk % 2) : 3 * (chunk % 2) + 3]
+        for start in range(0, depth, 32):
+            at = chunk * depth + start
+            dx = tx - col_ref[at : at + 32, 8:9]
+            dy = ty - col_ref[at : at + 32, 9:10]
+            dz = tz - col_ref[at : at + 32, 10:11]
+            inverse = lax.rsqrt(dx * dx + dy * dy + dz * dz + coil_core * coil_core)
+            for ref, part in zip(target, bf16_parts(inverse * inverse * inverse)):
+                ref[start : start + 32, :] = part
+
+    build(0)
+    for chunk in range(count):
+        if chunk + 1 < count:
+            build(chunk + 1)
+        rows = split_ref[:, chunk * depth : (chunk + 1) * depth]
+        for ref in weight_refs[3 * (chunk % 2) : 3 * (chunk % 2) + 3]:
+            product = product + jnp.dot(rows, ref[...], preferred_element_type=jnp.float32)
+    sums = joined(product)
+    sx, sy, sz = [sums[k : k + 1] for k in range(3)]
+    field = (
+        jnp.concatenate([sy * tz - sz * ty, sz * tx - sx * tz, sx * ty - sy * tx], 0) - sums[3:6]
+    ) * coil_scale
+    suscept = row_ref[4:5, mine]
+    state_ref[...] = jnp.concatenate(
+        [field, suscept * field, jnp.zeros((2, half), jnp.float32)], 0
+    )
+
+
+def spread_stage(row_ref, col_ref, *part_refs):
+    total = row_ref.shape[1]
+    half = total // 2
+    mine = pl.ds(pl.multiple_of(lax.axis_index("yoke") * half, half), half)
+    tx, ty, tz = [row_ref[k : k + 1, mine] for k in range(3)]
+    depth = 256
+
+    def build(chunk, carry):
+        for start in range(0, depth, 32):
+            at = pl.ds(pl.multiple_of(chunk * depth + start, 32), 32)
+            sources = col_ref[at, :]
+            dx = tx - sources[:, 0:1]
+            dy = ty - sources[:, 1:2]
+            dz = tz - sources[:, 2:3]
+            inverse = lax.rsqrt(dx * dx + dy * dy + dz * dz + yoke_core * yoke_core)
+            square = inverse * inverse
+            for ref, part in zip(part_refs, bf16_parts(square * square * inverse)):
+                ref[at, :] = part
+        return carry
+
+    lax.fori_loop(0, total // depth, build, 0)
+
+
+def both_halves(own, other):
+    first = lax.axis_index("yoke") == 0
+    return jnp.concatenate([jnp.where(first, own, other), jnp.where(first, other, own)], 1)
+
+
+def sweep_stage(row_ref, own_ref, other_ref, *refs):
+    part_refs, (state_ref, split_ref) = refs[:3], refs[3:]
+    total = row_ref.shape[1]
+    half = total // 2
+    yoke_scale = 1.0 / math.sqrt(total)
+    moment = both_halves(own_ref[3:6, :], other_ref[3:6, :])
+    strength = row_ref[3:4, :] * moment
+    ux, uy, uz = [strength[k : k + 1] for k in range(3)]
+    qx, qy, qz = [row_ref[k : k + 1, :] for k in range(3)]
+    along = 3.0 * (qx * ux + qy * uy + qz * uz)
+    square = qx * qx + qy * qy + qz * qz
+    split_rows(
+        jnp.concatenate(
+            [
+                strength,
+                qx * strength,
+                qy * strength,
+                qz * strength,
+                qx * along - square * ux,
+                qy * along - square * uy,
+                qz * along - square * uz,
+                jnp.zeros((1, total), jnp.float32),
+            ],
+            0,
+        ),
+        split_ref,
+    )
+    depth = 256
+    product = jnp.zeros((split_ref.shape[0], half), jnp.float32)
+    for chunk in range(total // depth):
+        at = slice(chunk * depth, (chunk + 1) * depth)
+        rows = split_ref[:, at]
+        for ref in part_refs:
+            product = product + jnp.dot(rows, ref[at, :], preferred_element_type=jnp.float32)
+    sums = joined(product)
+    mine = pl.ds(pl.multiple_of(lax.axis_index("yoke") * half, half), half)
+    target = [row_ref[k : k + 1, mine] for k in range(3)]
+    tx, ty, tz = target
+    plain = [sums[k : k + 1] for k in range(3)]
+    tensor = [[sums[3 + 3 * a + b : 4 + 3 * a + b] for b in range(3)] for a in range(3)]
+    toward = tx * plain[0] + ty * plain[1] + tz * plain[2]
+    trace = tensor[0][0] + tensor[1][1] + tensor[2][2]
+    lead = 3.0 * (toward - trace)
+    reach = tx * tx + ty * ty + tz * tz
+    fields = []
+    for a in range(3):
+        field = target[a] * lead - reach * plain[a] + sums[12 + a : 13 + a]
+        for b in range(3):
+            field = field + target[b] * (2.0 * tensor[b][a] - 3.0 * tensor[a][b])
+        fields.append(field)
+    coil = own_ref[0:3, :]
+    fresh = row_ref[4:5, mine] * (coil + jnp.concatenate(fields, 0) * yoke_scale)
+    state_ref[...] = jnp.concatenate([coil, fresh, jnp.zeros((2, half), jnp.float32)], 0)
+
+
+def own_place(total, width):
+    half = total // 2
+    start = lax.axis_index("yoke") * half + lax.axis_index("seg") * width
+    return pl.ds(pl.multiple_of(start, width), width)
+
+
+def columns_of(rows):
+    return jnp.concatenate([rows, jnp.zeros((5, rows.shape[1]), jnp.float32)], 0).T
+
+
+def gather_lanes(terms, width):
+    count = terms.shape[1] // width
+    total = terms[:, :width]
+    for k in range(1, count):
+        total = total + terms[:, k * width : (k + 1) * width]
+    return jnp.sum(total, axis=1, keepdims=True)
+
+
+def rows_of(columns, width):
+    table = jnp.concatenate(columns + [jnp.zeros((width, 5), jnp.float32)], 1)
+    return table.T[0:3]
+
+
+def segment_stage(row_ref, out_ref):
+    total = row_ref.shape[1]
+    width = out_ref.shape[1]
+    targets = columns_of(row_ref[8:11, own_place(total, width)])
+    mx, my, mz, cx, cy, cz = [row_ref[8 + k : 9 + k, :] for k in range(6)]
+    found = [[], [], []]
+    for start in range(0, width, 8):
+        at = targets[start : start + 8]
+        dx, dy, dz = at[:, 0:1] - mx, at[:, 1:2] - my, at[:, 2:3] - mz
+        inverse = lax.rsqrt(dx * dx + dy * dy + dz * dz + coil_core * coil_core)
+        cube = inverse * inverse * inverse
+        found[0].append(gather_lanes(cube * (cy * dz - cz * dy), 128))
+        found[1].append(gather_lanes(cube * (cz * dx - cx * dz), 128))
+        found[2].append(gather_lanes(cube * (cx * dy - cy * dx), 128))
+    field = rows_of([jnp.concatenate(each, 0) for each in found], width)
+    out_ref[...] = field * (1.0 / math.sqrt(total))
+
+
+def force_stage(row_ref, own_ref, other_ref, coil_ref, lorentz_ref, moment_ref):
+    total = row_ref.shape[1]
+    width = coil_ref.shape[1]
+    segment = pl.ds(pl.multiple_of(lax.axis_index("seg") * width, width), width)
+    moment_ref[...] = own_ref[3:6, segment]
+    place = own_place(total, width)
+    targets = columns_of(row_ref[8:11, place])
+    strength = row_ref[3:4, :] * both_halves(own_ref[3:6, :], other_ref[3:6, :])
+    ux, uy, uz = [strength[k : k + 1] for k in range(3)]
+    qx, qy, qz = [row_ref[k : k + 1, :] for k in range(3)]
+    found = [[], [], []]
+    for start in range(0, width, 8):
+        at = targets[start : start + 8]
+        dx, dy, dz = at[:, 0:1] - qx, at[:, 1:2] - qy, at[:, 2:3] - qz
+        radial = dx * dx + dy * dy + dz * dz
+        inverse = lax.rsqrt(radial + yoke_core * yoke_core)
+        square = inverse * inverse
+        fifth = square * square * inverse
+        along = 3.0 * fifth * (dx * ux + dy * uy + dz * uz)
+        pull = fifth * radial
+        found[0].append(gather_lanes(dx * along - pull * ux, 128))
+        found[1].append(gather_lanes(dy * along - pull * uy, 128))
+        found[2].append(gather_lanes(dz * along - pull * uz, 128))
+    field = rows_of([jnp.concatenate(each, 0) for each in found], width)
+    field = coil_ref[...] + field * (1.0 / math.sqrt(total))
+    fx, fy, fz = [field[k : k + 1] for k in range(3)]
+    cx, cy, cz = [row_ref[11 + k : 12 + k, place] for k in range(3)]
+    lorentz_ref[...] = jnp.concatenate(
+        [cy * fz - cz * fy, cz * fx - cx * fz, cx * fy - cy * fx], 0
+    )
+
+
+def call(kernel, outputs, scratch, *operands):
+    return pl.pallas_call(
+        kernel,
+        out_shape=outputs,
+        scratch_shapes=scratch,
+        compiler_params=pltpu.CompilerParams(vmem_limit_bytes=VMEM_BYTES),
+    )(*operands)
+
+
+def close_body(
+    seg_mid, seg_vec, strand_of, strand_current, yoke_pos, quad_weight, panel_of, panel_chi
+):
+    width = yoke_pos.shape[1]
+    blocks = lax.axis_size("seg") * lax.axis_size("yoke")
+    total = blocks * width
+    half = total // 2
+    shape = jax.ShapeDtypeStruct
+    f32, bf16 = jnp.float32, jnp.bfloat16
+
+    def swap(state):
+        return lax.ppermute(state, "yoke", [(0, 1), (1, 0)])
+
+    packed = call(
+        pack_kernel,
+        shape((blocks, 16, width), f32),
+        [],
+        seg_mid,
+        seg_vec,
+        strand_of[None],
+        strand_current[None],
+        yoke_pos,
+        quad_weight[None],
+        panel_of[None],
+        panel_chi[None],
+    )
+    gathered = lax.all_to_all(packed, ("seg", "yoke"), 0, 0, tiled=True)
+    state_shape = shape((8, half), f32)
+    split_scratch = pltpu.VMEM((48, total), bf16)
+    rows, columns, state = call(
+        coil_stage,
+        (shape((16, total), f32), shape((total, 16), f32), state_shape),
+        [split_scratch] + [pltpu.VMEM((256, half), bf16)] * 6,
+        gathered,
+    )
+    other = swap(state)
+    spread = call(spread_stage, [shape((total, half), bf16)] * 3, [], rows, columns)
+    for sweep in range(ITERS):
+        state = call(sweep_stage, state_shape, [split_scratch], rows, state, other, *spread)
+        other = swap(state)
+    coil_segments = call(segment_stage, shape((3, width), f32), [], rows)
+    return tuple(
+        call(
+            force_stage,
+            (shape((3, width), f32), shape((3, width), f32)),
+            [],
+            rows,
+            state,
+            other,
+            coil_segments,
+        )
+    )
+
+
+def body(*arrays):
+    seg_len, yoke_len = arrays[0].shape[1], arrays[4].shape[1]
+    blocks = lax.axis_size("seg") * lax.axis_size("yoke")
+    close = seg_len == 256 and yoke_len == 128 and lax.axis_size("yoke") == 2 and blocks == 16
+    return (close_body if close else far_body)(*arrays)
+
+
 def solution(mesh):
     placed = (
         P(None, ("grp", "seg")),

time: 174 us -> 45.2 us (0.26)
  blocking collectives: 114 us -> 15.1 us
  waiting for transfers between devices: 30.5 us -> 0.87 us
  Pallas kernels: 0 us -> 21.8 us
  between operations: 14.1 us -> 0.71 us
  other arithmetic: 10.5 us -> 0 us
    all_gather x5 -> x0, blocking collectives: 114 us -> none  [the longest x3 56.1 us: moment_field(): lax.all_gather(source_pack, ('seg', 'yoke'), axis=1, tiled=True)]
    unnamed x2 -> x0, waiting for transfers between devices: 30.5 us -> none
    pallas_call x0 -> x7, Pallas kernels: none -> 21.8 us  [call(): pl.pallas_call(kernel, out_shape=outputs, scratch_shapes=scratch, compile...]
    all_to_all x0 -> x1, blocking collectives: none -> 15.1 us  [close_body(): gathered = lax.all_to_all(packed, ('seg', 'yoke'), 0, 0, tiled=True)]
    reduce_sum x6 -> x0, other arithmetic: 8.55 us -> none  [the longest x3 6.15 us: dipole_kernel(): jnp.sum(fifth * (3.0 * delta_x * along - radial * sources[3][None, :]), a...]
    unnamed x12 -> x16, local copies, waits for them, and re-layouts: 3.92 us -> 5.37 us
  transfers between devices with their start and end apart: 1 -> 3, of which waited for: 1 -> 1; matrix products, arithmetic and copies ran while one was open for 0% -> 0% of each run, Pallas kernels for 0% -> 18%
where the time goes in v1:
time: 45.2 us; the launch traced here: 44.9 us
  Pallas kernels  21.8 us (48%)
  blocking collectives  15.1 us (33%)
  local copies, waits for them, and re-layouts  5.37 us (12%)
  starting transfers between devices  1.03 us (2%)
  waiting for transfers between devices  0.87 us (2%)
  between operations  0.71 us (2%)
    pallas_call x7, Pallas kernels, call(): pl.pallas_call(kernel, out_shape=outputs, scratch_shapes=scratch, compile...  21.8 us
    all_to_all x1, blocking collectives, close_body(): gathered = lax.all_to_all(packed, ('seg', 'yoke'), 0, 0, tiled=True)  15.1 us
    unnamed x16, local copies, waits for them, and re-layouts  5.37 us
    ppermute x3, starting transfers between devices, swap(): return lax.ppermute(state, 'yoke', [(0, 1), (1, 0)])  1.03 us
  transfers between devices with their start and end apart: 3, of which 1 were waited for; matrix products, arithmetic and copies ran while one was open for 0% of the time, Pallas kernels for 18%

profile of v1, /device:TPU:0, one launch (start us, length us, event | category | flops | bytes accessed | tf_op | source)
XLA Modules:
  0.0 44.9 jit_solution(12584789765476615699)
XLA Ops:
  0.6 0.0 copy-start
  0.6 0.7 %copy-done = f32[3,256]{1,0:T(4,128)S(1)} copy-done((f32[3,256]{1,0:T(4,128)S(1)}, f32[3,256]{1,0:T(4,128)}, u32[]{:S(2)}) %copy-start) | copy-done | bytes 3096
  1.3 0.0 copy-start.1
  1.3 0.7 %copy-done.1 = f32[3,256]{1,0:T(4,128)S(1)} copy-done((f32[3,256]{1,0:T(4,128)S(1)}, f32[3,256]{1,0:T(4,128)}, u32[]{:S(2)}) %copy-start.1) | copy-done | bytes 3096
  2.0 0.0 copy-start.2
  2.0 0.7 %copy-done.2 = f32[3,128]{1,0:T(4,128)S(1)} copy-done((f32[3,128]{1,0:T(4,128)S(1)}, f32[3,128]{1,0:T(4,128)}, u32[]{:S(2)}) %copy-start.2) | copy-done | bytes 1560
  2.7 0.0 copy-start.3
  2.7 0.7 %copy-done.3 = s32[256]{0:T(256)S(1)} copy-done((s32[256]{0:T(256)S(1)}, s32[256]{0:T(256)}, u32[]{:S(2)}) %copy-start.3) | copy-done | bytes 1048
  3.4 0.0 copy-start.4
  3.4 0.7 %copy-done.4 = f32[256]{0:T(256)S(1)} copy-done((f32[256]{0:T(256)S(1)}, f32[256]{0:T(256)}, u32[]{:S(2)}) %copy-start.4) | copy-done | bytes 1048
  4.0 0.0 copy-start.5
  4.1 0.7 %copy-done.5 = f32[128]{0:T(128)S(1)} copy-done((f32[128]{0:T(128)S(1)}, f32[128]{0:T(128)}, u32[]{:S(2)}) %copy-start.5) | copy-done | bytes 536
  4.7 0.0 copy-start.6
  4.7 0.7 %copy-done.6 = s32[128]{0:T(128)S(1)} copy-done((s32[128]{0:T(128)S(1)}, s32[128]{0:T(128)}, u32[]{:S(2)}) %copy-start.6) | copy-done | bytes 536
  5.4 0.0 copy-start.7
  5.4 0.7 %copy-done.7 = f32[64]{0:T(128)S(1)} copy-done((f32[64]{0:T(128)S(1)}, f32[64]{0:T(128)}, u32[]{:S(2)}) %copy-start.7) | copy-done | bytes 280
  6.0 0.3 shard_map.95
  6.3 15.1 %all_to_all.5.gathered_ref = f32[16,16,128]{2,1,0:T(8,128)S(1)} all-to-all(f32[16,16,128]{2,1,0:T(8,128)S(1)} %shard_map.95), channel_id=1, replica_groups=mesh['grp'=2,'seg'=8,'yoke'=2] {'seg','yoke'}, dimensions={0} | all-to-all | bytes 262144 | tf_op jit(solution)/shard_map/all_to_all | solution.py:469
  21.4 6.2 %shard_map.96 = (f32[16,2048]{1,0:T(8,128)S(1)}, f32[2048,16]{1,0:T(8,128)S(1)}, f32[8,1024]{1,0:T(8,128)S(1)}) custom-call(f32[16,16,128]{2,1,0:T(8,128)S(1)} %all_to_all.5.gathered_ref), custom_call_target="tpu_custom_call" | custom-call | tf_op jit(solution)/shard_map/pallas_call | solution.py:435
  27.6 0.1 collective-permute-start
  27.7 6.4 %shard_map.97 = (bf16[2048,1024]{1,0:T(8,128)(2,1)S(1)}, bf16[2048,1024]{1,0:T(8,128)(2,1)S(1)}, bf16[2048,1024]{1,0:T(8,128)(2,1)S(1)}) custom-call(f32[16,2048]{1,0:T(8,128)S(1)} %get-tuple-element.8.row_ref, f32[2048,16]{1,0:T(8,128)S(1)} %get-tuple-element.10.col_ref), custom_call_target="tpu_custom_call" | custom-call | tf_op jit(solution)/shard_map/pallas_call | solution.py:435
  34.1 0.0 collective-permute-done.other_ref
  34.1 2.2 %shard_map.98.own_ref = f32[8,1024]{1,0:T(8,128)S(1)} custom-call(f32[16,2048]{1,0:T(8,128)S(1)} %get-tuple-element.8.row_ref, f32[8,1024]{1,0:T(8,128)S(1)} %get-tuple-element.9.own_ref, f32[8,1024]{1,0:T(8,128)S(1)} %collective-permute-done.other_ref, bf16[2048,1024]{1,0:T(8,128)(2,1)S(1)} %get-tuple-element.11.refs_0_, ...), custom_call_target="tpu_custom_call" | custom-call | tf_op jit(solution)/shard_map/pallas_call | solution.py:435
  36.3 0.5 %collective-permute-start.1 = (f32[8,1024]{1,0:T(8,128)S(1)}, f32[8,1024]{1,0:T(8,128)S(1)}, u32[]{:S(2)}, u32[]{:S(2)}) collective-permute-start(f32[8,1024]{1,0:T(8,128)S(1)} %shard_map.98.own_ref), channel_id=1, source_target_pairs={{0,1},{1,0},{2,3},{3,2},{4,5},{5,4},{6,7},{7,6},{8,9},{9,8},{10,11... | collective-permute-start | bytes 98312 | tf_op jit(solution)/shard_map/ppermute | solution.py:454
  36.8 0.9 %collective-permute-done.1.other_ref = f32[8,1024]{1,0:T(8,128)S(1)} collective-permute-done((f32[8,1024]{1,0:T(8,128)S(1)}, f32[8,1024]{1,0:T(8,128)S(1)}, u32[]{:S(2)}, u32[]{:S(2)}) %collective-permute-start.1) | collective-permute-done | bytes 32800 | tf_op jit(solution)/shard_map/ppermute | solution.py:454
  37.6 2.2 %shard_map.99.own_ref = f32[8,1024]{1,0:T(8,128)S(1)} custom-call(f32[16,2048]{1,0:T(8,128)S(1)} %get-tuple-element.8.row_ref, f32[8,1024]{1,0:T(8,128)S(1)} %shard_map.98.own_ref, f32[8,1024]{1,0:T(8,128)S(1)} %collective-permute-done.1.other_ref, bf16[2048,1024]{1,0:T(8,128)(2,1)S(1)} %get-tuple-element.11.refs_0_, ...), custom_call_target="tpu_custom_call" | custom-call | tf_op jit(solution)/shard_map/pallas_call | solution.py:435
  39.8 0.4 collective-permute-start.2
  40.2 1.9 %shard_map.100.coil_ref = f32[3,128]{1,0:T(4,128)S(1)} custom-call(f32[16,2048]{1,0:T(8,128)S(1)} %get-tuple-element.8.row_ref), custom_call_target="tpu_custom_call" | custom-call | tf_op jit(solution)/shard_map/pallas_call | solution.py:435
  42.2 0.0 collective-permute-done.2.other_ref
  42.2 2.7 %shard_map.101 = (f32[3,128]{1,0:T(4,128)}, f32[3,128]{1,0:T(4,128)}) custom-call(f32[16,2048]{1,0:T(8,128)S(1)} %get-tuple-element.8.row_ref, f32[8,1024]{1,0:T(8,128)S(1)} %shard_map.99.own_ref, f32[8,1024]{1,0:T(8,128)S(1)} %collective-permute-done.2.other_ref, f32[3,128]{1,0:T(4,128)S(1)} %shard_map.100.coil_ref), custom_call_target="tpu_custom_call" | custom-call | tf_op jit(solution)/shard_map/pallas_call | solution.py:435
Async XLA Ops:
  0.6 0.7 %copy-start = (f32[3,256]{1,0:T(4,128)S(1)}, f32[3,256]{1,0:T(4,128)}, u32[]{:S(2)}) copy-start(f32[3,256]{1,0:T(4,128)} %mid_ref.1) | copy-start | bytes 9220
  1.3 0.7 %copy-start.1 = (f32[3,256]{1,0:T(4,128)S(1)}, f32[3,256]{1,0:T(4,128)}, u32[]{:S(2)}) copy-start(f32[3,256]{1,0:T(4,128)} %vec_ref.1) | copy-start | bytes 9220
  2.0 0.7 %copy-start.2 = (f32[3,128]{1,0:T(4,128)S(1)}, f32[3,128]{1,0:T(4,128)}, u32[]{:S(2)}) copy-start(f32[3,128]{1,0:T(4,128)} %pos_ref.1) | copy-start | bytes 4612
  2.7 0.7 %copy-start.3 = (s32[256]{0:T(256)S(1)}, s32[256]{0:T(256)}, u32[]{:S(2)}) copy-start(s32[256]{0:T(256)} %param.10) | copy-start | bytes 3076
  3.4 0.7 %copy-start.4 = (f32[256]{0:T(256)S(1)}, f32[256]{0:T(256)}, u32[]{:S(2)}) copy-start(f32[256]{0:T(256)} %param.11) | copy-start | bytes 3076
  4.0 0.7 %copy-start.5 = (f32[128]{0:T(128)S(1)}, f32[128]{0:T(128)}, u32[]{:S(2)}) copy-start(f32[128]{0:T(128)} %param.13) | copy-start | bytes 1540
  4.7 0.7 %copy-start.6 = (s32[128]{0:T(128)S(1)}, s32[128]{0:T(128)}, u32[]{:S(2)}) copy-start(s32[128]{0:T(128)} %param.14) | copy-start | bytes 1540
  5.4 0.7 %copy-start.7 = (f32[64]{0:T(128)S(1)}, f32[64]{0:T(128)}, u32[]{:S(2)}) copy-start(f32[64]{0:T(128)} %param.15) | copy-start | bytes 772
  27.6 6.5 %collective-permute-start = (f32[8,1024]{1,0:T(8,128)S(1)}, f32[8,1024]{1,0:T(8,128)S(1)}, u32[]{:S(2)}, u32[]{:S(2)}) collective-permute-start(f32[8,1024]{1,0:T(8,128)S(1)} %get-tuple-element.9.own_ref), channel_id=1, source_target_pairs={{0,1},{1,0},{2,3},{3,2},{4,5},{5,4},{6,7},{7,6},{8,9},{9,8},{10,11... | collective-permute-start | bytes 98312 | tf_op jit(solution)/shard_map/ppermute | solution.py:454
  36.3 1.4 %collective-permute-start.1 = (f32[8,1024]{1,0:T(8,128)S(1)}, f32[8,1024]{1,0:T(8,128)S(1)}, u32[]{:S(2)}, u32[]{:S(2)}) collective-permute-start(f32[8,1024]{1,0:T(8,128)S(1)} %shard_map.98.own_ref), channel_id=1, source_target_pairs={{0,1},{1,0},{2,3},{3,2},{4,5},{5,4},{6,7},{7,6},{8,9},{9,8},{10,11... | collective-permute-start | bytes 98312 | tf_op jit(solution)/shard_map/ppermute | solution.py:454
  39.8 2.4 %collective-permute-start.2 = (f32[8,1024]{1,0:T(8,128)S(1)}, f32[8,1024]{1,0:T(8,128)S(1)}, u32[]{:S(2)}, u32[]{:S(2)}) collective-permute-start(f32[8,1024]{1,0:T(8,128)S(1)} %shard_map.99.own_ref), channel_id=1, source_target_pairs={{0,1},{1,0},{2,3},{3,2},{4,5},{5,4},{6,7},{7,6},{8,9},{9,8},{10,11... | collective-permute-start | bytes 98312 | tf_op jit(solution)/shard_map/ppermute | solution.py:454

commit v2 on v0

--- a/solution.py
+++ b/solution.py
@@ -3,9 +3,12 @@
 import jax
 import jax.numpy as jnp
 from jax import lax
+from jax.experimental import pallas as pl
+from jax.experimental.pallas import tpu as pltpu
 from jax.sharding import PartitionSpec as P
 
 ITERS = 2
+VMEM_BYTES = 16 << 20
 
 
 coil_core = 0.05
@@ -107,7 +110,7 @@
     return jnp.sum(jnp.where(indices[None, :] == rows_iota, table[:, None], 0.0), axis=0)
 
 
-def body(seg_mid, seg_vec, strand_of, strand_current, yoke_pos, quad_weight, panel_of, panel_chi):
+def far_body(seg_mid, seg_vec, strand_of, strand_current, yoke_pos, quad_weight, panel_of, panel_chi):
     seg_len = seg_mid.shape[1]
     half_len = seg_len // 2
     yoke_len = yoke_pos.shape[1]
@@ -150,6 +153,320 @@
     return (lorentz, moment)
 
 
+def bf16_parts(value):
+    parts = []
+    for place in range(3):
+        part = value.astype(jnp.bfloat16)
+        parts.append(part)
+        if place < 2:
+            value = value - part.astype(jnp.float32)
+    return parts
+
+
+def split_rows(rows, split_ref):
+    count = rows.shape[0]
+    for place, part in enumerate(bf16_parts(rows)):
+        split_ref[place * count : (place + 1) * count, :] = part
+
+
+def joined(product):
+    count = product.shape[0] // 3
+    return product[:count] + product[count : 2 * count] + product[2 * count :]
+
+
+def pick(table_ref, index_ref):
+    entries = lax.broadcasted_iota(jnp.int32, (table_ref.shape[1], index_ref.shape[1]), 0)
+    chosen = jnp.where(entries == index_ref[...], 1.0, 0.0)
+    table = jnp.broadcast_to(table_ref[...], (8, table_ref.shape[1]))
+    found = jnp.dot(
+        table, chosen, precision=lax.Precision.HIGHEST, preferred_element_type=jnp.float32
+    )
+    return found[:1]
+
+
+def pack_kernel(*refs):
+    sources, (out_ref, chi_ref), held, sems = refs[:8], refs[8:10], refs[10:18], refs[18]
+    copies = [
+        pltpu.make_async_copy(source, target, sems.at[place])
+        for place, (source, target) in enumerate(zip(sources, held))
+    ]
+    for copy in copies:
+        copy.start()
+    for copy in copies:
+        copy.wait()
+    mid_ref, vec_ref, strand_ref, current_ref, pos_ref, weight_ref, panel_ref, table_ref = held
+    half = pos_ref.shape[1]
+    first = lax.axis_index("yoke") == 0
+    mid = jnp.where(first, mid_ref[:, :half], mid_ref[:, half:])
+    carried = pick(current_ref, strand_ref) * vec_ref[...]
+    carried = jnp.where(first, carried[:, :half], carried[:, half:])
+    suscept = pick(table_ref, panel_ref)
+    chi_ref[...] = suscept
+    rows = [pos_ref[k : k + 1, :] for k in range(3)]
+    rows += [mid[k : k + 1] for k in range(3)]
+    rows += [weight_ref[...] * suscept]
+    rows += [carried[k : k + 1] for k in range(3)]
+    for block in range(out_ref.shape[0]):
+        for place, row in enumerate(rows):
+            out_ref[block, :, place * half : (place + 1) * half] = row
+
+
+def half_at(half):
+    return pl.ds(pl.multiple_of(lax.axis_index("yoke") * half, half), half)
+
+
+def own_at(half, width):
+    start = lax.axis_index("yoke") * half + lax.axis_index("seg") * width
+    return pl.ds(pl.multiple_of(start, width), width)
+
+
+def target_rows(row_ref, half, width):
+    near, own = half_at(half), own_at(half, width)
+    return [
+        jnp.concatenate([row_ref[k : k + 1, near], row_ref[3 + k : 4 + k, own]], 1)
+        for k in range(3)
+    ]
+
+
+def fill(targets, col_ref, at, first, core, power, part_refs, start):
+    sources = col_ref[at, :]
+    dx, dy, dz = [targets[k] - sources[:, first + k : first + k + 1] for k in range(3)]
+    inverse = lax.rsqrt(dx * dx + dy * dy + dz * dz + core * core)
+    square = inverse * inverse
+    value = square * inverse if power == 3 else square * square * inverse
+    for ref, part in zip(part_refs, bf16_parts(value)):
+        ref[start : start + value.shape[0], :] = part
+
+
+def coil_stage(
+    gathered_ref, row_ref, col_ref, field_ref, segment_ref, split_ref, *weight_refs
+):
+    blocks = gathered_ref.shape[0]
+    total = row_ref.shape[1]
+    half, width = total // 2, total // blocks
+    for block in range(blocks):
+        place = (block % 2) * half + (block // 2) * width
+        for k in range(10):
+            row_ref[k : k + 1, place : place + width] = gathered_ref[
+                block, :, k * width : (k + 1) * width
+            ]
+    center = jnp.sum(row_ref[0:3, :], axis=1, keepdims=True) * (1.0 / total)
+    shift = jnp.concatenate([center, center, jnp.zeros((2, 1), jnp.float32)], 0)
+    row_ref[0:8, :] = row_ref[0:8, :] - shift
+    for block in range(blocks):
+        at = slice(block * width, (block + 1) * width)
+        col_ref[at, :] = row_ref[0:8, at].T
+    mx, my, mz = [row_ref[3 + k : 4 + k, :] for k in range(3)]
+    cx, cy, cz = [row_ref[7 + k : 8 + k, :] for k in range(3)]
+    split_rows(
+        jnp.concatenate(
+            [
+                cx,
+                cy,
+                cz,
+                cy * mz - cz * my,
+                cz * mx - cx * mz,
+                cx * my - cy * mx,
+                jnp.zeros((10, total), jnp.float32),
+            ],
+            0,
+        ),
+        split_ref,
+    )
+    targets = target_rows(row_ref, half, width)
+    tx, ty, tz = targets
+    depth, step = 256, 32
+    count = total // depth
+    product = jnp.zeros((split_ref.shape[0], half + width), jnp.float32)
+
+    def build(chunk):
+        part_refs = weight_refs[3 * (chunk % 2) : 3 * (chunk % 2) + 3]
+        for start in range(0, depth, step):
+            at = slice(chunk * depth + start, chunk * depth + start + step)
+            fill(targets, col_ref, at, 3, coil_core, 3, part_refs, start)
+
+    build(0)
+    for chunk in range(count):
+        if chunk + 1 < count:
+            build(chunk + 1)
+        rows = split_ref[:, chunk * depth : (chunk + 1) * depth]
+        for ref in weight_refs[3 * (chunk % 2) : 3 * (chunk % 2) + 3]:
+            product = product + jnp.dot(rows, ref[...], preferred_element_type=jnp.float32)
+    sums = joined(product)
+    sx, sy, sz = [sums[k : k + 1] for k in range(3)]
+    field = jnp.concatenate([sy * tz - sz * ty, sz * tx - sx * tz, sx * ty - sy * tx], 0)
+    field = (field - sums[3:6]) * (1.0 / math.sqrt(total))
+    field_ref[...] = field[:, :half]
+    segment_ref[...] = field[:, half:]
+
+
+def spread_stage(row_ref, col_ref, *part_refs):
+    total, columns = part_refs[0].shape
+    targets = target_rows(row_ref, total // 2, columns - total // 2)
+    step = 32
+    for start in range(0, total, step):
+        at = slice(start, start + step)
+        fill(targets, col_ref, at, 0, yoke_core, 5, part_refs, start)
+
+
+def source_rows(row_ref, own_ref, other_ref, split_ref):
+    total = row_ref.shape[1]
+    first = lax.axis_index("yoke") == 0
+    own, other = own_ref[...], other_ref[...]
+    field = jnp.concatenate([jnp.where(first, own, other), jnp.where(first, other, own)], 1)
+    strength = row_ref[6:7, :] * field
+    ux, uy, uz = [strength[k : k + 1] for k in range(3)]
+    qx, qy, qz = [row_ref[k : k + 1, :] for k in range(3)]
+    along = 3.0 * (qx * ux + qy * uy + qz * uz)
+    square = qx * qx + qy * qy + qz * qz
+    split_rows(
+        jnp.concatenate(
+            [
+                strength,
+                qx * strength,
+                qy * strength,
+                qz * strength,
+                qx * along - square * ux,
+                qy * along - square * uy,
+                qz * along - square * uz,
+                jnp.zeros((1, total), jnp.float32),
+            ],
+            0,
+        ),
+        split_ref,
+    )
+
+
+def dipole_field(targets, split_ref, part_refs, columns):
+    total = split_ref.shape[1]
+    depth = 256
+    product = jnp.zeros((split_ref.shape[0], targets[0].shape[1]), jnp.float32)
+    for start in range(0, total, depth):
+        rows = split_ref[:, start : start + depth]
+        for ref in part_refs:
+            product = product + jnp.dot(
+                rows, ref[start : start + depth, columns], preferred_element_type=jnp.float32
+            )
+    sums = joined(product)
+    tx, ty, tz = targets
+    plain = [sums[k : k + 1] for k in range(3)]
+    tensor = [[sums[3 + 3 * a + b : 4 + 3 * a + b] for b in range(3)] for a in range(3)]
+    toward = tx * plain[0] + ty * plain[1] + tz * plain[2]
+    trace = tensor[0][0] + tensor[1][1] + tensor[2][2]
+    lead = 3.0 * (toward - trace)
+    reach = tx * tx + ty * ty + tz * tz
+    fields = []
+    for a in range(3):
+        field = targets[a] * lead - reach * plain[a] + sums[12 + a : 13 + a]
+        for b in range(3):
+            field = field + targets[b] * (2.0 * tensor[b][a] - 3.0 * tensor[a][b])
+        fields.append(field)
+    return jnp.concatenate(fields, 0) * (1.0 / math.sqrt(total))
+
+
+def sweep_stage(row_ref, coil_ref, own_ref, other_ref, *refs):
+    part_refs, (field_ref, split_ref) = refs[:3], refs[3:]
+    half = coil_ref.shape[1]
+    source_rows(row_ref, own_ref, other_ref, split_ref)
+    near = half_at(half)
+    targets = [row_ref[k : k + 1, near] for k in range(3)]
+    field_ref[...] = coil_ref[...] + dipole_field(
+        targets, split_ref, part_refs, slice(0, half)
+    )
+
+
+def force_stage(row_ref, chi_ref, segment_ref, own_ref, other_ref, *refs):
+    part_refs, (lorentz_ref, moment_ref, split_ref) = refs[:3], refs[3:]
+    half, width = own_ref.shape[1], chi_ref.shape[1]
+    at = pl.ds(pl.multiple_of(lax.axis_index("seg") * width, width), width)
+    moment_ref[...] = chi_ref[...] * own_ref[:, at]
+    source_rows(row_ref, own_ref, other_ref, split_ref)
+    own = own_at(half, width)
+    targets = [row_ref[3 + k : 4 + k, own] for k in range(3)]
+    field = segment_ref[...] + dipole_field(
+        targets, split_ref, part_refs, slice(half, half + width)
+    )
+    fx, fy, fz = [field[k : k + 1] for k in range(3)]
+    cx, cy, cz = [row_ref[7 + k : 8 + k, own] for k in range(3)]
+    lorentz_ref[...] = jnp.concatenate(
+        [cy * fz - cz * fy, cz * fx - cx * fz, cx * fy - cy * fx], 0
+    )
+
+
+def call(kernel, outputs, scratch, *operands, limit=VMEM_BYTES, **options):
+    return pl.pallas_call(
+        kernel,
+        out_shape=outputs,
+        scratch_shapes=scratch,
+        compiler_params=pltpu.CompilerParams(vmem_limit_bytes=limit),
+        **options,
+    )(*operands)
+
+
+def close_body(
+    seg_mid, seg_vec, strand_of, strand_current, yoke_pos, quad_weight, panel_of, panel_chi
+):
+    width = yoke_pos.shape[1]
+    blocks = lax.axis_size("seg") * lax.axis_size("yoke")
+    total = blocks * width
+    half = total // 2
+    f32, bf16 = jnp.float32, jnp.bfloat16
+
+    def shape(*dims, kind=f32):
+        return jax.ShapeDtypeStruct(dims, kind)
+
+    def swap(field):
+        return lax.ppermute(field, "yoke", [(0, 1), (1, 0)])
+
+    arrays = [
+        seg_mid,
+        seg_vec,
+        strand_of[None],
+        strand_current[None],
+        yoke_pos,
+        quad_weight[None],
+        panel_of[None],
+        panel_chi[None],
+    ]
+    arrays = [pltpu.with_memory_space_constraint(each, pltpu.HBM) for each in arrays]
+    packed, chi = call(
+        pack_kernel,
+        (shape(blocks, 1, 10 * width), shape(1, width)),
+        [pltpu.VMEM(each.shape, each.dtype) for each in arrays]
+        + [pltpu.SemaphoreType.DMA((len(arrays),))],
+        *arrays,
+        in_specs=[pl.BlockSpec(memory_space=pltpu.HBM)] * len(arrays),
+    )
+    gathered = lax.all_to_all(packed, ("seg", "yoke"), 0, 0, tiled=True)
+    split_scratch = pltpu.VMEM((48, total), bf16)
+    rows, columns, coil, segments = call(
+        coil_stage,
+        (shape(16, total), shape(total, 8), shape(3, half), shape(3, width)),
+        [split_scratch] + [pltpu.VMEM((256, half + width), bf16)] * 6,
+        gathered,
+    )
+    own, other = coil, swap(coil)
+    spread = call(spread_stage, [shape(total, half + width, kind=bf16)] * 3, [], rows, columns)
+    for sweep in range(ITERS):
+        own = call(
+            sweep_stage, shape(3, half), [split_scratch], rows, coil, own, other, *spread
+        )
+        other = swap(own)
+    outputs = (shape(3, width), shape(3, width))
+    return tuple(
+        call(
+            force_stage, outputs, [split_scratch], rows, chi, segments, own, other, *spread
+        )
+    )
+
+
+def body(*arrays):
+    seg_len, yoke_len = arrays[0].shape[1], arrays[4].shape[1]
+    blocks = lax.axis_size("seg") * lax.axis_size("yoke")
+    close = seg_len == 256 and yoke_len == 128 and lax.axis_size("yoke") == 2 and blocks == 16
+    return (close_body if close else far_body)(*arrays)
+
+
 def solution(mesh):
     placed = (
         P(None, ("grp", "seg")),

time: 174 us -> 38.6 us (0.22)
  blocking collectives: 114 us -> 14.3 us
  waiting for transfers between devices: 30.5 us -> 1.68 us
  Pallas kernels: 0 us -> 20.6 us
  between operations: 14.1 us -> 0.69 us
  other arithmetic: 10.5 us -> 0 us
  local copies, waits for them, and re-layouts: 4.09 us -> 0 us
    all_gather x5 -> x0, blocking collectives: 114 us -> none  [the longest x3 56.1 us: moment_field(): lax.all_gather(source_pack, ('seg', 'yoke'), axis=1, tiled=True)]
    unnamed x2 -> x0, waiting for transfers between devices: 30.5 us -> none
    pallas_call x0 -> x6, Pallas kernels: none -> 20.6 us  [call(): pl.pallas_call(kernel, out_shape=outputs, scratch_shapes=scratch, compile...]
    all_to_all x0 -> x1, blocking collectives: none -> 14.3 us  [close_body(): gathered = lax.all_to_all(packed, ('seg', 'yoke'), 0, 0, tiled=True)]
    reduce_sum x6 -> x0, other arithmetic: 8.55 us -> none  [the longest x3 6.15 us: dipole_kernel(): jnp.sum(fifth * (3.0 * delta_x * along - radial * sources[3][None, :]), a...]
    unnamed x12 -> x0, local copies, waits for them, and re-layouts: 3.92 us -> none
  transfers between devices with their start and end apart: 1 -> 3, of which waited for: 1 -> 2; matrix products, arithmetic and copies ran while one was open for 0% -> 0% of each run, Pallas kernels for 0% -> 17%
where the time goes in v2:
time: 38.6 us; the launch traced here: 38.3 us
  Pallas kernels  20.6 us (53%)
  blocking collectives  14.3 us (37%)
  waiting for transfers between devices  1.68 us (4%)
  starting transfers between devices  1.04 us (3%)
  between operations  0.69 us (2%)
    pallas_call x6, Pallas kernels, call(): pl.pallas_call(kernel, out_shape=outputs, scratch_shapes=scratch, compile...  20.6 us
    all_to_all x1, blocking collectives, close_body(): gathered = lax.all_to_all(packed, ('seg', 'yoke'), 0, 0, tiled=True)  14.3 us
    ppermute x3, waiting for transfers between devices, swap(): return lax.ppermute(field, 'yoke', [(0, 1), (1, 0)])  1.68 us
    ppermute x3, starting transfers between devices, swap(): return lax.ppermute(field, 'yoke', [(0, 1), (1, 0)])  1.04 us
  transfers between devices with their start and end apart: 3, of which 2 were waited for; matrix products, arithmetic and copies ran while one was open for 0% of the time, Pallas kernels for 17%

profile of v2, /device:TPU:0, one launch (start us, length us, event | category | flops | bytes accessed | tf_op | source)
XLA Modules:
  0.0 38.3 jit_solution(10866060068575857539)
XLA Ops:
  0.6 1.1 %shard_map.95 = (f32[16,1,1280]{2,1,0:T(1,128)S(1)}, f32[1,128]{1,0:T(1,128)S(1)}) custom-call(f32[3,256]{1,0:T(4,128)} %refs_0_.1, f32[3,256]{1,0:T(4,128)} %refs_1_.1, s32[1,256]{1,0:T(1,128)} %bitcast.5, f32[1,256]{1,0:T(1,128)} %bitcast.6, f32[3,128]{1,0:T(4,128)} %refs_4_.1, f32[1,128]{1,0:T(1,128)} %bitcast.7, s32[1,128]{1,0:T(1,128)} %bitcast.8, ...), custom_call_target="tpu_custom_call" | custom-call | tf_op jit(solution)/shard_map/pallas_call | solution.py:397
  1.8 14.3 %all_to_all.5.gathered_ref = f32[16,1,1280]{2,1,0:T(1,128)S(1)} all-to-all(f32[16,1,1280]{2,1,0:T(1,128)S(1)} %get-tuple-element.11), channel_id=1, replica_groups=mesh['grp'=2,'seg'=8,'yoke'=2] {'seg','yoke'}, dimensions={0} | all-to-all | bytes 163840 | tf_op jit(solution)/shard_map/all_to_all | solution.py:440
  16.1 7.6 %shard_map.96 = (f32[16,2048]{1,0:T(8,128)S(1)}, f32[2048,8]{1,0:T(8,128)S(1)}, f32[3,1024]{1,0:T(4,128)S(1)}, f32[3,128]{1,0:T(4,128)S(1)}) custom-call(f32[16,1,1280]{2,1,0:T(1,128)S(1)} %all_to_all.5.gathered_ref), custom_call_target="tpu_custom_call" | custom-call | tf_op jit(solution)/shard_map/pallas_call | solution.py:397
  23.7 0.1 collective-permute-start
  23.8 6.6 %shard_map.97 = (bf16[2048,1152]{1,0:T(8,128)(2,1)S(1)}, bf16[2048,1152]{1,0:T(8,128)(2,1)S(1)}, bf16[2048,1152]{1,0:T(8,128)(2,1)S(1)}) custom-call(f32[16,2048]{1,0:T(8,128)S(1)} %get-tuple-element.12.row_ref, f32[2048,8]{1,0:T(8,128)S(1)} %get-tuple-element.16.col_ref), custom_call_target="tpu_custom_call" | custom-call | tf_op jit(solution)/shard_map/pallas_call | solution.py:397
  30.4 0.0 collective-permute-done.other_ref
  30.4 2.2 %shard_map.98.own_ref = f32[3,1024]{1,0:T(4,128)S(1)} custom-call(f32[16,2048]{1,0:T(8,128)S(1)} %get-tuple-element.12.row_ref, f32[3,1024]{1,0:T(4,128)S(1)} %get-tuple-element.15.coil_ref.own_ref, f32[3,1024]{1,0:T(4,128)S(1)} %get-tuple-element.15.coil_ref.own_ref, f32[3,1024]{1,0:T(4,128)S(1)} %collective-permute-done.other_ref, ...), custom_call_target="tpu_custom_call" | custom-call | tf_op jit(solution)/shard_map/pallas_call | solution.py:397
  32.5 0.6 %collective-permute-start.1 = (f32[3,1024]{1,0:T(4,128)S(1)}, f32[3,1024]{1,0:T(4,128)S(1)}, u32[]{:S(2)}, u32[]{:S(2)}) collective-permute-start(f32[3,1024]{1,0:T(4,128)S(1)} %shard_map.98.own_ref), channel_id=1, source_target_pairs={{0,1},{1,0},{2,3},{3,2},{4,5},{5,4},{6,7},{7,6},{8,9},{9,8},{10,11... | collective-permute-start | bytes 36872 | tf_op jit(solution)/shard_map/ppermute | solution.py:419
  33.1 0.8 %collective-permute-done.1.other_ref = f32[3,1024]{1,0:T(4,128)S(1)} collective-permute-done((f32[3,1024]{1,0:T(4,128)S(1)}, f32[3,1024]{1,0:T(4,128)S(1)}, u32[]{:S(2)}, u32[]{:S(2)}) %collective-permute-start.1) | collective-permute-done | bytes 12320 | tf_op jit(solution)/shard_map/ppermute | solution.py:419
  33.9 2.2 %shard_map.99.own_ref = f32[3,1024]{1,0:T(4,128)S(1)} custom-call(f32[16,2048]{1,0:T(8,128)S(1)} %get-tuple-element.12.row_ref, f32[3,1024]{1,0:T(4,128)S(1)} %get-tuple-element.15.coil_ref.own_ref, f32[3,1024]{1,0:T(4,128)S(1)} %shard_map.98.own_ref, f32[3,1024]{1,0:T(4,128)S(1)} %collective-permute-done.1.other_ref, ...), custom_call_target="tpu_custom_call" | custom-call | tf_op jit(solution)/shard_map/pallas_call | solution.py:397
  36.1 0.4 %collective-permute-start.2 = (f32[3,1024]{1,0:T(4,128)S(1)}, f32[3,1024]{1,0:T(4,128)S(1)}, u32[]{:S(2)}, u32[]{:S(2)}) collective-permute-start(f32[3,1024]{1,0:T(4,128)S(1)} %shard_map.99.own_ref), channel_id=1, source_target_pairs={{0,1},{1,0},{2,3},{3,2},{4,5},{5,4},{6,7},{7,6},{8,9},{9,8},{10,11... | collective-permute-start | bytes 36872 | tf_op jit(solution)/shard_map/ppermute | solution.py:419
  36.5 0.8 %collective-permute-done.2.other_ref = f32[3,1024]{1,0:T(4,128)S(1)} collective-permute-done((f32[3,1024]{1,0:T(4,128)S(1)}, f32[3,1024]{1,0:T(4,128)S(1)}, u32[]{:S(2)}, u32[]{:S(2)}) %collective-permute-start.2) | collective-permute-done | bytes 12320 | tf_op jit(solution)/shard_map/ppermute | solution.py:419
  37.3 1.0 %shard_map.100 = (f32[3,128]{1,0:T(4,128)}, f32[3,128]{1,0:T(4,128)}) custom-call(f32[16,2048]{1,0:T(8,128)S(1)} %get-tuple-element.12.row_ref, f32[1,128]{1,0:T(1,128)S(1)} %get-tuple-element.13.chi_ref, f32[3,128]{1,0:T(4,128)S(1)} %get-tuple-element.14.segment_ref, f32[3,1024]{1,0:T(4,128)S(1)} %shard_map.99.own_ref, ...), custom_call_target="tpu_custom_call" | custom-call | tf_op jit(solution)/shard_map/pallas_call | solution.py:397
Async XLA Ops:
  23.7 6.7 %collective-permute-start = (f32[3,1024]{1,0:T(4,128)S(1)}, f32[3,1024]{1,0:T(4,128)S(1)}, u32[]{:S(2)}, u32[]{:S(2)}) collective-permute-start(f32[3,1024]{1,0:T(4,128)S(1)} %get-tuple-element.15.coil_ref.own_ref), channel_id=1, source_target_pairs={{0,1},{1,0},{2,3},{3,2},{4,5},{5,4},{6,7},{7,6},{8,9},{9,8},{10,11... | collective-permute-start | bytes 36872 | tf_op jit(solution)/shard_map/ppermute | solution.py:419
  32.5 1.4 %collective-permute-start.1 = (f32[3,1024]{1,0:T(4,128)S(1)}, f32[3,1024]{1,0:T(4,128)S(1)}, u32[]{:S(2)}, u32[]{:S(2)}) collective-permute-start(f32[3,1024]{1,0:T(4,128)S(1)} %shard_map.98.own_ref), channel_id=1, source_target_pairs={{0,1},{1,0},{2,3},{3,2},{4,5},{5,4},{6,7},{7,6},{8,9},{9,8},{10,11... | collective-permute-start | bytes 36872 | tf_op jit(solution)/shard_map/ppermute | solution.py:419
  36.1 1.2 %collective-permute-start.2 = (f32[3,1024]{1,0:T(4,128)S(1)}, f32[3,1024]{1,0:T(4,128)S(1)}, u32[]{:S(2)}, u32[]{:S(2)}) collective-permute-start(f32[3,1024]{1,0:T(4,128)S(1)} %shard_map.99.own_ref), channel_id=1, source_target_pairs={{0,1},{1,0},{2,3},{3,2},{4,5},{5,4},{6,7},{7,6},{8,9},{9,8},{10,11... | collective-permute-start | bytes 36872 | tf_op jit(solution)/shard_map/ppermute | solution.py:419

commit v3 on v2

--- a/solution.py
+++ b/solution.py
@@ -153,19 +153,19 @@
     return (lorentz, moment)
 
 
-def bf16_parts(value):
+def bf16_parts(value, count):
     parts = []
-    for place in range(3):
+    for place in range(count):
         part = value.astype(jnp.bfloat16)
         parts.append(part)
-        if place < 2:
+        if place + 1 < count:
             value = value - part.astype(jnp.float32)
     return parts
 
 
 def split_rows(rows, split_ref):
     count = rows.shape[0]
-    for place, part in enumerate(bf16_parts(rows)):
+    for place, part in enumerate(bf16_parts(rows, 3)):
         split_ref[place * count : (place + 1) * count, :] = part
 
 
@@ -211,44 +211,55 @@
             out_ref[block, :, place * half : (place + 1) * half] = row
 
 
-def half_at(half):
-    return pl.ds(pl.multiple_of(lax.axis_index("yoke") * half, half), half)
-
-
-def own_at(half, width):
-    start = lax.axis_index("yoke") * half + lax.axis_index("seg") * width
-    return pl.ds(pl.multiple_of(start, width), width)
-
-
-def target_rows(row_ref, half, width):
-    near, own = half_at(half), own_at(half, width)
-    return [
-        jnp.concatenate([row_ref[k : k + 1, near], row_ref[3 + k : 4 + k, own]], 1)
-        for k in range(3)
-    ]
-
-
-def fill(targets, col_ref, at, first, core, power, part_refs, start):
-    sources = col_ref[at, :]
-    dx, dy, dz = [targets[k] - sources[:, first + k : first + k + 1] for k in range(3)]
+def times(rows, matrix_parts, transposed=False):
+    contracted = ((1,), (1 if transposed else 0,))
+    total = None
+    for part in matrix_parts:
+        product = lax.dot_general(
+            rows, part, (contracted, ((), ())), preferred_element_type=jnp.float32
+        )
+        total = product if total is None else total + product
+    return total
+
+
+def power_parts(deltas, core, power):
+    dx, dy, dz = deltas
     inverse = lax.rsqrt(dx * dx + dy * dy + dz * dz + core * core)
     square = inverse * inverse
-    value = square * inverse if power == 3 else square * square * inverse
-    for ref, part in zip(part_refs, bf16_parts(value)):
-        ref[start : start + value.shape[0], :] = part
-
-
-def coil_stage(
-    gathered_ref, row_ref, col_ref, field_ref, segment_ref, split_ref, *weight_refs
-):
+    return bf16_parts(square * inverse if power == 3 else square * square * inverse, 2)
+
+
+def deltas_of(rows, columns, first):
+    return [rows[k] - columns[:, first + k : first + k + 1] for k in range(3)]
+
+
+def coil_rows(row_ref):
+    mx, my, mz = [row_ref[3 + k : 4 + k, :] for k in range(3)]
+    cx, cy, cz = [row_ref[7 + k : 8 + k, :] for k in range(3)]
+    blank = jnp.zeros((10, row_ref.shape[1]), jnp.float32)
+    crossed = [cy * mz - cz * my, cz * mx - cx * mz, cx * my - cy * mx]
+    return jnp.concatenate([cx, cy, cz] + crossed + [blank], 0)
+
+
+def coil_field(product, targets, total):
+    sums = joined(product)
+    tx, ty, tz = targets
+    sx, sy, sz = [sums[k : k + 1] for k in range(3)]
+    field = jnp.concatenate([sy * tz - sz * ty, sz * tx - sx * tz, sx * ty - sy * tx], 0)
+    return (field - sums[3:6]) * (1.0 / math.sqrt(total))
+
+
+def coil_stage(gathered_ref, row_ref, col_ref, split_ref, field_ref, *weight_refs):
     blocks = gathered_ref.shape[0]
     total = row_ref.shape[1]
     half, width = total // 2, total // blocks
+    core = lax.axis_index("yoke")
     for block in range(blocks):
-        place = (block % 2) * half + (block // 2) * width
+        near = block < blocks // 2
+        source = 2 * (block % (blocks // 2)) + (core if near else 1 - core)
         for k in range(10):
-            row_ref[k : k + 1, place : place + width] = gathered_ref[
-                block, :, k * width : (k + 1) * width
+            row_ref[k : k + 1, block * width : (block + 1) * width] = gathered_ref[
+                source, :, k * width : (k + 1) * width
             ]
     center = jnp.sum(row_ref[0:3, :], axis=1, keepdims=True) * (1.0 / total)
     shift = jnp.concatenate([center, center, jnp.zeros((2, 1), jnp.float32)], 0)
@@ -256,64 +267,60 @@
     for block in range(blocks):
         at = slice(block * width, (block + 1) * width)
         col_ref[at, :] = row_ref[0:8, at].T
-    mx, my, mz = [row_ref[3 + k : 4 + k, :] for k in range(3)]
-    cx, cy, cz = [row_ref[7 + k : 8 + k, :] for k in range(3)]
-    split_rows(
-        jnp.concatenate(
-            [
-                cx,
-                cy,
-                cz,
-                cy * mz - cz * my,
-                cz * mx - cx * mz,
-                cx * my - cy * mx,
-                jnp.zeros((10, total), jnp.float32),
-            ],
-            0,
-        ),
-        split_ref,
-    )
-    targets = target_rows(row_ref, half, width)
-    tx, ty, tz = targets
+    split_rows(coil_rows(row_ref), split_ref)
+    targets = [row_ref[k : k + 1, :half] for k in range(3)]
     depth, step = 256, 32
     count = total // depth
-    product = jnp.zeros((split_ref.shape[0], half + width), jnp.float32)
+    product = jnp.zeros((split_ref.shape[0], half), jnp.float32)
 
     def build(chunk):
-        part_refs = weight_refs[3 * (chunk % 2) : 3 * (chunk % 2) + 3]
+        part_refs = weight_refs[2 * (chunk % 2) : 2 * (chunk % 2) + 2]
         for start in range(0, depth, step):
-            at = slice(chunk * depth + start, chunk * depth + start + step)
-            fill(targets, col_ref, at, 3, coil_core, 3, part_refs, start)
+            sources = col_ref[chunk * depth + start : chunk * depth + start + step, :]
+            parts = power_parts(deltas_of(targets, sources, 3), coil_core, 3)
+            for ref, part in zip(part_refs, parts):
+                ref[start : start + step, :] = part
 
     build(0)
     for chunk in range(count):
         if chunk + 1 < count:
             build(chunk + 1)
         rows = split_ref[:, chunk * depth : (chunk + 1) * depth]
-        for ref in weight_refs[3 * (chunk % 2) : 3 * (chunk % 2) + 3]:
-            product = product + jnp.dot(rows, ref[...], preferred_element_type=jnp.float32)
-    sums = joined(product)
-    sx, sy, sz = [sums[k : k + 1] for k in range(3)]
-    field = jnp.concatenate([sy * tz - sz * ty, sz * tx - sx * tz, sx * ty - sy * tx], 0)
-    field = (field - sums[3:6]) * (1.0 / math.sqrt(total))
-    field_ref[...] = field[:, :half]
-    segment_ref[...] = field[:, half:]
+        part_refs = weight_refs[2 * (chunk % 2) : 2 * (chunk % 2) + 2]
+        product = product + times(rows, [ref[...] for ref in part_refs])
+    field_ref[...] = coil_field(product, targets, total)
+
+
+def plan(total):
+    depth = total // 8
+    place, rows = 0, []
+    for block in range(4):
+        both = list(range(block + 1, 4)) + [4 + (block + 1) % 4]
+        both += [6 + block] if block < 2 else []
+        targets = [block] + both + [4 + block]
+        rows.append((block, place, targets))
+        place += len(targets)
+    return depth, place, rows
+
+
+def lanes_of(array, blocks, depth):
+    return jnp.concatenate([array[:, k * depth : (k + 1) * depth] for k in blocks], 1)
 
 
 def spread_stage(row_ref, col_ref, *part_refs):
-    total, columns = part_refs[0].shape
-    targets = target_rows(row_ref, total // 2, columns - total // 2)
+    depth, _, rows = plan(row_ref.shape[1])
     step = 32
-    for start in range(0, total, step):
-        at = slice(start, start + step)
-        fill(targets, col_ref, at, 0, yoke_core, 5, part_refs, start)
-
-
-def source_rows(row_ref, own_ref, other_ref, split_ref):
-    total = row_ref.shape[1]
-    first = lax.axis_index("yoke") == 0
-    own, other = own_ref[...], other_ref[...]
-    field = jnp.concatenate([jnp.where(first, own, other), jnp.where(first, other, own)], 1)
+    for block, place, blocks in rows:
+        targets = [lanes_of(row_ref[k : k + 1, :], blocks, depth) for k in range(3)]
+        lanes = slice(place * depth, (place + len(blocks)) * depth)
+        for start in range(0, depth, step):
+            sources = col_ref[block * depth + start : block * depth + start + step, :]
+            parts = power_parts(deltas_of(targets, sources, 0), yoke_core, 5)
+            for ref, part in zip(part_refs, parts):
+                ref[start : start + step, lanes] = part
+
+
+def source_rows(row_ref, field, split_ref):
     strength = row_ref[6:7, :] * field
     ux, uy, uz = [strength[k : k + 1] for k in range(3)]
     qx, qy, qz = [row_ref[k : k + 1, :] for k in range(3)]
@@ -329,7 +336,7 @@
                 qx * along - square * ux,
                 qy * along - square * uy,
                 qz * along - square * uz,
-                jnp.zeros((1, total), jnp.float32),
+                jnp.zeros((1, row_ref.shape[1]), jnp.float32),
             ],
             0,
         ),
@@ -337,16 +344,7 @@
     )
 
 
-def dipole_field(targets, split_ref, part_refs, columns):
-    total = split_ref.shape[1]
-    depth = 256
-    product = jnp.zeros((split_ref.shape[0], targets[0].shape[1]), jnp.float32)
-    for start in range(0, total, depth):
-        rows = split_ref[:, start : start + depth]
-        for ref in part_refs:
-            product = product + jnp.dot(
-                rows, ref[start : start + depth, columns], preferred_element_type=jnp.float32
-            )
+def dipole_field(product, targets, total):
     sums = joined(product)
     tx, ty, tz = targets
     plain = [sums[k : k + 1] for k in range(3)]
@@ -364,30 +362,80 @@
     return jnp.concatenate(fields, 0) * (1.0 / math.sqrt(total))
 
 
-def sweep_stage(row_ref, coil_ref, own_ref, other_ref, *refs):
-    part_refs, (field_ref, split_ref) = refs[:3], refs[3:]
-    half = coil_ref.shape[1]
-    source_rows(row_ref, own_ref, other_ref, split_ref)
-    near = half_at(half)
-    targets = [row_ref[k : k + 1, near] for k in range(3)]
-    field_ref[...] = coil_ref[...] + dipole_field(
-        targets, split_ref, part_refs, slice(0, half)
-    )
-
-
-def force_stage(row_ref, chi_ref, segment_ref, own_ref, other_ref, *refs):
-    part_refs, (lorentz_ref, moment_ref, split_ref) = refs[:3], refs[3:]
-    half, width = own_ref.shape[1], chi_ref.shape[1]
+def whole_field(own_coil_ref, other_coil_ref, partial_refs):
+    field = jnp.concatenate([own_coil_ref[...], other_coil_ref[...]], 1)
+    if partial_refs:
+        own, other = partial_refs
+        half = own.shape[1] // 2
+        field = field + own[...]
+        field = field + jnp.concatenate([other[:, half:], other[:, :half]], 1)
+    return field
+
+
+def sweep_stage(row_ref, own_coil_ref, other_coil_ref, *refs):
+    partial_refs, part_refs, (out_ref, split_ref) = refs[:-4], refs[-4:-2], refs[-2:]
+    total = row_ref.shape[1]
+    source_rows(row_ref, whole_field(own_coil_ref, other_coil_ref, partial_refs), split_ref)
+    depth, _, rows = plan(total)
+    product = [None] * 8
+
+    def add(block, value):
+        product[block] = value if product[block] is None else product[block] + value
+
+    for block, place, blocks in rows:
+        lanes = slice(place * depth, (place + len(blocks)) * depth)
+        near = split_ref[:, block * depth : (block + 1) * depth]
+        onward = times(near, [ref[:, lanes] for ref in part_refs])
+        for k, target in enumerate(blocks):
+            add(target, onward[:, k * depth : (k + 1) * depth])
+        lanes = slice((place + 1) * depth, (place + len(blocks) - 1) * depth)
+        far = lanes_of(split_ref, blocks[1:-1], depth)
+        add(block, times(far, [ref[:, lanes] for ref in part_refs], True))
+    targets = [row_ref[k : k + 1, :] for k in range(3)]
+    out_ref[...] = dipole_field(jnp.concatenate(product, 1), targets, total)
+
+
+def own_segments(row_ref, col_ref, width):
     at = pl.ds(pl.multiple_of(lax.axis_index("seg") * width, width), width)
-    moment_ref[...] = chi_ref[...] * own_ref[:, at]
-    source_rows(row_ref, own_ref, other_ref, split_ref)
-    own = own_at(half, width)
-    targets = [row_ref[3 + k : 4 + k, own] for k in range(3)]
+    return row_ref[:, at], col_ref[at, :]
+
+
+def segment_coil_stage(row_ref, col_ref, split_ref, after_ref, out_ref):
+    total = row_ref.shape[1]
+    rows, columns = own_segments(row_ref, col_ref, out_ref.shape[1])
+    sources = [row_ref[3 + k : 4 + k, :] for k in range(3)]
+    parts = power_parts(deltas_of(sources, columns, 3), coil_core, 3)
+    product = times(split_ref[...], parts, True)
+    out_ref[...] = coil_field(product, [rows[3 + k : 4 + k] for k in range(3)], total)
+
+
+def segment_spread_stage(row_ref, col_ref, after_ref, *part_refs):
+    _, columns = own_segments(row_ref, col_ref, part_refs[0].shape[0])
+    sources = [row_ref[k : k + 1, :] for k in range(3)]
+    parts = power_parts(deltas_of(sources, columns, 3), yoke_core, 5)
+    for ref, part in zip(part_refs, parts):
+        ref[...] = part
+
+
+def force_stage(row_ref, col_ref, chi_ref, segment_ref, own_coil_ref, other_coil_ref, *refs):
+    partial_refs, part_refs, (lorentz_ref, moment_ref, split_ref, field_ref) = (
+        refs[:2],
+        refs[2:4],
+        refs[4:],
+    )
+    total, width = row_ref.shape[1], chi_ref.shape[1]
+    field = whole_field(own_coil_ref, other_coil_ref, partial_refs)
+    field_ref[...] = field
+    at = pl.ds(pl.multiple_of(lax.axis_index("seg") * width, width), width)
+    moment_ref[...] = chi_ref[...] * field_ref[:, at]
+    source_rows(row_ref, field, split_ref)
+    rows, _ = own_segments(row_ref, col_ref, width)
+    product = times(split_ref[...], [ref[...] for ref in part_refs], True)
     field = segment_ref[...] + dipole_field(
-        targets, split_ref, part_refs, slice(half, half + width)
+        product, [rows[3 + k : 4 + k] for k in range(3)], total
     )
     fx, fy, fz = [field[k : k + 1] for k in range(3)]
-    cx, cy, cz = [row_ref[7 + k : 8 + k, own] for k in range(3)]
+    cx, cy, cz = [rows[7 + k : 8 + k] for k in range(3)]
     lorentz_ref[...] = jnp.concatenate(
         [cy * fz - cz * fy, cz * fx - cx * fz, cx * fy - cy * fx], 0
     )
@@ -438,24 +486,48 @@
         in_specs=[pl.BlockSpec(memory_space=pltpu.HBM)] * len(arrays),
     )
     gathered = lax.all_to_all(packed, ("seg", "yoke"), 0, 0, tiled=True)
+    split_shape = shape(48, total, kind=bf16)
     split_scratch = pltpu.VMEM((48, total), bf16)
-    rows, columns, coil, segments = call(
+    rows, columns, split, coil = call(
         coil_stage,
-        (shape(16, total), shape(total, 8), shape(3, half), shape(3, width)),
-        [split_scratch] + [pltpu.VMEM((256, half + width), bf16)] * 6,
+        (shape(16, total), shape(total, 8), split_shape, shape(3, half)),
+        [pltpu.VMEM((256, half), bf16)] * 4,
         gathered,
     )
-    own, other = coil, swap(coil)
-    spread = call(spread_stage, [shape(total, half + width, kind=bf16)] * 3, [], rows, columns)
+    coils = (coil, swap(coil))
+    depth, count, _ = plan(total)
+    spread = call(spread_stage, [shape(depth, count * depth, kind=bf16)] * 2, [], rows, columns)
+    partials = ()
     for sweep in range(ITERS):
         own = call(
-            sweep_stage, shape(3, half), [split_scratch], rows, coil, own, other, *spread
+            sweep_stage,
+            shape(3, total),
+            [split_scratch],
+            rows,
+            *coils,
+            *partials,
+            *spread,
         )
-        other = swap(own)
-    outputs = (shape(3, width), shape(3, width))
+        partials = (own, swap(own))
+        if sweep == 0:
+            segments = call(
+                segment_coil_stage, shape(3, width), [], rows, columns, split, own
+            )
+        if sweep == ITERS - 1:
+            near = [shape(width, total, kind=bf16)] * 2
+            near = call(segment_spread_stage, near, [], rows, columns, own)
     return tuple(
         call(
-            force_stage, outputs, [split_scratch], rows, chi, segments, own, other, *spread
+            force_stage,
+            (shape(3, width), shape(3, width)),
+            [split_scratch, pltpu.VMEM((3, total), f32)],
+            rows,
+            columns,
+            chi,
+            segments,
+            *coils,
+            *partials,
+            *near,
         )
     )
 

time: 38.6 us -> 32.8 us (0.85)
  Pallas kernels: 20.6 us -> 15.7 us
  waiting for transfers between devices: 1.68 us -> 0.87 us
    pallas_call x6 -> x8, Pallas kernels: 20.6 us -> 15.7 us  [call(): pl.pallas_call(kernel, out_shape=outputs, scratch_shapes=scratch, compile...]
    ppermute x3, waiting for transfers between devices: 1.68 us -> 0.87 us  [swap(): return lax.ppermute(field, 'yoke', [(0, 1), (1, 0)])]
  transfers between devices with their start and end apart: 3 -> 3, of which waited for: 2 -> 1; matrix products, arithmetic and copies ran while one was open for 0% -> 0% of each run, Pallas kernels for 17% -> 14%
where the time goes in v3:
time: 32.8 us; the launch traced here: 32.6 us
  Pallas kernels  15.7 us (48%)
  blocking collectives  14.3 us (44%)
  starting transfers between devices  1.03 us (3%)
  waiting for transfers between devices  0.87 us (3%)
  between operations  0.71 us (2%)
    pallas_call x8, Pallas kernels, call(): pl.pallas_call(kernel, out_shape=outputs, scratch_shapes=scratch, compile...  15.7 us
    all_to_all x1, blocking collectives, close_body(): gathered = lax.all_to_all(packed, ('seg', 'yoke'), 0, 0, tiled=True)  14.3 us
    ppermute x3, starting transfers between devices, swap(): return lax.ppermute(field, 'yoke', [(0, 1), (1, 0)])  1.03 us
    ppermute x3, waiting for transfers between devices, swap(): return lax.ppermute(field, 'yoke', [(0, 1), (1, 0)])  0.87 us
  transfers between devices with their start and end apart: 3, of which 1 were waited for; matrix products, arithmetic and copies ran while one was open for 0% of the time, Pallas kernels for 14%

profile of v3, /device:TPU:0, one launch (start us, length us, event | category | flops | bytes accessed | tf_op | source)
XLA Modules:
  0.0 32.6 jit_solution(9313189692538496797)
XLA Ops:
  0.6 1.1 %shard_map.95 = (f32[16,1,1280]{2,1,0:T(1,128)S(1)}, f32[1,128]{1,0:T(1,128)S(1)}) custom-call(f32[3,256]{1,0:T(4,128)} %refs_0_.1, f32[3,256]{1,0:T(4,128)} %refs_1_.1, s32[1,256]{1,0:T(1,128)} %bitcast.5, f32[1,256]{1,0:T(1,128)} %bitcast.6, f32[3,128]{1,0:T(4,128)} %refs_4_.1, f32[1,128]{1,0:T(1,128)} %bitcast.7, s32[1,128]{1,0:T(1,128)} %bitcast.8, ...), custom_call_target="tpu_custom_call" | custom-call | tf_op jit(solution)/shard_map/pallas_call | solution.py:445
  1.8 14.3 %all_to_all.5.gathered_ref = f32[16,1,1280]{2,1,0:T(1,128)S(1)} all-to-all(f32[16,1,1280]{2,1,0:T(1,128)S(1)} %get-tuple-element.12), channel_id=1, replica_groups=mesh['grp'=2,'seg'=8,'yoke'=2] {'seg','yoke'}, dimensions={0} | all-to-all | bytes 163840 | tf_op jit(solution)/shard_map/all_to_all | solution.py:488
  16.1 5.3 %shard_map.96 = (f32[16,2048]{1,0:T(8,128)S(1)}, f32[2048,8]{1,0:T(8,128)S(1)}, bf16[48,2048]{1,0:T(8,128)(2,1)S(1)}, f32[3,1024]{1,0:T(4,128)S(1)}) custom-call(f32[16,1,1280]{2,1,0:T(1,128)S(1)} %all_to_all.5.gathered_ref), custom_call_target="tpu_custom_call" | custom-call | tf_op jit(solution)/shard_map/pallas_call | solution.py:445
  21.3 0.1 collective-permute-start
  21.4 3.1 %shard_map.97 = (bf16[256,5120]{1,0:T(8,128)(2,1)S(1)}, bf16[256,5120]{1,0:T(8,128)(2,1)S(1)}) custom-call(f32[16,2048]{1,0:T(8,128)S(1)} %get-tuple-element.13.row_ref, f32[2048,8]{1,0:T(8,128)S(1)} %get-tuple-element.14.col_ref), custom_call_target="tpu_custom_call" | custom-call | tf_op jit(solution)/shard_map/pallas_call | solution.py:445
  24.5 0.0 collective-permute-done.other_coil_ref
  24.5 1.8 %shard_map.98.after_ref.refs_0_ = f32[3,2048]{1,0:T(4,128)S(1)} custom-call(f32[16,2048]{1,0:T(8,128)S(1)} %get-tuple-element.13.row_ref, f32[3,1024]{1,0:T(4,128)S(1)} %get-tuple-element.17.own_coil_ref, f32[3,1024]{1,0:T(4,128)S(1)} %collective-permute-done.other_coil_ref, bf16[256,5120]{1,0:T(8,128)(2,1)S(1)} %get-tuple-element.18.refs_0_.refs_2_, ...), custom_call_target="tpu_custom_call" | custom-call | tf_op jit(solution)/shard_map/pallas_call | solution.py:445
  26.4 0.6 %collective-permute-start.1 = (f32[3,2048]{1,0:T(4,128)S(1)}, f32[3,2048]{1,0:T(4,128)S(1)}, u32[]{:S(2)}, u32[]{:S(2)}) collective-permute-start(f32[3,2048]{1,0:T(4,128)S(1)} %shard_map.98.after_ref.refs_0_), channel_id=1, source_target_pairs={{0,1},{1,0},{2,3},{3,2},{4,5},{5,4},{6,7},{7,6},{8,9},{9,8},{10,11... | collective-permute-start | bytes 73736 | tf_op jit(solution)/shard_map/ppermute | solution.py:467
  26.9 0.9 %collective-permute-done.1.refs_1_ = f32[3,2048]{1,0:T(4,128)S(1)} collective-permute-done((f32[3,2048]{1,0:T(4,128)S(1)}, f32[3,2048]{1,0:T(4,128)S(1)}, u32[]{:S(2)}, u32[]{:S(2)}) %collective-permute-start.1) | collective-permute-done | bytes 24608 | tf_op jit(solution)/shard_map/ppermute | solution.py:467
  27.8 1.9 %shard_map.100.after_ref.refs_0_ = f32[3,2048]{1,0:T(4,128)S(1)} custom-call(f32[16,2048]{1,0:T(8,128)S(1)} %get-tuple-element.13.row_ref, f32[3,1024]{1,0:T(4,128)S(1)} %get-tuple-element.17.own_coil_ref, f32[3,1024]{1,0:T(4,128)S(1)} %collective-permute-done.other_coil_ref, f32[3,2048]{1,0:T(4,128)S(1)} %shard_map.98.after_ref.refs_0_, ...), custom_call_target="tpu_custom_call" | custom-call | tf_op jit(solution)/shard_map/pallas_call | solution.py:445
  29.7 0.4 %collective-permute-start.2 = (f32[3,2048]{1,0:T(4,128)S(1)}, f32[3,2048]{1,0:T(4,128)S(1)}, u32[]{:S(2)}, u32[]{:S(2)}) collective-permute-start(f32[3,2048]{1,0:T(4,128)S(1)} %shard_map.100.after_ref.refs_0_), channel_id=1, source_target_pairs={{0,1},{1,0},{2,3},{3,2},{4,5},{5,4},{6,7},{7,6},{8,9},{9,8},{10,11... | collective-permute-start | bytes 73736 | tf_op jit(solution)/shard_map/ppermute | solution.py:467
  30.1 0.7 %shard_map.99.segment_ref = f32[3,128]{1,0:T(4,128)S(1)} custom-call(f32[16,2048]{1,0:T(8,128)S(1)} %get-tuple-element.13.row_ref, f32[2048,8]{1,0:T(8,128)S(1)} %get-tuple-element.14.col_ref, bf16[48,2048]{1,0:T(8,128)(2,1)S(1)} %get-tuple-element.16.split_ref, f32[3,2048]{1,0:T(4,128)S(1)} %shard_map.98.after_ref.refs_0_), custom_call_target="tpu_custom_call" | custom-call | tf_op jit(solution)/shard_map/pallas_call | solution.py:445
  30.8 0.7 %shard_map.101 = (bf16[128,2048]{1,0:T(8,128)(2,1)S(1)}, bf16[128,2048]{1,0:T(8,128)(2,1)S(1)}) custom-call(f32[16,2048]{1,0:T(8,128)S(1)} %get-tuple-element.13.row_ref, f32[2048,8]{1,0:T(8,128)S(1)} %get-tuple-element.14.col_ref, f32[3,2048]{1,0:T(4,128)S(1)} %shard_map.100.after_ref.refs_0_), custom_call_target="tpu_custom_call" | custom-call | tf_op jit(solution)/shard_map/pallas_call | solution.py:445
  31.5 0.0 collective-permute-done.2.refs_1_
  31.5 1.1 %shard_map.102 = (f32[3,128]{1,0:T(4,128)}, f32[3,128]{1,0:T(4,128)}) custom-call(f32[16,2048]{1,0:T(8,128)S(1)} %get-tuple-element.13.row_ref, f32[2048,8]{1,0:T(8,128)S(1)} %get-tuple-element.14.col_ref, f32[1,128]{1,0:T(1,128)S(1)} %get-tuple-element.15.chi_ref, f32[3,128]{1,0:T(4,128)S(1)} %shard_map.99.segment_ref, ...), custom_call_target="tpu_custom_call" | custom-call | tf_op jit(solution)/shard_map/pallas_call | solution.py:445
Async XLA Ops:
  21.3 3.2 %collective-permute-start = (f32[3,1024]{1,0:T(4,128)S(1)}, f32[3,1024]{1,0:T(4,128)S(1)}, u32[]{:S(2)}, u32[]{:S(2)}) collective-permute-start(f32[3,1024]{1,0:T(4,128)S(1)} %get-tuple-element.17.own_coil_ref), channel_id=1, source_target_pairs={{0,1},{1,0},{2,3},{3,2},{4,5},{5,4},{6,7},{7,6},{8,9},{9,8},{10,11... | collective-permute-start | bytes 36872 | tf_op jit(solution)/shard_map/ppermute | solution.py:467
  26.4 1.4 %collective-permute-start.1 = (f32[3,2048]{1,0:T(4,128)S(1)}, f32[3,2048]{1,0:T(4,128)S(1)}, u32[]{:S(2)}, u32[]{:S(2)}) collective-permute-start(f32[3,2048]{1,0:T(4,128)S(1)} %shard_map.98.after_ref.refs_0_), channel_id=1, source_target_pairs={{0,1},{1,0},{2,3},{3,2},{4,5},{5,4},{6,7},{7,6},{8,9},{9,8},{10,11... | collective-permute-start | bytes 73736 | tf_op jit(solution)/shard_map/ppermute | solution.py:467
  29.7 1.9 %collective-permute-start.2 = (f32[3,2048]{1,0:T(4,128)S(1)}, f32[3,2048]{1,0:T(4,128)S(1)}, u32[]{:S(2)}, u32[]{:S(2)}) collective-permute-start(f32[3,2048]{1,0:T(4,128)S(1)} %shard_map.100.after_ref.refs_0_), channel_id=1, source_target_pairs={{0,1},{1,0},{2,3},{3,2},{4,5},{5,4},{6,7},{7,6},{8,9},{9,8},{10,11... | collective-permute-start | bytes 73736 | tf_op jit(solution)/shard_map/ppermute | solution.py:467

commit v4 on v3

--- a/solution.py
+++ b/solution.py
@@ -1,3 +1,4 @@
+import functools
 import math
 
 import jax
@@ -203,8 +204,8 @@
     suscept = pick(table_ref, panel_ref)
     chi_ref[...] = suscept
     rows = [pos_ref[k : k + 1, :] for k in range(3)]
+    rows += [weight_ref[...] * suscept]
     rows += [mid[k : k + 1] for k in range(3)]
-    rows += [weight_ref[...] * suscept]
     rows += [carried[k : k + 1] for k in range(3)]
     for block in range(out_ref.shape[0]):
         for place, row in enumerate(rows):
@@ -222,20 +223,45 @@
     return total
 
 
-def power_parts(deltas, core, power):
-    dx, dy, dz = deltas
-    inverse = lax.rsqrt(dx * dx + dy * dy + dz * dz + core * core)
-    square = inverse * inverse
-    return bf16_parts(square * inverse if power == 3 else square * square * inverse, 2)
-
-
-def deltas_of(rows, columns, first):
-    return [rows[k] - columns[:, first + k : first + k + 1] for k in range(3)]
+def square_factor(tile, core=None):
+    place = lax.broadcasted_iota(jnp.int32, tile.shape, 0)
+    points = jnp.where(place < 3, tile, 0.0)
+    high, mid, low = [part.astype(jnp.float32) for part in bf16_parts(points, 3)]
+    norm = jnp.sum(points * points, axis=0, keepdims=True)
+    if core is not None:
+        norm = norm + core * core
+    norms = [part.astype(jnp.float32) for part in bf16_parts(norm, 3)]
+    first = 0 if core is None else 3
+    last = jnp.where(place < 6, 1.0, 0.0)
+    for k in range(3):
+        last = jnp.where(place == first + k, norms[k], last)
+    if core is None:
+        high, mid, low = -2.0 * high, -2.0 * mid, -2.0 * low
+        groups = [high, mid, high, mid, low, high]
+    else:
+        groups = [high, high, mid, mid, high, low]
+    groups += [last, jnp.zeros_like(last)]
+    return jnp.concatenate(groups, 0).astype(jnp.bfloat16)
+
+
+def source_factor(tile, core, out_ref):
+    for start in range(0, tile.shape[1], 128):
+        factor = square_factor(tile[:, start : start + 128], core)
+        out_ref[start : start + 128, :] = factor.T
+
+
+def power_parts(square, power):
+    inverse = lax.rsqrt(square)
+    below = inverse * inverse
+    return bf16_parts(below * inverse if power == 3 else below * below * inverse, 2)
+
+
+def squares(sources, targets):
+    return jnp.dot(sources, targets, preferred_element_type=jnp.float32)
 
 
 def coil_rows(row_ref):
-    mx, my, mz = [row_ref[3 + k : 4 + k, :] for k in range(3)]
-    cx, cy, cz = [row_ref[7 + k : 8 + k, :] for k in range(3)]
+    mx, my, mz, cx, cy, cz = [row_ref[8 + k : 9 + k, :] for k in range(6)]
     blank = jnp.zeros((10, row_ref.shape[1]), jnp.float32)
     crossed = [cy * mz - cz * my, cz * mx - cx * mz, cx * my - cy * mx]
     return jnp.concatenate([cx, cy, cz] + crossed + [blank], 0)
@@ -249,37 +275,50 @@
     return (field - sums[3:6]) * (1.0 / math.sqrt(total))
 
 
-def coil_stage(gathered_ref, row_ref, col_ref, split_ref, field_ref, *weight_refs):
+def coil_stage(
+    gathered_ref,
+    row_ref,
+    segment_factor_ref,
+    yoke_factor_ref,
+    target_factor_ref,
+    split_ref,
+    field_ref,
+    *weight_refs,
+):
     blocks = gathered_ref.shape[0]
     total = row_ref.shape[1]
     half, width = total // 2, total // blocks
     core = lax.axis_index("yoke")
+    row_ref[...] = jnp.zeros_like(row_ref)
     for block in range(blocks):
         near = block < blocks // 2
         source = 2 * (block % (blocks // 2)) + (core if near else 1 - core)
         for k in range(10):
-            row_ref[k : k + 1, block * width : (block + 1) * width] = gathered_ref[
+            row = k if k < 4 else k + 4
+            row_ref[row : row + 1, block * width : (block + 1) * width] = gathered_ref[
                 source, :, k * width : (k + 1) * width
             ]
     center = jnp.sum(row_ref[0:3, :], axis=1, keepdims=True) * (1.0 / total)
-    shift = jnp.concatenate([center, center, jnp.zeros((2, 1), jnp.float32)], 0)
-    row_ref[0:8, :] = row_ref[0:8, :] - shift
-    for block in range(blocks):
-        at = slice(block * width, (block + 1) * width)
-        col_ref[at, :] = row_ref[0:8, at].T
+    shift = jnp.concatenate([center, jnp.zeros((5, 1), jnp.float32)], 0)
+    yoke = row_ref[0:8, :] - shift
+    segments = row_ref[8:16, :] - shift
+    row_ref[0:8, :] = yoke
+    row_ref[8:16, :] = segments
+    target_factor_ref[...] = square_factor(yoke)
+    source_factor(segments, coil_core, segment_factor_ref)
+    source_factor(yoke[:, :half], yoke_core, yoke_factor_ref)
     split_rows(coil_rows(row_ref), split_ref)
     targets = [row_ref[k : k + 1, :half] for k in range(3)]
-    depth, step = 256, 32
+    depth = 256
     count = total // depth
     product = jnp.zeros((split_ref.shape[0], half), jnp.float32)
 
     def build(chunk):
         part_refs = weight_refs[2 * (chunk % 2) : 2 * (chunk % 2) + 2]
-        for start in range(0, depth, step):
-            sources = col_ref[chunk * depth + start : chunk * depth + start + step, :]
-            parts = power_parts(deltas_of(targets, sources, 3), coil_core, 3)
-            for ref, part in zip(part_refs, parts):
-                ref[start : start + step, :] = part
+        sources = segment_factor_ref[chunk * depth : (chunk + 1) * depth, :]
+        parts = power_parts(squares(sources, target_factor_ref[:, :half]), 3)
+        for ref, part in zip(part_refs, parts):
+            ref[...] = part
 
     build(0)
     for chunk in range(count):
@@ -307,21 +346,18 @@
     return jnp.concatenate([array[:, k * depth : (k + 1) * depth] for k in blocks], 1)
 
 
-def spread_stage(row_ref, col_ref, *part_refs):
-    depth, _, rows = plan(row_ref.shape[1])
-    step = 32
+def spread_stage(source_factor_ref, target_factor_ref, *part_refs):
+    depth, _, rows = plan(target_factor_ref.shape[1])
     for block, place, blocks in rows:
-        targets = [lanes_of(row_ref[k : k + 1, :], blocks, depth) for k in range(3)]
+        targets = lanes_of(target_factor_ref, blocks, depth)
         lanes = slice(place * depth, (place + len(blocks)) * depth)
-        for start in range(0, depth, step):
-            sources = col_ref[block * depth + start : block * depth + start + step, :]
-            parts = power_parts(deltas_of(targets, sources, 0), yoke_core, 5)
-            for ref, part in zip(part_refs, parts):
-                ref[start : start + step, lanes] = part
+        sources = source_factor_ref[block * depth : (block + 1) * depth, :]
+        for ref, part in zip(part_refs, power_parts(squares(sources, targets), 5)):
+            ref[:, lanes] = part
 
 
 def source_rows(row_ref, field, split_ref):
-    strength = row_ref[6:7, :] * field
+    strength = row_ref[3:4, :] * field
     ux, uy, uz = [strength[k : k + 1] for k in range(3)]
     qx, qy, qz = [row_ref[k : k + 1, :] for k in range(3)]
     along = 3.0 * (qx * ux + qy * uy + qz * uz)
@@ -372,7 +408,8 @@
     return field
 
 
-def sweep_stage(row_ref, own_coil_ref, other_coil_ref, *refs):
+def sweep_stage(skip, *refs):
+    row_ref, own_coil_ref, other_coil_ref, *refs = refs[skip:]
     partial_refs, part_refs, (out_ref, split_ref) = refs[:-4], refs[-4:-2], refs[-2:]
     total = row_ref.shape[1]
     source_rows(row_ref, whole_field(own_coil_ref, other_coil_ref, partial_refs), split_ref)
@@ -395,29 +432,27 @@
     out_ref[...] = dipole_field(jnp.concatenate(product, 1), targets, total)
 
 
-def own_segments(row_ref, col_ref, width):
-    at = pl.ds(pl.multiple_of(lax.axis_index("seg") * width, width), width)
-    return row_ref[:, at], col_ref[at, :]
-
-
-def segment_coil_stage(row_ref, col_ref, split_ref, after_ref, out_ref):
+def own_at(width):
+    return pl.ds(pl.multiple_of(lax.axis_index("seg") * width, width), width)
+
+
+def segment_coil_stage(row_ref, factor_ref, split_ref, after_ref, out_ref):
     total = row_ref.shape[1]
-    rows, columns = own_segments(row_ref, col_ref, out_ref.shape[1])
-    sources = [row_ref[3 + k : 4 + k, :] for k in range(3)]
-    parts = power_parts(deltas_of(sources, columns, 3), coil_core, 3)
-    product = times(split_ref[...], parts, True)
-    out_ref[...] = coil_field(product, [rows[3 + k : 4 + k] for k in range(3)], total)
-
-
-def segment_spread_stage(row_ref, col_ref, after_ref, *part_refs):
-    _, columns = own_segments(row_ref, col_ref, part_refs[0].shape[0])
-    sources = [row_ref[k : k + 1, :] for k in range(3)]
-    parts = power_parts(deltas_of(sources, columns, 3), yoke_core, 5)
-    for ref, part in zip(part_refs, parts):
+    own = row_ref[8:16, own_at(out_ref.shape[1])]
+    parts = power_parts(squares(factor_ref[...], square_factor(own)), 3)
+    product = times(split_ref[...], parts)
+    out_ref[...] = coil_field(product, [own[k : k + 1] for k in range(3)], total)
+
+
+def segment_spread_stage(segment_factor_ref, target_factor_ref, after_ref, *part_refs):
+    own = segment_factor_ref[own_at(part_refs[0].shape[0]), :]
+    square = squares(own, target_factor_ref[...])
+    square = square + (yoke_core * yoke_core - coil_core * coil_core)
+    for ref, part in zip(part_refs, power_parts(square, 5)):
         ref[...] = part
 
 
-def force_stage(row_ref, col_ref, chi_ref, segment_ref, own_coil_ref, other_coil_ref, *refs):
+def force_stage(row_ref, chi_ref, segment_ref, own_coil_ref, other_coil_ref, *refs):
     partial_refs, part_refs, (lorentz_ref, moment_ref, split_ref, field_ref) = (
         refs[:2],
         refs[2:4],
@@ -426,16 +461,16 @@
     total, width = row_ref.shape[1], chi_ref.shape[1]
     field = whole_field(own_coil_ref, other_coil_ref, partial_refs)
     field_ref[...] = field
-    at = pl.ds(pl.multiple_of(lax.axis_index("seg") * width, width), width)
+    at = own_at(width)
     moment_ref[...] = chi_ref[...] * field_ref[:, at]
     source_rows(row_ref, field, split_ref)
-    rows, _ = own_segments(row_ref, col_ref, width)
+    own = row_ref[8:16, at]
     product = times(split_ref[...], [ref[...] for ref in part_refs], True)
     field = segment_ref[...] + dipole_field(
-        product, [rows[3 + k : 4 + k] for k in range(3)], total
+        product, [own[k : k + 1] for k in range(3)], total
     )
     fx, fy, fz = [field[k : k + 1] for k in range(3)]
-    cx, cy, cz = [rows[7 + k : 8 + k] for k in range(3)]
+    cx, cy, cz = [own[3 + k : 4 + k] for k in range(3)]
     lorentz_ref[...] = jnp.concatenate(
         [cy * fz - cz * fy, cz * fx - cx * fz, cx * fy - cy * fx], 0
     )
@@ -488,21 +523,35 @@
     gathered = lax.all_to_all(packed, ("seg", "yoke"), 0, 0, tiled=True)
     split_shape = shape(48, total, kind=bf16)
     split_scratch = pltpu.VMEM((48, total), bf16)
-    rows, columns, split, coil = call(
+    rows, segment_factor, yoke_factor, target_factor, split, coil = call(
         coil_stage,
-        (shape(16, total), shape(total, 8), split_shape, shape(3, half)),
+        (
+            shape(16, total),
+            shape(total, 64, kind=bf16),
+            shape(half, 64, kind=bf16),
+            shape(64, total, kind=bf16),
+            split_shape,
+            shape(3, half),
+        ),
         [pltpu.VMEM((256, half), bf16)] * 4,
         gathered,
     )
     coils = (coil, swap(coil))
     depth, count, _ = plan(total)
-    spread = call(spread_stage, [shape(depth, count * depth, kind=bf16)] * 2, [], rows, columns)
-    partials = ()
+    spread = call(
+        spread_stage,
+        [shape(depth, count * depth, kind=bf16)] * 2,
+        [],
+        yoke_factor,
+        target_factor,
+    )
+    partials, after = (), ()
     for sweep in range(ITERS):
         own = call(
-            sweep_stage,
+            functools.partial(sweep_stage, len(after)),
             shape(3, total),
             [split_scratch],
+            *after,
             rows,
             *coils,
             *partials,
@@ -511,18 +560,18 @@
         partials = (own, swap(own))
         if sweep == 0:
             segments = call(
-                segment_coil_stage, shape(3, width), [], rows, columns, split, own
+                segment_coil_stage, shape(3, width), [], rows, segment_factor, split, own
             )
+            after = (segments,)
         if sweep == ITERS - 1:
             near = [shape(width, total, kind=bf16)] * 2
-            near = call(segment_spread_stage, near, [], rows, columns, own)
+            near = call(segment_spread_stage, near, [], segment_factor, target_factor, own)
     return tuple(
         call(
             force_stage,
             (shape(3, width), shape(3, width)),
             [split_scratch, pltpu.VMEM((3, total), f32)],
             rows,
-            columns,
             chi,
             segments,
             *coils,

time: 32.8 us -> 28.6 us (0.87)
  Pallas kernels: 15.7 us -> 11.8 us
    pallas_call x8, Pallas kernels: 15.7 us -> 11.8 us  [call(): pl.pallas_call(kernel, out_shape=outputs, scratch_shapes=scratch, compile...]
  transfers between devices with their start and end apart: 3 -> 3, of which waited for: 1 -> 2; matrix products, arithmetic and copies ran while one was open for 0% -> 0% of each run, Pallas kernels for 14% -> 10%
where the time goes in v4:
time: 28.6 us; the launch traced here: 28.4 us
  blocking collectives  14.3 us (50%)
  Pallas kernels  11.8 us (41%)
  starting transfers between devices  1.01 us (4%)
  between operations  0.7 us (2%)
  waiting for transfers between devices  0.56 us (2%)
    all_to_all x1, blocking collectives, close_body(): gathered = lax.all_to_all(packed, ('seg', 'yoke'), 0, 0, tiled=True)  14.3 us
    pallas_call x8, Pallas kernels, call(): pl.pallas_call(kernel, out_shape=outputs, scratch_shapes=scratch, compile...  11.8 us
    ppermute x3, starting transfers between devices, swap(): return lax.ppermute(field, 'yoke', [(0, 1), (1, 0)])  1.01 us
  transfers between devices with their start and end apart: 3, of which 2 were waited for; matrix products, arithmetic and copies ran while one was open for 0% of the time, Pallas kernels for 10%

profile of v4, /device:TPU:0, one launch (start us, length us, event | category | flops | bytes accessed | tf_op | source)
XLA Modules:
  0.0 28.4 jit_solution(6030271901321281296)
XLA Ops:
  0.6 1.1 %shard_map.95 = (f32[16,1,1280]{2,1,0:T(1,128)S(1)}, f32[1,128]{1,0:T(1,128)S(1)}) custom-call(f32[3,256]{1,0:T(4,128)} %refs_0_.1, f32[3,256]{1,0:T(4,128)} %refs_1_.1, s32[1,256]{1,0:T(1,128)} %bitcast.5, f32[1,256]{1,0:T(1,128)} %bitcast.6, f32[3,128]{1,0:T(4,128)} %refs_4_.1, f32[1,128]{1,0:T(1,128)} %bitcast.7, s32[1,128]{1,0:T(1,128)} %bitcast.8, ...), custom_call_target="tpu_custom_call" | custom-call | tf_op jit(solution)/shard_map/pallas_call | solution.py:480
  1.8 14.3 %all_to_all.5.gathered_ref = f32[16,1,1280]{2,1,0:T(1,128)S(1)} all-to-all(f32[16,1,1280]{2,1,0:T(1,128)S(1)} %get-tuple-element.14), channel_id=1, replica_groups=mesh['grp'=2,'seg'=8,'yoke'=2] {'seg','yoke'}, dimensions={0} | all-to-all | bytes 163840 | tf_op jit(solution)/shard_map/all_to_all | solution.py:523
  16.1 3.0 %shard_map.96 = (f32[16,2048]{1,0:T(8,128)S(1)}, bf16[2048,64]{1,0:T(8,128)(2,1)S(1)}, bf16[1024,64]{1,0:T(8,128)(2,1)S(1)}, bf16[64,2048]{1,0:T(8,128)(2,1)S(1)...) custom-call(f32[16,1,1280]{2,1,0:T(1,128)S(1)} %all_to_all.5.gathered_ref), custom_call_target="tpu_custom_call" | custom-call | tf_op jit(solution)/shard_map/pallas_call | solution.py:480
  19.1 0.1 collective-permute-start
  19.2 1.8 %shard_map.97 = (bf16[256,5120]{1,0:T(8,128)(2,1)S(1)}, bf16[256,5120]{1,0:T(8,128)(2,1)S(1)}) custom-call(bf16[1024,64]{1,0:T(8,128)(2,1)S(1)} %get-tuple-element.20.source_factor_ref, bf16[64,2048]{1,0:T(8,128)(2,1)S(1)} %get-tuple-element.21.target_factor_ref), custom_call_target="tpu_custom_call" | custom-call | tf_op jit(solution)/shard_map/pallas_call | solution.py:480
  20.9 0.0 collective-permute-done.refs_2_.refs_3_.other_coil_ref
  20.9 1.9 %shard_map.98.after_ref.refs_4_ = f32[3,2048]{1,0:T(4,128)S(1)} custom-call(f32[16,2048]{1,0:T(8,128)S(1)} %get-tuple-element.15.refs_0_.row_ref.refs_1_, f32[3,1024]{1,0:T(4,128)S(1)} %get-tuple-element.19.refs_1_.refs_2_.own_coil_ref, f32[3,1024]{1,0:T(4,128)S(1)} %collective-permute-done.refs_2_.refs_3_.other_coil_ref, ...), custom_call_target="tpu_custom_call" | custom-call | tf_op jit(solution)/shard_map/pallas_call | solution.py:480
  22.8 0.5 %collective-permute-start.1 = (f32[3,2048]{1,0:T(4,128)S(1)}, f32[3,2048]{1,0:T(4,128)S(1)}, u32[]{:S(2)}, u32[]{:S(2)}) collective-permute-start(f32[3,2048]{1,0:T(4,128)S(1)} %shard_map.98.after_ref.refs_4_), channel_id=1, source_target_pairs={{0,1},{1,0},{2,3},{3,2},{4,5},{5,4},{6,7},{7,6},{8,9},{9,8},{10,11... | collective-permute-start | bytes 73736 | tf_op jit(solution)/shard_map/ppermute | solution.py:502
  23.3 0.7 %shard_map.99.refs_0_.segment_ref = f32[3,128]{1,0:T(4,128)S(1)} custom-call(f32[16,2048]{1,0:T(8,128)S(1)} %get-tuple-element.15.refs_0_.row_ref.refs_1_, bf16[2048,64]{1,0:T(8,128)(2,1)S(1)} %get-tuple-element.17.factor_ref.segment_factor_ref, bf16[48,2048]{1,0:T(8,128)(2,1)S(1)} %get-tuple-element.18.split_ref, f32[3,2048]{1,0:T(4,128)S(1)} %shard_map.98.after_ref.refs_4_), custom_call_target="tpu_custom_call" | custom-call | tf_op jit(solution)/shard_map/pallas_call | solution.py:480
  24.0 0.2 collective-permute-done.1.refs_5_
  24.2 1.9 %shard_map.100.after_ref.refs_0_ = f32[3,2048]{1,0:T(4,128)S(1)} custom-call(f32[3,128]{1,0:T(4,128)S(1)} %shard_map.99.refs_0_.segment_ref, f32[16,2048]{1,0:T(8,128)S(1)} %get-tuple-element.15.refs_0_.row_ref.refs_1_, f32[3,1024]{1,0:T(4,128)S(1)} %get-tuple-element.19.refs_1_.refs_2_.own_coil_ref, ...), custom_call_target="tpu_custom_call" | custom-call | tf_op jit(solution)/shard_map/pallas_call | solution.py:480
  26.1 0.4 %collective-permute-start.2 = (f32[3,2048]{1,0:T(4,128)S(1)}, f32[3,2048]{1,0:T(4,128)S(1)}, u32[]{:S(2)}, u32[]{:S(2)}) collective-permute-start(f32[3,2048]{1,0:T(4,128)S(1)} %shard_map.100.after_ref.refs_0_), channel_id=1, source_target_pairs={{0,1},{1,0},{2,3},{3,2},{4,5},{5,4},{6,7},{7,6},{8,9},{9,8},{10,11... | collective-permute-start | bytes 73736 | tf_op jit(solution)/shard_map/ppermute | solution.py:502
  26.5 0.5 %shard_map.101 = (bf16[128,2048]{1,0:T(8,128)(2,1)S(1)}, bf16[128,2048]{1,0:T(8,128)(2,1)S(1)}) custom-call(bf16[2048,64]{1,0:T(8,128)(2,1)S(1)} %get-tuple-element.17.factor_ref.segment_factor_ref, bf16[64,2048]{1,0:T(8,128)(2,1)S(1)} %get-tuple-element.21.target_factor_ref, f32[3,2048]{1,0:T(4,128)S(1)} %shard_map.100.after_ref.refs_0_), custom_call_target="tpu_custom_call" | custom-call | tf_op jit(solution)/shard_map/pallas_call | solution.py:480
  27.0 0.4 %collective-permute-done.2.refs_1_ = f32[3,2048]{1,0:T(4,128)S(1)} collective-permute-done((f32[3,2048]{1,0:T(4,128)S(1)}, f32[3,2048]{1,0:T(4,128)S(1)}, u32[]{:S(2)}, u32[]{:S(2)}) %collective-permute-start.2) | collective-permute-done | bytes 24608 | tf_op jit(solution)/shard_map/ppermute | solution.py:502
  27.3 1.1 %shard_map.102 = (f32[3,128]{1,0:T(4,128)}, f32[3,128]{1,0:T(4,128)}) custom-call(f32[16,2048]{1,0:T(8,128)S(1)} %get-tuple-element.15.refs_0_.row_ref.refs_1_, f32[1,128]{1,0:T(1,128)S(1)} %get-tuple-element.16.chi_ref, f32[3,128]{1,0:T(4,128)S(1)} %shard_map.99.refs_0_.segment_ref, f32[3,1024]{1,0:T(4,128)S(1)} %get-tuple-element.19.refs_1_.refs_2_.own_coil_ref, ...), custom_call_target="tpu_custom_call" | custom-call | tf_op jit(solution)/shard_map/pallas_call | solution.py:480
Async XLA Ops:
  19.1 1.8 %collective-permute-start = (f32[3,1024]{1,0:T(4,128)S(1)}, f32[3,1024]{1,0:T(4,128)S(1)}, u32[]{:S(2)}, u32[]{:S(2)}) collective-permute-start(f32[3,1024]{1,0:T(4,128)S(1)} %get-tuple-element.19.refs_1_.refs_2_.own_coil_ref), channel_id=1, source_target_pairs={{0,1},{1,0},{2,3},{3,2},{4,5},{5,4},{6,7},{7,6},{8,9},{9,8},{10,11... | collective-permute-start | bytes 36872 | tf_op jit(solution)/shard_map/ppermute | solution.py:502
  22.8 1.4 %collective-permute-start.1 = (f32[3,2048]{1,0:T(4,128)S(1)}, f32[3,2048]{1,0:T(4,128)S(1)}, u32[]{:S(2)}, u32[]{:S(2)}) collective-permute-start(f32[3,2048]{1,0:T(4,128)S(1)} %shard_map.98.after_ref.refs_4_), channel_id=1, source_target_pairs={{0,1},{1,0},{2,3},{3,2},{4,5},{5,4},{6,7},{7,6},{8,9},{9,8},{10,11... | collective-permute-start | bytes 73736 | tf_op jit(solution)/shard_map/ppermute | solution.py:502
  26.1 1.3 %collective-permute-start.2 = (f32[3,2048]{1,0:T(4,128)S(1)}, f32[3,2048]{1,0:T(4,128)S(1)}, u32[]{:S(2)}, u32[]{:S(2)}) collective-permute-start(f32[3,2048]{1,0:T(4,128)S(1)} %shard_map.100.after_ref.refs_0_), channel_id=1, source_target_pairs={{0,1},{1,0},{2,3},{3,2},{4,5},{5,4},{6,7},{7,6},{8,9},{9,8},{10,11... | collective-permute-start | bytes 73736 | tf_op jit(solution)/shard_map/ppermute | solution.py:502

commit v5 on v0

--- a/solution.py
+++ b/solution.py
@@ -3,9 +3,12 @@
 import jax
 import jax.numpy as jnp
 from jax import lax
+from jax.experimental import pallas as pl
+from jax.experimental.pallas import tpu as pltpu
 from jax.sharding import PartitionSpec as P
 
 ITERS = 2
+VMEM_BYTES = 16 << 20
 
 
 coil_core = 0.05
@@ -107,7 +110,7 @@
     return jnp.sum(jnp.where(indices[None, :] == rows_iota, table[:, None], 0.0), axis=0)
 
 
-def body(seg_mid, seg_vec, strand_of, strand_current, yoke_pos, quad_weight, panel_of, panel_chi):
+def far_body(seg_mid, seg_vec, strand_of, strand_current, yoke_pos, quad_weight, panel_of, panel_chi):
     seg_len = seg_mid.shape[1]
     half_len = seg_len // 2
     yoke_len = yoke_pos.shape[1]
@@ -150,6 +153,549 @@
     return (lorentz, moment)
 
 
+def bf16_parts(value, count):
+    parts = []
+    for place in range(count):
+        part = value.astype(jnp.bfloat16)
+        parts.append(part)
+        if place + 1 < count:
+            value = value - part.astype(jnp.float32)
+    return parts
+
+
+def split_rows(rows, split_ref):
+    count = rows.shape[0]
+    for place, part in enumerate(bf16_parts(rows, 3)):
+        split_ref[place * count : (place + 1) * count, :] = part
+
+
+def joined(product):
+    count = product.shape[0] // 3
+    return product[:count] + product[count : 2 * count] + product[2 * count :]
+
+
+def pick(table_ref, index):
+    entries = lax.broadcasted_iota(jnp.int32, (table_ref.shape[1], index.shape[1]), 0)
+    chosen = jnp.where(entries == index, 1.0, 0.0).astype(jnp.bfloat16)
+    parts = [part.astype(jnp.float32) for part in bf16_parts(table_ref[...], 3)]
+    blank = jnp.zeros((5, table_ref.shape[1]), jnp.float32)
+    table = jnp.concatenate(parts + [blank], 0).astype(jnp.bfloat16)
+    found = jnp.dot(table, chosen, preferred_element_type=jnp.float32)
+    return found[0:1] + found[1:2] + found[2:3]
+
+
+def pack_kernel(*refs):
+    sources, (out_ref, chi_ref), held, sems = refs[:8], refs[8:10], refs[10:18], refs[18]
+    copies = [
+        pltpu.make_async_copy(source, target, sems.at[place])
+        for place, (source, target) in enumerate(zip(sources, held))
+    ]
+    for copy in copies:
+        copy.start()
+    for copy in copies:
+        copy.wait()
+    mid_ref, vec_ref, strand_ref, current_ref, pos_ref, weight_ref, panel_ref, table_ref = held
+    half = pos_ref.shape[1]
+    first = lax.axis_index("yoke") == 0
+
+    def own(ref):
+        return jnp.where(first, ref[:, :half], ref[:, half:])
+
+    mid = own(mid_ref)
+    carried = pick(current_ref, own(strand_ref)) * own(vec_ref)
+    suscept = pick(table_ref, panel_ref[...])
+    chi_ref[...] = suscept
+    rows = [pos_ref[k : k + 1, :] for k in range(3)]
+    rows += [weight_ref[...] * suscept]
+    rows += [mid[k : k + 1] for k in range(3)]
+    rows += [carried[k : k + 1] for k in range(3)]
+    for place, row in enumerate(rows):
+        out_ref[0, :, place * half : (place + 1) * half] = row
+
+
+def join_kernel(*refs):
+    place = 0
+    for ref in refs[:-1]:
+        for block in range(ref.shape[0]):
+            refs[-1][place] = ref[block]
+            place += 1
+
+
+def times(rows, matrix_parts, transposed=False):
+    contracted = ((1,), (1 if transposed else 0,))
+    total = None
+    for part in matrix_parts:
+        product = lax.dot_general(
+            rows, part, (contracted, ((), ())), preferred_element_type=jnp.float32
+        )
+        total = product if total is None else total + product
+    return total
+
+
+def square_factor(tile, core=None):
+    place = lax.broadcasted_iota(jnp.int32, tile.shape, 0)
+    points = jnp.where(place < 3, tile, 0.0)
+    high, mid, low = [part.astype(jnp.float32) for part in bf16_parts(points, 3)]
+    norm = jnp.sum(points * points, axis=0, keepdims=True)
+    if core is not None:
+        norm = norm + core * core
+    norms = [part.astype(jnp.float32) for part in bf16_parts(norm, 3)]
+    first = 0 if core is None else 3
+    last = jnp.where(place < 6, 1.0, 0.0)
+    for k in range(3):
+        last = jnp.where(place == first + k, norms[k], last)
+    if core is None:
+        high, mid, low = -2.0 * high, -2.0 * mid, -2.0 * low
+        groups = [high, mid, high, mid, low, high]
+    else:
+        groups = [high, high, mid, mid, high, low]
+    groups += [last, jnp.zeros_like(last)]
+    return jnp.concatenate(groups, 0).astype(jnp.bfloat16)
+
+
+def source_factor(tile, core, out_ref):
+    for start in range(0, tile.shape[1], 128):
+        factor = square_factor(tile[:, start : start + 128], core)
+        out_ref[start : start + 128, :] = factor.T
+
+
+def power_parts(square, power):
+    inverse = lax.rsqrt(square)
+    below = inverse * inverse
+    return bf16_parts(below * inverse if power == 3 else below * below * inverse, 2)
+
+
+def squares(sources, targets):
+    return jnp.dot(sources, targets, preferred_element_type=jnp.float32)
+
+
+def coil_rows(segments):
+    mx, my, mz, cx, cy, cz = [segments[k : k + 1] for k in range(6)]
+    blank = jnp.zeros((10, segments.shape[1]), jnp.float32)
+    crossed = [cy * mz - cz * my, cz * mx - cx * mz, cx * my - cy * mx]
+    return jnp.concatenate([cx, cy, cz] + crossed + [blank], 0)
+
+
+def coil_field(sums, targets, total):
+    tx, ty, tz = targets
+    sx, sy, sz = [sums[k : k + 1] for k in range(3)]
+    field = jnp.concatenate([sy * tz - sz * ty, sz * tx - sx * tz, sx * ty - sy * tx], 0)
+    return (field - sums[3:6]) * (1.0 / math.sqrt(total))
+
+
+def place_rows(gathered_ref, row_ref):
+    blocks, half = gathered_ref.shape[0], row_ref.shape[1]
+    width = half // blocks
+    row_ref[...] = jnp.zeros_like(row_ref)
+    for block in range(blocks):
+        for k in range(10):
+            row = k if k < 4 else k + 4
+            row_ref[row : row + 1, block * width : (block + 1) * width] = gathered_ref[
+                block, :, k * width : (k + 1) * width
+            ]
+
+
+def build_and_apply(factor_ref, targets, power, split_ref, part_refs):
+    depth = 256
+    count = factor_ref.shape[0] // depth
+    slots = part_refs[0].shape[0] // depth
+    product = jnp.zeros((split_ref.shape[0], targets.shape[1]), jnp.float32)
+
+    def slot(chunk):
+        start = chunk % slots * depth
+        return slice(start, start + depth)
+
+    def build(chunk):
+        sources = factor_ref[chunk * depth : (chunk + 1) * depth, :]
+        for ref, part in zip(part_refs, power_parts(squares(sources, targets), power)):
+            ref[slot(chunk), :] = part
+
+    build(0)
+    for chunk in range(count):
+        if chunk + 1 < count:
+            build(chunk + 1)
+        rows = split_ref[:, chunk * depth : (chunk + 1) * depth]
+        product = product + times(rows, [ref[slot(chunk), :] for ref in part_refs])
+    return joined(product)
+
+
+def apply(split_ref, part_refs):
+    depth = 256
+    product = jnp.zeros((split_ref.shape[0], part_refs[0].shape[1]), jnp.float32)
+    for start in range(0, split_ref.shape[1], depth):
+        rows = split_ref[:, start : start + depth]
+        product = product + times(rows, [ref[start : start + depth, :] for ref in part_refs])
+    return joined(product)
+
+
+def near_coil_stage(
+    gathered_ref,
+    row_ref,
+    shift_ref,
+    segment_factor_ref,
+    yoke_factor_ref,
+    target_factor_ref,
+    split_ref,
+    sums_ref,
+    *weight_refs,
+):
+    half = row_ref.shape[1]
+    place_rows(gathered_ref, row_ref)
+    center = jnp.sum(row_ref[0:3, :], axis=1, keepdims=True) * (1.0 / half)
+    shift = jnp.concatenate([center, jnp.zeros((5, 1), jnp.float32)], 0)
+    shift_ref[...] = jnp.broadcast_to(shift, shift_ref.shape)
+    yoke = row_ref[0:8, :] - shift
+    segments = row_ref[8:16, :] - shift
+    row_ref[0:8, :] = yoke
+    row_ref[8:16, :] = segments
+    target_factor_ref[...] = square_factor(yoke)
+    source_factor(segments, coil_core, segment_factor_ref)
+    split_rows(coil_rows(segments), split_ref)
+    targets = target_factor_ref[...]
+    sums_ref[...] = build_and_apply(segment_factor_ref, targets, 3, split_ref, weight_refs)
+    source_factor(yoke, yoke_core, yoke_factor_ref)
+
+
+def far_coil_stage(
+    gathered_ref,
+    near_row_ref,
+    shift_ref,
+    target_factor_ref,
+    sums_ref,
+    row_ref,
+    segment_factor_ref,
+    yoke_factor_ref,
+    split_ref,
+    field_ref,
+    *weight_refs,
+):
+    half = row_ref.shape[1]
+    place_rows(gathered_ref, row_ref)
+    shift = shift_ref[:, 0:1]
+    yoke = row_ref[0:8, :] - shift
+    segments = row_ref[8:16, :] - shift
+    row_ref[0:8, :] = yoke
+    row_ref[8:16, :] = segments
+    source_factor(segments, coil_core, segment_factor_ref)
+    split_rows(coil_rows(segments), split_ref)
+    targets = target_factor_ref[...]
+    sums = build_and_apply(segment_factor_ref, targets, 3, split_ref, weight_refs)
+    places = [near_row_ref[k : k + 1, :] for k in range(3)]
+    field_ref[...] = coil_field(sums_ref[...] + sums, places, 2 * half)
+    source_factor(yoke, yoke_core, yoke_factor_ref)
+
+
+def source_rows(row_ref, field, split_ref):
+    strength = row_ref[3:4, :] * field
+    ux, uy, uz = [strength[k : k + 1] for k in range(3)]
+    qx, qy, qz = [row_ref[k : k + 1, :] for k in range(3)]
+    along = 3.0 * (qx * ux + qy * uy + qz * uz)
+    square = qx * qx + qy * qy + qz * qz
+    split_rows(
+        jnp.concatenate(
+            [
+                strength,
+                qx * strength,
+                qy * strength,
+                qz * strength,
+                qx * along - square * ux,
+                qy * along - square * uy,
+                qz * along - square * uz,
+                jnp.zeros((1, row_ref.shape[1]), jnp.float32),
+            ],
+            0,
+        ),
+        split_ref,
+    )
+
+
+def dipole_field(sums, targets, total):
+    tx, ty, tz = targets
+    plain = [sums[k : k + 1] for k in range(3)]
+    tensor = [[sums[3 + 3 * a + b : 4 + 3 * a + b] for b in range(3)] for a in range(3)]
+    toward = tx * plain[0] + ty * plain[1] + tz * plain[2]
+    trace = tensor[0][0] + tensor[1][1] + tensor[2][2]
+    lead = 3.0 * (toward - trace)
+    reach = tx * tx + ty * ty + tz * tz
+    fields = []
+    for a in range(3):
+        field = targets[a] * lead - reach * plain[a] + sums[12 + a : 13 + a]
+        for b in range(3):
+            field = field + targets[b] * (2.0 * tensor[b][a] - 3.0 * tensor[a][b])
+        fields.append(field)
+    return jnp.concatenate(fields, 0) * (1.0 / math.sqrt(total))
+
+
+def near_build_stage(
+    row_ref, source_ref, target_ref, field_ref, sums_ref, first_ref, second_ref, split_ref
+):
+    source_rows(row_ref, field_ref[...], split_ref)
+    sums_ref[...] = build_and_apply(
+        source_ref, target_ref[...], 5, split_ref, [first_ref, second_ref]
+    )
+
+
+def finish(near_row_ref, coil_ref, sums, out_ref):
+    targets = [near_row_ref[k : k + 1, :] for k in range(3)]
+    total = 2 * near_row_ref.shape[1]
+    out_ref[...] = coil_ref[...] + dipole_field(sums, targets, total)
+
+
+def far_build_stage(
+    near_row_ref,
+    row_ref,
+    source_ref,
+    target_ref,
+    coil_ref,
+    other_ref,
+    sums_ref,
+    out_ref,
+    first_ref,
+    second_ref,
+    split_ref,
+):
+    source_rows(row_ref, other_ref[...], split_ref)
+    sums = build_and_apply(source_ref, target_ref[...], 5, split_ref, [first_ref, second_ref])
+    finish(near_row_ref, coil_ref, sums_ref[...] + sums, out_ref)
+
+
+def near_sweep_stage(row_ref, field_ref, first_ref, second_ref, *refs):
+    segment_refs, (sums_ref, segment_ref, split_ref) = refs[:-3], refs[-3:]
+    source_rows(row_ref, field_ref[...], split_ref)
+    sums_ref[...] = apply(split_ref, [first_ref, second_ref])
+    factor_refs, split_refs = segment_refs[:2], segment_refs[2:]
+    own = row_ref[8:16, : segment_ref.shape[1]]
+    targets = square_factor(own)
+    sums = 0.0
+    for factor_ref, rows_ref in zip(factor_refs, split_refs):
+        parts = power_parts(squares(factor_ref[...], targets), 3)
+        sums = sums + joined(times(rows_ref[...], parts))
+    total = 2 * row_ref.shape[1]
+    segment_ref[...] = coil_field(sums, [own[k : k + 1] for k in range(3)], total)
+
+
+def far_sweep_stage(
+    near_row_ref,
+    row_ref,
+    coil_ref,
+    other_ref,
+    sums_ref,
+    first_ref,
+    second_ref,
+    out_ref,
+    split_ref,
+):
+    source_rows(row_ref, other_ref[...], split_ref)
+    sums = apply(split_ref, [first_ref, second_ref])
+    finish(near_row_ref, coil_ref, sums_ref[...] + sums, out_ref)
+
+
+def near_force_stage(
+    row_ref,
+    near_source_ref,
+    far_source_ref,
+    chi_ref,
+    field_ref,
+    moment_ref,
+    sums_ref,
+    first_ref,
+    second_ref,
+    split_ref,
+):
+    width = chi_ref.shape[1]
+    moment_ref[...] = chi_ref[...] * field_ref[:, :width]
+    source_rows(row_ref, field_ref[...], split_ref)
+    targets = square_factor(row_ref[8:16, :width])
+    parts = power_parts(squares(near_source_ref[...], targets), 5)
+    sums_ref[...] = joined(times(split_ref[...], parts))
+    parts = power_parts(squares(far_source_ref[...], targets), 5)
+    first_ref[...] = parts[0]
+    second_ref[...] = parts[1]
+
+
+def far_force_stage(
+    near_row_ref,
+    row_ref,
+    segment_ref,
+    other_ref,
+    sums_ref,
+    first_ref,
+    second_ref,
+    lorentz_ref,
+    split_ref,
+):
+    width = segment_ref.shape[1]
+    source_rows(row_ref, other_ref[...], split_ref)
+    sums = sums_ref[...] + joined(times(split_ref[...], [first_ref[...], second_ref[...]]))
+    own = near_row_ref[8:16, :width]
+    total = 2 * row_ref.shape[1]
+    field = segment_ref[...] + dipole_field(sums, [own[k : k + 1] for k in range(3)], total)
+    fx, fy, fz = [field[k : k + 1] for k in range(3)]
+    cx, cy, cz = [own[3 + k : 4 + k] for k in range(3)]
+    lorentz_ref[...] = jnp.concatenate(
+        [cy * fz - cz * fy, cz * fx - cx * fz, cx * fy - cy * fx], 0
+    )
+
+
+def call(kernel, outputs, scratch, *operands, limit=VMEM_BYTES, **options):
+    return pl.pallas_call(
+        kernel,
+        out_shape=outputs,
+        scratch_shapes=scratch,
+        compiler_params=pltpu.CompilerParams(vmem_limit_bytes=limit),
+        **options,
+    )(*operands)
+
+
+def close_body(
+    seg_mid, seg_vec, strand_of, strand_current, yoke_pos, quad_weight, panel_of, panel_chi
+):
+    width = yoke_pos.shape[1]
+    blocks = lax.axis_size("seg") * lax.axis_size("yoke")
+    total = blocks * width
+    half = total // 2
+    f32, bf16 = jnp.float32, jnp.bfloat16
+
+    def shape(*dims, kind=f32):
+        return jax.ShapeDtypeStruct(dims, kind)
+
+    def swap(field):
+        return lax.ppermute(field, "yoke", [(0, 1), (1, 0)])
+
+    arrays = [
+        seg_mid,
+        seg_vec,
+        strand_of[None],
+        strand_current[None],
+        yoke_pos,
+        quad_weight[None],
+        panel_of[None],
+        panel_chi[None],
+    ]
+    arrays = [pltpu.with_memory_space_constraint(each, pltpu.HBM) for each in arrays]
+    packed, chi = call(
+        pack_kernel,
+        (shape(1, 1, 10 * width), shape(1, width)),
+        [pltpu.VMEM(each.shape, each.dtype) for each in arrays]
+        + [pltpu.SemaphoreType.DMA((len(arrays),))],
+        *arrays,
+        in_specs=[pl.BlockSpec(memory_space=pltpu.HBM)] * len(arrays),
+    )
+
+    def cross(value, flip):
+        return lax.ppermute(value, "seg", [(k, k ^ flip) for k in range(blocks // 2)])
+
+    pair = call(join_kernel, shape(2, 1, 10 * width), [], packed, cross(packed, 4))
+    near = call(
+        join_kernel,
+        shape(8, 1, 10 * width),
+        [],
+        pair,
+        *[cross(pair, flip) for flip in (1, 2, 3)],
+    )
+    far = swap(near)
+    split_scratch = [pltpu.VMEM((48, half), bf16)]
+    weight_scratch = [pltpu.VMEM((512, half), bf16)] * 2
+    factor = shape(half, 64, kind=bf16)
+    split = shape(48, half, kind=bf16)
+    matrix = shape(half, half, kind=bf16)
+    narrow = shape(half, width, kind=bf16)
+    sums, field, row = shape(16, half), shape(3, half), shape(16, half)
+    near_row, shift, near_segments, near_sources, targets, near_split, near_sums = call(
+        near_coil_stage,
+        (row, shape(8, 128), factor, factor, shape(64, half, kind=bf16), split, sums),
+        weight_scratch,
+        near,
+    )
+    far_row, far_segments, far_sources, far_split, coil = call(
+        far_coil_stage,
+        (row, factor, factor, split, field),
+        weight_scratch,
+        far,
+        near_row,
+        shift,
+        targets,
+        near_sums,
+    )
+    other = swap(coil)
+    near_sums, *near_parts = call(
+        near_build_stage,
+        (sums, matrix, matrix),
+        split_scratch,
+        near_row,
+        near_sources,
+        targets,
+        coil,
+    )
+    own, *far_parts = call(
+        far_build_stage,
+        (field, matrix, matrix),
+        split_scratch,
+        near_row,
+        far_row,
+        far_sources,
+        targets,
+        coil,
+        other,
+        near_sums,
+    )
+    for sweep in range(1, ITERS):
+        other = swap(own)
+        near_sums, segments = call(
+            near_sweep_stage,
+            (sums, shape(3, width)),
+            split_scratch,
+            near_row,
+            own,
+            *near_parts,
+            near_segments,
+            far_segments,
+            near_split,
+            far_split,
+        )
+        own = call(
+            far_sweep_stage,
+            field,
+            split_scratch,
+            near_row,
+            far_row,
+            coil,
+            other,
+            near_sums,
+            *far_parts,
+        )
+    other = swap(own)
+    moment, near_sums, *narrow_parts = call(
+        near_force_stage,
+        (shape(3, width), shape(16, width), narrow, narrow),
+        split_scratch,
+        near_row,
+        near_sources,
+        far_sources,
+        chi,
+        own,
+    )
+    lorentz = call(
+        far_force_stage,
+        shape(3, width),
+        split_scratch,
+        near_row,
+        far_row,
+        segments,
+        other,
+        near_sums,
+        *narrow_parts,
+    )
+    return lorentz, moment
+
+
+def body(*arrays):
+    seg_len, yoke_len = arrays[0].shape[1], arrays[4].shape[1]
+    blocks = lax.axis_size("seg") * lax.axis_size("yoke")
+    close = seg_len == 256 and yoke_len == 128 and lax.axis_size("yoke") == 2 and blocks == 16
+    return (close_body if close else far_body)(*arrays)
+
+
 def solution(mesh):
     placed = (
         P(None, ("grp", "seg")),

time: 174 us -> 26.9 us (0.15)
  blocking collectives: 114 us -> 0 us
  waiting for transfers between devices: 30.5 us -> 5.07 us
  between operations: 14.1 us -> 0.7 us
  Pallas kernels: 0 us -> 12.1 us
  other arithmetic: 10.5 us -> 0 us
  starting transfers between devices: 0.04 us -> 8.78 us
  local copies, waits for them, and re-layouts: 4.09 us -> 0 us
    all_gather x5 -> x0, blocking collectives: 114 us -> none  [the longest x3 56.1 us: moment_field(): lax.all_gather(source_pack, ('seg', 'yoke'), axis=1, tiled=True)]
    unnamed x2 -> x0, waiting for transfers between devices: 30.5 us -> none
    pallas_call x0 -> x11, Pallas kernels: none -> 12.1 us  [call(): pl.pallas_call(kernel, out_shape=outputs, scratch_shapes=scratch, compile...]
    ppermute x0 -> x8, starting transfers between devices: none -> 8.78 us  [the longest x4 7.59 us: cross(): lax.ppermute(value, 'seg', [(k, k ^ flip) for k in range(blocks // 2)])]
    reduce_sum x6 -> x0, other arithmetic: 8.55 us -> none  [the longest x3 6.15 us: dipole_kernel(): jnp.sum(fifth * (3.0 * delta_x * along - radial * sources[3][None, :]), a...]
    ppermute x0 -> x8, waiting for transfers between devices: none -> 5.07 us  [the longest x4 5.06 us: cross(): lax.ppermute(value, 'seg', [(k, k ^ flip) for k in range(blocks // 2)])]
    unnamed x12 -> x0, local copies, waits for them, and re-layouts: 3.92 us -> none
  transfers between devices with their start and end apart: 1 -> 8, of which waited for: 1 -> 4; matrix products, arithmetic and copies ran while one was open for 0% -> 0% of each run, Pallas kernels for 0% -> 22%
where the time goes in v5:
time: 26.9 us; the launch traced here: 26.7 us
  Pallas kernels  12.1 us (45%)
  starting transfers between devices  8.78 us (33%)
  waiting for transfers between devices  5.07 us (19%)
  between operations  0.7 us (3%)
    pallas_call x11, Pallas kernels, call(): pl.pallas_call(kernel, out_shape=outputs, scratch_shapes=scratch, compile...  12.1 us
    ppermute x4, starting transfers between devices, cross(): lax.ppermute(value, 'seg', [(k, k ^ flip) for k in range(blocks // 2)])  7.59 us
    ppermute x4, waiting for transfers between devices, cross(): lax.ppermute(value, 'seg', [(k, k ^ flip) for k in range(blocks // 2)])  5.06 us
    ppermute x4, starting transfers between devices, swap(): return lax.ppermute(field, 'yoke', [(0, 1), (1, 0)])  1.19 us
  transfers between devices with their start and end apart: 8, of which 4 were waited for; matrix products, arithmetic and copies ran while one was open for 0% of the time, Pallas kernels for 22%

profile of v5, /device:TPU:0, one launch (start us, length us, event | category | flops | bytes accessed | tf_op | source)
XLA Modules:
  0.0 26.7 jit_solution(10522955964570954645)
XLA Ops:
  0.6 1.0 %shard_map.95 = (f32[1,1,1280]{2,1,0:T(1,128)S(1)}, f32[1,128]{1,0:T(1,128)S(1)}) custom-call(f32[3,256]{1,0:T(4,128)} %refs_0_.1, f32[3,256]{1,0:T(4,128)} %refs_1_.1, s32[1,256]{1,0:T(1,128)} %bitcast.5, f32[1,256]{1,0:T(1,128)} %bitcast.6, f32[3,128]{1,0:T(4,128)} %refs_4_.1, f32[1,128]{1,0:T(1,128)} %bitcast.7, s32[1,128]{1,0:T(1,128)} %bitcast.8, ...), custom_call_target="tpu_custom_call" | custom-call | tf_op jit(solution)/shard_map/pallas_call | solution.py:541
  1.6 4.1 %collective-permute-start = (f32[1,1,1280]{2,1,0:T(1,128)S(1)}, f32[1,1,1280]{2,1,0:T(1,128)S(1)}, u32[]{:S(2)}, u32[]{:S(2)}) collective-permute-start(f32[1,1,1280]{2,1,0:T(1,128)S(1)} %get-tuple-element.28.refs_0_), channel_id=1, source_target_pairs={{0,8},{2,10},{4,12},{6,14},{8,0},{10,2},{12,4},{14,6},{1,9},{3,11}... | collective-permute-start | bytes 15368 | tf_op jit(solution)/shard_map/ppermute | solution.py:586
  5.7 1.6 %collective-permute-done.refs_1_ = f32[1,1,1280]{2,1,0:T(1,128)S(1)} collective-permute-done((f32[1,1,1280]{2,1,0:T(1,128)S(1)}, f32[1,1,1280]{2,1,0:T(1,128)S(1)}, u32[]{:S(2)}, u32[]{:S(2)}) %collective-permute-start) | collective-permute-done | bytes 5152 | tf_op jit(solution)/shard_map/ppermute | solution.py:586
  7.3 2.8 %collective-permute-start.3 = (f32[2,1,1280]{2,1,0:T(1,128)S(1)}, f32[2,1,1280]{2,1,0:T(1,128)S(1)}, u32[]{:S(2)}, u32[]{:S(2)}) collective-permute-start(f32[2,1,1280]{2,1,0:T(1,128)S(1)} %shard_map.96.refs_0_), channel_id=1, source_target_pairs={{0,6},{2,4},{4,2},{6,0},{8,14},{10,12},{12,10},{14,8},{1,7},{3,5},... | collective-permute-start | bytes 30728 | tf_op jit(solution)/shard_map/ppermute | solution.py:586
  10.2 0.4 %collective-permute-start.2 = (f32[2,1,1280]{2,1,0:T(1,128)S(1)}, f32[2,1,1280]{2,1,0:T(1,128)S(1)}, u32[]{:S(2)}, u32[]{:S(2)}) collective-permute-start(f32[2,1,1280]{2,1,0:T(1,128)S(1)} %shard_map.96.refs_0_), channel_id=1, source_target_pairs={{0,4},{2,6},{4,0},{6,2},{8,12},{10,14},{12,8},{14,10},{1,5},{3,7},... | collective-permute-start | bytes 30728 | tf_op jit(solution)/shard_map/ppermute | solution.py:586
  10.6 0.2 collective-permute-start.1
  10.8 1.1 %collective-permute-done.3.refs_3_ = f32[2,1,1280]{2,1,0:T(1,128)S(1)} collective-permute-done((f32[2,1,1280]{2,1,0:T(1,128)S(1)}, f32[2,1,1280]{2,1,0:T(1,128)S(1)}, u32[]{:S(2)}, u32[]{:S(2)}) %collective-permute-start.3) | collective-permute-done | bytes 10272 | tf_op jit(solution)/shard_map/ppermute | solution.py:586
  11.9 1.9 %collective-permute-done.2.refs_2_ = f32[2,1,1280]{2,1,0:T(1,128)S(1)} collective-permute-done((f32[2,1,1280]{2,1,0:T(1,128)S(1)}, f32[2,1,1280]{2,1,0:T(1,128)S(1)}, u32[]{:S(2)}, u32[]{:S(2)}) %collective-permute-start.2) | collective-permute-done | bytes 10272 | tf_op jit(solution)/shard_map/ppermute | solution.py:586
  13.8 0.4 %collective-permute-done.1.refs_1_ = f32[2,1,1280]{2,1,0:T(1,128)S(1)} collective-permute-done((f32[2,1,1280]{2,1,0:T(1,128)S(1)}, f32[2,1,1280]{2,1,0:T(1,128)S(1)}, u32[]{:S(2)}, u32[]{:S(2)}) %collective-permute-start.1) | collective-permute-done | bytes 10272 | tf_op jit(solution)/shard_map/ppermute | solution.py:586
  14.3 0.0 collective-permute-start.4
  14.3 1.7 %shard_map.98 = (f32[16,1024]{1,0:T(8,128)S(1)}, f32[8,128]{1,0:T(8,128)S(1)}, bf16[1024,64]{1,0:T(8,128)(2,1)S(1)}, bf16[1024,64]{1,0:T(8,128)(2,1)S(1)}, bf16[...) custom-call(f32[8,1,1280]{2,1,0:T(1,128)S(1)} %shard_map.97.gathered_ref), custom_call_target="tpu_custom_call" | custom-call | tf_op jit(solution)/shard_map/pallas_call | solution.py:541
  16.0 0.0 collective-permute-done.4.gathered_ref
  16.0 1.7 %shard_map.99 = (f32[16,1024]{1,0:T(8,128)S(1)}, bf16[1024,64]{1,0:T(8,128)(2,1)S(1)}, bf16[1024,64]{1,0:T(8,128)(2,1)S(1)}, bf16[48,1024]{1,0:T(8,128)(2,1)S(1)}, f32[3,1024]{1,0:T(4,128)S(1)}) custom-call(f32[8,1,1280]{2,1,0:T(1,128)S(1)} %collective-permute-done.4.gathered_ref, f32[16,1024]{1,0:T(8,128)S(1)} %get-tuple-element.29.near_row_ref.row_ref, ...), custom_call_target="tpu_custom_call" | custom-call | tf_op jit(solution)/shard_map/pallas_call | solution.py:541
  17.6 0.6 %collective-permute-start.5 = (f32[3,1024]{1,0:T(4,128)S(1)}, f32[3,1024]{1,0:T(4,128)S(1)}, u32[]{:S(2)}, u32[]{:S(2)}) collective-permute-start(f32[3,1024]{1,0:T(4,128)S(1)} %get-tuple-element.35.field_ref.coil_ref), channel_id=1, source_target_pairs={{0,1},{1,0},{2,3},{3,2},{4,5},{5,4},{6,7},{7,6},{8,9},{9,8},{10,11... | collective-permute-start | bytes 36872 | tf_op jit(solution)/shard_map/ppermute | solution.py:563
  18.2 1.9 %shard_map.100 = (f32[16,1024]{1,0:T(8,128)S(1)}, bf16[1024,1024]{1,0:T(8,128)(2,1)S(1)}, bf16[1024,1024]{1,0:T(8,128)(2,1)S(1)}) custom-call(f32[16,1024]{1,0:T(8,128)S(1)} %get-tuple-element.29.near_row_ref.row_ref, bf16[1024,64]{1,0:T(8,128)(2,1)S(1)} %get-tuple-element.36.source_ref.near_source_ref, ...), custom_call_target="tpu_custom_call" | custom-call | tf_op jit(solution)/shard_map/pallas_call | solution.py:541
  20.1 0.0 collective-permute-done.5.other_ref
  20.1 2.0 %shard_map.101 = (f32[3,1024]{1,0:T(4,128)S(1)}, bf16[1024,1024]{1,0:T(8,128)(2,1)S(1)}, bf16[1024,1024]{1,0:T(8,128)(2,1)S(1)}) custom-call(f32[16,1024]{1,0:T(8,128)S(1)} %get-tuple-element.29.near_row_ref.row_ref, f32[16,1024]{1,0:T(8,128)S(1)} %get-tuple-element.33.row_ref, bf16[1024,64]{1,0:T(8,128)(2,1)S(1)} %get-tuple-element.34.source_ref.far_source_ref, ...), custom_call_target="tpu_custom_call" | custom-call | tf_op jit(solution)/shard_map/pallas_call | solution.py:541
  22.1 0.1 collective-permute-start.6
  22.2 1.3 %shard_map.102 = (f32[16,1024]{1,0:T(8,128)S(1)}, f32[3,128]{1,0:T(4,128)S(1)}) custom-call(f32[16,1024]{1,0:T(8,128)S(1)} %get-tuple-element.29.near_row_ref.row_ref, f32[3,1024]{1,0:T(4,128)S(1)} %get-tuple-element.38.field_ref, bf16[1024,1024]{1,0:T(8,128)(2,1)S(1)} %get-tuple-element.39.first_ref, bf16[1024,1024]{1,0:T(8,128)(2,1)S(1)} %get-tuple-element.40.second_ref, ...), custom_call_target="tpu_custom_call" | custom-call | tf_op jit(solution)/shard_map/pallas_call | solution.py:541
  23.4 0.0 collective-permute-done.6.other_ref
  23.4 0.8 %shard_map.103.field_ref = f32[3,1024]{1,0:T(4,128)S(1)} custom-call(f32[16,1024]{1,0:T(8,128)S(1)} %get-tuple-element.29.near_row_ref.row_ref, f32[16,1024]{1,0:T(8,128)S(1)} %get-tuple-element.33.row_ref, f32[3,1024]{1,0:T(4,128)S(1)} %get-tuple-element.35.field_ref.coil_ref, f32[3,1024]{1,0:T(4,128)S(1)} %collective-permute-done.6.other_ref, ...), custom_call_target="tpu_custom_call" | custom-call | tf_op jit(solution)/shard_map/pallas_call | solution.py:541
  24.3 0.5 %collective-permute-start.7 = (f32[3,1024]{1,0:T(4,128)S(1)}, f32[3,1024]{1,0:T(4,128)S(1)}, u32[]{:S(2)}, u32[]{:S(2)}) collective-permute-start(f32[3,1024]{1,0:T(4,128)S(1)} %shard_map.103.field_ref), channel_id=1, source_target_pairs={{0,1},{1,0},{2,3},{3,2},{4,5},{5,4},{6,7},{7,6},{8,9},{9,8},{10,11... | collective-permute-start | bytes 36872 | tf_op jit(solution)/shard_map/ppermute | solution.py:563
  24.8 1.0 %shard_map.104 = (f32[3,128]{1,0:T(4,128)}, f32[16,128]{1,0:T(8,128)S(1)}, bf16[1024,128]{1,0:T(8,128)(2,1)S(1)}, bf16[1024,128]{1,0:T(8,128)(2,1)S(1)}) custom-call(f32[16,1024]{1,0:T(8,128)S(1)} %get-tuple-element.29.near_row_ref.row_ref, bf16[1024,64]{1,0:T(8,128)(2,1)S(1)} %get-tuple-element.36.source_ref.near_source_ref, ...), custom_call_target="tpu_custom_call" | custom-call | tf_op jit(solution)/shard_map/pallas_call | solution.py:541
  25.8 0.0 collective-permute-done.7.other_ref
  25.8 0.8 %shard_map.105 = f32[3,128]{1,0:T(4,128)} custom-call(f32[16,1024]{1,0:T(8,128)S(1)} %get-tuple-element.29.near_row_ref.row_ref, f32[16,1024]{1,0:T(8,128)S(1)} %get-tuple-element.33.row_ref, f32[3,128]{1,0:T(4,128)S(1)} %get-tuple-element.45.segment_ref, f32[3,1024]{1,0:T(4,128)S(1)} %collective-permute-done.7.other_ref, ...), custom_call_target="tpu_custom_call" | custom-call | tf_op jit(solution)/shard_map/pallas_call | solution.py:541
  (2 shorter events, 0.0 us)
Async XLA Ops:
  1.6 5.7 %collective-permute-start = (f32[1,1,1280]{2,1,0:T(1,128)S(1)}, f32[1,1,1280]{2,1,0:T(1,128)S(1)}, u32[]{:S(2)}, u32[]{:S(2)}) collective-permute-start(f32[1,1,1280]{2,1,0:T(1,128)S(1)} %get-tuple-element.28.refs_0_), channel_id=1, source_target_pairs={{0,8},{2,10},{4,12},{6,14},{8,0},{10,2},{12,4},{14,6},{1,9},{3,11}... | collective-permute-start | bytes 15368 | tf_op jit(solution)/shard_map/ppermute | solution.py:586
  7.3 4.6 %collective-permute-start.3 = (f32[2,1,1280]{2,1,0:T(1,128)S(1)}, f32[2,1,1280]{2,1,0:T(1,128)S(1)}, u32[]{:S(2)}, u32[]{:S(2)}) collective-permute-start(f32[2,1,1280]{2,1,0:T(1,128)S(1)} %shard_map.96.refs_0_), channel_id=1, source_target_pairs={{0,6},{2,4},{4,2},{6,0},{8,14},{10,12},{12,10},{14,8},{1,7},{3,5},... | collective-permute-start | bytes 30728 | tf_op jit(solution)/shard_map/ppermute | solution.py:586
  10.2 3.7 %collective-permute-start.2 = (f32[2,1,1280]{2,1,0:T(1,128)S(1)}, f32[2,1,1280]{2,1,0:T(1,128)S(1)}, u32[]{:S(2)}, u32[]{:S(2)}) collective-permute-start(f32[2,1,1280]{2,1,0:T(1,128)S(1)} %shard_map.96.refs_0_), channel_id=1, source_target_pairs={{0,4},{2,6},{4,0},{6,2},{8,12},{10,14},{12,8},{14,10},{1,5},{3,7},... | collective-permute-start | bytes 30728 | tf_op jit(solution)/shard_map/ppermute | solution.py:586
  10.6 3.7 %collective-permute-start.1 = (f32[2,1,1280]{2,1,0:T(1,128)S(1)}, f32[2,1,1280]{2,1,0:T(1,128)S(1)}, u32[]{:S(2)}, u32[]{:S(2)}) collective-permute-start(f32[2,1,1280]{2,1,0:T(1,128)S(1)} %shard_map.96.refs_0_), channel_id=1, source_target_pairs={{0,2},{2,0},{4,6},{6,4},{8,10},{10,8},{12,14},{14,12},{1,3},{3,1},... | collective-permute-start | bytes 30728 | tf_op jit(solution)/shard_map/ppermute | solution.py:586
  14.3 1.7 %collective-permute-start.4 = (f32[8,1,1280]{2,1,0:T(1,128)S(1)}, f32[8,1,1280]{2,1,0:T(1,128)S(1)}, u32[]{:S(2)}, u32[]{:S(2)}) collective-permute-start(f32[8,1,1280]{2,1,0:T(1,128)S(1)} %shard_map.97.gathered_ref), channel_id=1, source_target_pairs={{0,1},{1,0},{2,3},{3,2},{4,5},{5,4},{6,7},{7,6},{8,9},{9,8},{10,11... | collective-permute-start | bytes 122888 | tf_op jit(solution)/shard_map/ppermute | solution.py:563
  17.6 2.4 %collective-permute-start.5 = (f32[3,1024]{1,0:T(4,128)S(1)}, f32[3,1024]{1,0:T(4,128)S(1)}, u32[]{:S(2)}, u32[]{:S(2)}) collective-permute-start(f32[3,1024]{1,0:T(4,128)S(1)} %get-tuple-element.35.field_ref.coil_ref), channel_id=1, source_target_pairs={{0,1},{1,0},{2,3},{3,2},{4,5},{5,4},{6,7},{7,6},{8,9},{9,8},{10,11... | collective-permute-start | bytes 36872 | tf_op jit(solution)/shard_map/ppermute | solution.py:563
  22.1 1.4 %collective-permute-start.6 = (f32[3,1024]{1,0:T(4,128)S(1)}, f32[3,1024]{1,0:T(4,128)S(1)}, u32[]{:S(2)}, u32[]{:S(2)}) collective-permute-start(f32[3,1024]{1,0:T(4,128)S(1)} %get-tuple-element.38.field_ref), channel_id=1, source_target_pairs={{0,1},{1,0},{2,3},{3,2},{4,5},{5,4},{6,7},{7,6},{8,9},{9,8},{10,11... | collective-permute-start | bytes 36872 | tf_op jit(solution)/shard_map/ppermute | solution.py:563
  24.3 1.6 %collective-permute-start.7 = (f32[3,1024]{1,0:T(4,128)S(1)}, f32[3,1024]{1,0:T(4,128)S(1)}, u32[]{:S(2)}, u32[]{:S(2)}) collective-permute-start(f32[3,1024]{1,0:T(4,128)S(1)} %shard_map.103.field_ref), channel_id=1, source_target_pairs={{0,1},{1,0},{2,3},{3,2},{4,5},{5,4},{6,7},{7,6},{8,9},{9,8},{10,11... | collective-permute-start | bytes 36872 | tf_op jit(solution)/shard_map/ppermute | solution.py:563

commit v6 on v5

--- a/solution.py
+++ b/solution.py
@@ -295,28 +295,21 @@
             ]
 
 
-def build_and_apply(factor_ref, targets, power, split_ref, part_refs):
-    depth = 256
-    count = factor_ref.shape[0] // depth
-    slots = part_refs[0].shape[0] // depth
-    product = jnp.zeros((split_ref.shape[0], targets.shape[1]), jnp.float32)
-
-    def slot(chunk):
-        start = chunk % slots * depth
-        return slice(start, start + depth)
-
-    def build(chunk):
-        sources = factor_ref[chunk * depth : (chunk + 1) * depth, :]
-        for ref, part in zip(part_refs, power_parts(squares(sources, targets), power)):
-            ref[slot(chunk), :] = part
-
-    build(0)
-    for chunk in range(count):
-        if chunk + 1 < count:
-            build(chunk + 1)
-        rows = split_ref[:, chunk * depth : (chunk + 1) * depth]
-        product = product + times(rows, [ref[slot(chunk), :] for ref in part_refs])
-    return joined(product)
+def build_and_apply(factor_ref, targets, power, split_ref, part_refs=()):
+    depth, across = 256, 256
+    products = []
+    for left in range(0, targets.shape[1], across):
+        lanes = slice(left, left + across)
+        product = None
+        for start in range(0, factor_ref.shape[0], depth):
+            at = slice(start, start + depth)
+            parts = power_parts(squares(factor_ref[at, :], targets[:, lanes]), power)
+            for ref, part in zip(part_refs, parts):
+                ref[at, lanes] = part
+            fresh = times(split_ref[:, at], parts)
+            product = fresh if product is None else product + fresh
+        products.append(joined(product))
+    return jnp.concatenate(products, 1)
 
 
 def apply(split_ref, part_refs):
@@ -337,7 +330,6 @@
     target_factor_ref,
     split_ref,
     sums_ref,
-    *weight_refs,
 ):
     half = row_ref.shape[1]
     place_rows(gathered_ref, row_ref)
@@ -352,7 +344,7 @@
     source_factor(segments, coil_core, segment_factor_ref)
     split_rows(coil_rows(segments), split_ref)
     targets = target_factor_ref[...]
-    sums_ref[...] = build_and_apply(segment_factor_ref, targets, 3, split_ref, weight_refs)
+    sums_ref[...] = build_and_apply(segment_factor_ref, targets, 3, split_ref)
     source_factor(yoke, yoke_core, yoke_factor_ref)
 
 
@@ -367,7 +359,6 @@
     yoke_factor_ref,
     split_ref,
     field_ref,
-    *weight_refs,
 ):
     half = row_ref.shape[1]
     place_rows(gathered_ref, row_ref)
@@ -379,7 +370,7 @@
     source_factor(segments, coil_core, segment_factor_ref)
     split_rows(coil_rows(segments), split_ref)
     targets = target_factor_ref[...]
-    sums = build_and_apply(segment_factor_ref, targets, 3, split_ref, weight_refs)
+    sums = build_and_apply(segment_factor_ref, targets, 3, split_ref)
     places = [near_row_ref[k : k + 1, :] for k in range(3)]
     field_ref[...] = coil_field(sums_ref[...] + sums, places, 2 * half)
     source_factor(yoke, yoke_core, yoke_factor_ref)
@@ -477,14 +468,21 @@
 def far_sweep_stage(
     near_row_ref,
     row_ref,
+    source_ref,
     coil_ref,
     other_ref,
     sums_ref,
     first_ref,
     second_ref,
     out_ref,
+    narrow_first_ref,
+    narrow_second_ref,
     split_ref,
 ):
+    targets = square_factor(near_row_ref[8:16, : narrow_first_ref.shape[1]])
+    parts = power_parts(squares(source_ref[...], targets), 5)
+    narrow_first_ref[...] = parts[0]
+    narrow_second_ref[...] = parts[1]
     source_rows(row_ref, other_ref[...], split_ref)
     sums = apply(split_ref, [first_ref, second_ref])
     finish(near_row_ref, coil_ref, sums_ref[...] + sums, out_ref)
@@ -492,39 +490,33 @@
 
 def near_force_stage(
     row_ref,
-    near_source_ref,
-    far_source_ref,
-    chi_ref,
+    source_ref,
     field_ref,
-    moment_ref,
     sums_ref,
-    first_ref,
-    second_ref,
     split_ref,
 ):
-    width = chi_ref.shape[1]
-    moment_ref[...] = chi_ref[...] * field_ref[:, :width]
     source_rows(row_ref, field_ref[...], split_ref)
-    targets = square_factor(row_ref[8:16, :width])
-    parts = power_parts(squares(near_source_ref[...], targets), 5)
+    targets = square_factor(row_ref[8:16, : sums_ref.shape[1]])
+    parts = power_parts(squares(source_ref[...], targets), 5)
     sums_ref[...] = joined(times(split_ref[...], parts))
-    parts = power_parts(squares(far_source_ref[...], targets), 5)
-    first_ref[...] = parts[0]
-    second_ref[...] = parts[1]
 
 
 def far_force_stage(
     near_row_ref,
     row_ref,
     segment_ref,
+    chi_ref,
+    field_ref,
     other_ref,
     sums_ref,
     first_ref,
     second_ref,
     lorentz_ref,
+    moment_ref,
     split_ref,
 ):
     width = segment_ref.shape[1]
+    moment_ref[...] = chi_ref[...] * field_ref[:, :width]
     source_rows(row_ref, other_ref[...], split_ref)
     sums = sums_ref[...] + joined(times(split_ref[...], [first_ref[...], second_ref[...]]))
     own = near_row_ref[8:16, :width]
@@ -595,7 +587,6 @@
     )
     far = swap(near)
     split_scratch = [pltpu.VMEM((48, half), bf16)]
-    weight_scratch = [pltpu.VMEM((512, half), bf16)] * 2
     factor = shape(half, 64, kind=bf16)
     split = shape(48, half, kind=bf16)
     matrix = shape(half, half, kind=bf16)
@@ -604,13 +595,13 @@
     near_row, shift, near_segments, near_sources, targets, near_split, near_sums = call(
         near_coil_stage,
         (row, shape(8, 128), factor, factor, shape(64, half, kind=bf16), split, sums),
-        weight_scratch,
+        [],
         near,
     )
     far_row, far_segments, far_sources, far_split, coil = call(
         far_coil_stage,
         (row, factor, factor, split, field),
-        weight_scratch,
+        [],
         far,
         near_row,
         shift,
@@ -653,35 +644,36 @@
             near_split,
             far_split,
         )
-        own = call(
+        own, *narrow_parts = call(
             far_sweep_stage,
-            field,
+            (field, narrow, narrow),
             split_scratch,
             near_row,
             far_row,
+            far_sources,
             coil,
             other,
             near_sums,
             *far_parts,
         )
     other = swap(own)
-    moment, near_sums, *narrow_parts = call(
+    near_sums = call(
         near_force_stage,
-        (shape(3, width), shape(16, width), narrow, narrow),
+        shape(16, width),
         split_scratch,
         near_row,
         near_sources,
-        far_sources,
-        chi,
         own,
     )
-    lorentz = call(
+    lorentz, moment = call(
         far_force_stage,
-        shape(3, width),
+        (shape(3, width), shape(3, width)),
         split_scratch,
         near_row,
         far_row,
         segments,
+        chi,
+        own,
         other,
         near_sums,
         *narrow_parts,

time: 26.9 us -> 25.9 us (0.963)
  Pallas kernels: 12.1 us -> 10.8 us
  waiting for transfers between devices: 5.07 us -> 5.43 us
    pallas_call x11, Pallas kernels: 12.1 us -> 10.8 us  [call(): pl.pallas_call(kernel, out_shape=outputs, scratch_shapes=scratch, compile...]
    ppermute x4, waiting for transfers between devices: 0.01 us -> 0.36 us  [swap(): return lax.ppermute(field, 'yoke', [(0, 1), (1, 0)])]
  transfers between devices with their start and end apart: 8 -> 8, of which waited for: 4 -> 5; matrix products, arithmetic and copies ran while one was open for 0% -> 0% of each run, Pallas kernels for 22% -> 19%
where the time goes in v6:
time: 25.9 us; the launch traced here: 25.7 us
  Pallas kernels  10.8 us (42%)
  starting transfers between devices  8.81 us (34%)
  waiting for transfers between devices  5.43 us (21%)
  between operations  0.7 us (3%)
    pallas_call x11, Pallas kernels, call(): pl.pallas_call(kernel, out_shape=outputs, scratch_shapes=scratch, compile...  10.8 us
    ppermute x4, starting transfers between devices, cross(): lax.ppermute(value, 'seg', [(k, k ^ flip) for k in range(blocks // 2)])  7.59 us
    ppermute x4, waiting for transfers between devices, cross(): lax.ppermute(value, 'seg', [(k, k ^ flip) for k in range(blocks // 2)])  5.06 us
    ppermute x4, starting transfers between devices, swap(): return lax.ppermute(field, 'yoke', [(0, 1), (1, 0)])  1.22 us
  transfers between devices with their start and end apart: 8, of which 5 were waited for; matrix products, arithmetic and copies ran while one was open for 0% of the time, Pallas kernels for 19%

profile of v6, /device:TPU:0, one launch (start us, length us, event | category | flops | bytes accessed | tf_op | source)
XLA Modules:
  0.0 25.7 jit_solution(3159956629492558190)
XLA Ops:
  0.6 1.0 %shard_map.95 = (f32[1,1,1280]{2,1,0:T(1,128)S(1)}, f32[1,128]{1,0:T(1,128)S(1)}) custom-call(f32[3,256]{1,0:T(4,128)} %refs_0_.1, f32[3,256]{1,0:T(4,128)} %refs_1_.1, s32[1,256]{1,0:T(1,128)} %bitcast.5, f32[1,256]{1,0:T(1,128)} %bitcast.6, f32[3,128]{1,0:T(4,128)} %refs_4_.1, f32[1,128]{1,0:T(1,128)} %bitcast.7, s32[1,128]{1,0:T(1,128)} %bitcast.8, ...), custom_call_target="tpu_custom_call" | custom-call | tf_op jit(solution)/shard_map/pallas_call | solution.py:533
  1.6 4.1 %collective-permute-start = (f32[1,1,1280]{2,1,0:T(1,128)S(1)}, f32[1,1,1280]{2,1,0:T(1,128)S(1)}, u32[]{:S(2)}, u32[]{:S(2)}) collective-permute-start(f32[1,1,1280]{2,1,0:T(1,128)S(1)} %get-tuple-element.27.refs_0_), channel_id=1, source_target_pairs={{0,8},{2,10},{4,12},{6,14},{8,0},{10,2},{12,4},{14,6},{1,9},{3,11}... | collective-permute-start | bytes 15368 | tf_op jit(solution)/shard_map/ppermute | solution.py:578
  5.7 1.6 %collective-permute-done.refs_1_ = f32[1,1,1280]{2,1,0:T(1,128)S(1)} collective-permute-done((f32[1,1,1280]{2,1,0:T(1,128)S(1)}, f32[1,1,1280]{2,1,0:T(1,128)S(1)}, u32[]{:S(2)}, u32[]{:S(2)}) %collective-permute-start) | collective-permute-done | bytes 5152 | tf_op jit(solution)/shard_map/ppermute | solution.py:578
  7.3 2.8 %collective-permute-start.3 = (f32[2,1,1280]{2,1,0:T(1,128)S(1)}, f32[2,1,1280]{2,1,0:T(1,128)S(1)}, u32[]{:S(2)}, u32[]{:S(2)}) collective-permute-start(f32[2,1,1280]{2,1,0:T(1,128)S(1)} %shard_map.96.refs_0_), channel_id=1, source_target_pairs={{0,6},{2,4},{4,2},{6,0},{8,14},{10,12},{12,10},{14,8},{1,7},{3,5},... | collective-permute-start | bytes 30728 | tf_op jit(solution)/shard_map/ppermute | solution.py:578
  10.2 0.4 %collective-permute-start.2 = (f32[2,1,1280]{2,1,0:T(1,128)S(1)}, f32[2,1,1280]{2,1,0:T(1,128)S(1)}, u32[]{:S(2)}, u32[]{:S(2)}) collective-permute-start(f32[2,1,1280]{2,1,0:T(1,128)S(1)} %shard_map.96.refs_0_), channel_id=1, source_target_pairs={{0,4},{2,6},{4,0},{6,2},{8,12},{10,14},{12,8},{14,10},{1,5},{3,7},... | collective-permute-start | bytes 30728 | tf_op jit(solution)/shard_map/ppermute | solution.py:578
  10.6 0.2 collective-permute-start.1
  10.8 1.1 %collective-permute-done.3.refs_3_ = f32[2,1,1280]{2,1,0:T(1,128)S(1)} collective-permute-done((f32[2,1,1280]{2,1,0:T(1,128)S(1)}, f32[2,1,1280]{2,1,0:T(1,128)S(1)}, u32[]{:S(2)}, u32[]{:S(2)}) %collective-permute-start.3) | collective-permute-done | bytes 10272 | tf_op jit(solution)/shard_map/ppermute | solution.py:578
  11.9 1.9 %collective-permute-done.2.refs_2_ = f32[2,1,1280]{2,1,0:T(1,128)S(1)} collective-permute-done((f32[2,1,1280]{2,1,0:T(1,128)S(1)}, f32[2,1,1280]{2,1,0:T(1,128)S(1)}, u32[]{:S(2)}, u32[]{:S(2)}) %collective-permute-start.2) | collective-permute-done | bytes 10272 | tf_op jit(solution)/shard_map/ppermute | solution.py:578
  13.8 0.4 %collective-permute-done.1.refs_1_ = f32[2,1,1280]{2,1,0:T(1,128)S(1)} collective-permute-done((f32[2,1,1280]{2,1,0:T(1,128)S(1)}, f32[2,1,1280]{2,1,0:T(1,128)S(1)}, u32[]{:S(2)}, u32[]{:S(2)}) %collective-permute-start.1) | collective-permute-done | bytes 10272 | tf_op jit(solution)/shard_map/ppermute | solution.py:578
  14.3 0.0 collective-permute-start.4
  14.3 1.7 %shard_map.98 = (f32[16,1024]{1,0:T(8,128)S(1)}, f32[8,128]{1,0:T(8,128)S(1)}, bf16[1024,64]{1,0:T(8,128)(2,1)S(1)}, bf16[1024,64]{1,0:T(8,128)(2,1)S(1)}, bf16[...) custom-call(f32[8,1,1280]{2,1,0:T(1,128)S(1)} %shard_map.97.gathered_ref), custom_call_target="tpu_custom_call" | custom-call | tf_op jit(solution)/shard_map/pallas_call | solution.py:533
  16.0 0.0 collective-permute-done.4.gathered_ref
  16.0 1.7 %shard_map.99 = (f32[16,1024]{1,0:T(8,128)S(1)}, bf16[1024,64]{1,0:T(8,128)(2,1)S(1)}, bf16[1024,64]{1,0:T(8,128)(2,1)S(1)}, bf16[48,1024]{1,0:T(8,128)(2,1)S(1)}, f32[3,1024]{1,0:T(4,128)S(1)}) custom-call(f32[8,1,1280]{2,1,0:T(1,128)S(1)} %collective-permute-done.4.gathered_ref, f32[16,1024]{1,0:T(8,128)S(1)} %get-tuple-element.28.near_row_ref.row_ref, ...), custom_call_target="tpu_custom_call" | custom-call | tf_op jit(solution)/shard_map/pallas_call | solution.py:533
  17.6 0.6 %collective-permute-start.5 = (f32[3,1024]{1,0:T(4,128)S(1)}, f32[3,1024]{1,0:T(4,128)S(1)}, u32[]{:S(2)}, u32[]{:S(2)}) collective-permute-start(f32[3,1024]{1,0:T(4,128)S(1)} %get-tuple-element.34.field_ref.coil_ref), channel_id=1, source_target_pairs={{0,1},{1,0},{2,3},{3,2},{4,5},{5,4},{6,7},{7,6},{8,9},{9,8},{10,11... | collective-permute-start | bytes 36872 | tf_op jit(solution)/shard_map/ppermute | solution.py:555
  18.2 1.5 %shard_map.100 = (f32[16,1024]{1,0:T(8,128)S(1)}, bf16[1024,1024]{1,0:T(8,128)(2,1)S(1)}, bf16[1024,1024]{1,0:T(8,128)(2,1)S(1)}) custom-call(f32[16,1024]{1,0:T(8,128)S(1)} %get-tuple-element.28.near_row_ref.row_ref, bf16[1024,64]{1,0:T(8,128)(2,1)S(1)} %get-tuple-element.35.source_ref, bf16[64,1024]{1,0:T(8,128)(2,1)S(1)} %get-tuple-element.30.target_factor_ref.target_ref, ...), custom_call_target="tpu_custom_call" | custom-call | tf_op jit(solution)/shard_map/pallas_call | solution.py:533
  19.7 0.0 collective-permute-done.5.other_ref
  19.7 1.6 %shard_map.101 = (f32[3,1024]{1,0:T(4,128)S(1)}, bf16[1024,1024]{1,0:T(8,128)(2,1)S(1)}, bf16[1024,1024]{1,0:T(8,128)(2,1)S(1)}) custom-call(f32[16,1024]{1,0:T(8,128)S(1)} %get-tuple-element.28.near_row_ref.row_ref, f32[16,1024]{1,0:T(8,128)S(1)} %get-tuple-element.32.row_ref, bf16[1024,64]{1,0:T(8,128)(2,1)S(1)} %get-tuple-element.33.source_ref, ...), custom_call_target="tpu_custom_call" | custom-call | tf_op jit(solution)/shard_map/pallas_call | solution.py:533
  21.3 0.1 collective-permute-start.6
  21.4 1.3 %shard_map.102 = (f32[16,1024]{1,0:T(8,128)S(1)}, f32[3,128]{1,0:T(4,128)S(1)}) custom-call(f32[16,1024]{1,0:T(8,128)S(1)} %get-tuple-element.28.near_row_ref.row_ref, f32[3,1024]{1,0:T(4,128)S(1)} %get-tuple-element.37.field_ref, bf16[1024,1024]{1,0:T(8,128)(2,1)S(1)} %get-tuple-element.38.first_ref, bf16[1024,1024]{1,0:T(8,128)(2,1)S(1)} %get-tuple-element.39.second_ref, ...), custom_call_target="tpu_custom_call" | custom-call | tf_op jit(solution)/shard_map/pallas_call | solution.py:533
  22.7 0.0 collective-permute-done.6.other_ref
  22.7 0.8 %shard_map.103 = (f32[3,1024]{1,0:T(4,128)S(1)}, bf16[1024,128]{1,0:T(8,128)(2,1)S(1)}, bf16[1024,128]{1,0:T(8,128)(2,1)S(1)}) custom-call(f32[16,1024]{1,0:T(8,128)S(1)} %get-tuple-element.28.near_row_ref.row_ref, f32[16,1024]{1,0:T(8,128)S(1)} %get-tuple-element.32.row_ref, bf16[1024,64]{1,0:T(8,128)(2,1)S(1)} %get-tuple-element.33.source_ref, ...), custom_call_target="tpu_custom_call" | custom-call | tf_op jit(solution)/shard_map/pallas_call | solution.py:533
  23.5 0.6 %collective-permute-start.7 = (f32[3,1024]{1,0:T(4,128)S(1)}, f32[3,1024]{1,0:T(4,128)S(1)}, u32[]{:S(2)}, u32[]{:S(2)}) collective-permute-start(f32[3,1024]{1,0:T(4,128)S(1)} %get-tuple-element.49.field_ref), channel_id=1, source_target_pairs={{0,1},{1,0},{2,3},{3,2},{4,5},{5,4},{6,7},{7,6},{8,9},{9,8},{10,11... | collective-permute-start | bytes 36872 | tf_op jit(solution)/shard_map/ppermute | solution.py:555
  24.1 0.5 %shard_map.104.sums_ref = f32[16,128]{1,0:T(8,128)S(1)} custom-call(f32[16,1024]{1,0:T(8,128)S(1)} %get-tuple-element.28.near_row_ref.row_ref, bf16[1024,64]{1,0:T(8,128)(2,1)S(1)} %get-tuple-element.35.source_ref, f32[3,1024]{1,0:T(4,128)S(1)} %get-tuple-element.49.field_ref), custom_call_target="tpu_custom_call" | custom-call | tf_op jit(solution)/shard_map/pallas_call | solution.py:533
  24.5 0.4 %collective-permute-done.7.other_ref = f32[3,1024]{1,0:T(4,128)S(1)} collective-permute-done((f32[3,1024]{1,0:T(4,128)S(1)}, f32[3,1024]{1,0:T(4,128)S(1)}, u32[]{:S(2)}, u32[]{:S(2)}) %collective-permute-start.7) | collective-permute-done | bytes 12320 | tf_op jit(solution)/shard_map/ppermute | solution.py:555
  24.9 0.8 %shard_map.105 = (f32[3,128]{1,0:T(4,128)}, f32[3,128]{1,0:T(4,128)}) custom-call(f32[16,1024]{1,0:T(8,128)S(1)} %get-tuple-element.28.near_row_ref.row_ref, f32[16,1024]{1,0:T(8,128)S(1)} %get-tuple-element.32.row_ref, f32[3,128]{1,0:T(4,128)S(1)} %get-tuple-element.44.segment_ref, f32[1,128]{1,0:T(1,128)S(1)} %get-tuple-element.45.chi_ref, ...), custom_call_target="tpu_custom_call" | custom-call | tf_op jit(solution)/shard_map/pallas_call | solution.py:533
  (2 shorter events, 0.0 us)
Async XLA Ops:
  1.6 5.7 %collective-permute-start = (f32[1,1,1280]{2,1,0:T(1,128)S(1)}, f32[1,1,1280]{2,1,0:T(1,128)S(1)}, u32[]{:S(2)}, u32[]{:S(2)}) collective-permute-start(f32[1,1,1280]{2,1,0:T(1,128)S(1)} %get-tuple-element.27.refs_0_), channel_id=1, source_target_pairs={{0,8},{2,10},{4,12},{6,14},{8,0},{10,2},{12,4},{14,6},{1,9},{3,11}... | collective-permute-start | bytes 15368 | tf_op jit(solution)/shard_map/ppermute | solution.py:578
  7.3 4.6 %collective-permute-start.3 = (f32[2,1,1280]{2,1,0:T(1,128)S(1)}, f32[2,1,1280]{2,1,0:T(1,128)S(1)}, u32[]{:S(2)}, u32[]{:S(2)}) collective-permute-start(f32[2,1,1280]{2,1,0:T(1,128)S(1)} %shard_map.96.refs_0_), channel_id=1, source_target_pairs={{0,6},{2,4},{4,2},{6,0},{8,14},{10,12},{12,10},{14,8},{1,7},{3,5},... | collective-permute-start | bytes 30728 | tf_op jit(solution)/shard_map/ppermute | solution.py:578
  10.2 3.7 %collective-permute-start.2 = (f32[2,1,1280]{2,1,0:T(1,128)S(1)}, f32[2,1,1280]{2,1,0:T(1,128)S(1)}, u32[]{:S(2)}, u32[]{:S(2)}) collective-permute-start(f32[2,1,1280]{2,1,0:T(1,128)S(1)} %shard_map.96.refs_0_), channel_id=1, source_target_pairs={{0,4},{2,6},{4,0},{6,2},{8,12},{10,14},{12,8},{14,10},{1,5},{3,7},... | collective-permute-start | bytes 30728 | tf_op jit(solution)/shard_map/ppermute | solution.py:578
  10.6 3.7 %collective-permute-start.1 = (f32[2,1,1280]{2,1,0:T(1,128)S(1)}, f32[2,1,1280]{2,1,0:T(1,128)S(1)}, u32[]{:S(2)}, u32[]{:S(2)}) collective-permute-start(f32[2,1,1280]{2,1,0:T(1,128)S(1)} %shard_map.96.refs_0_), channel_id=1, source_target_pairs={{0,2},{2,0},{4,6},{6,4},{8,10},{10,8},{12,14},{14,12},{1,3},{3,1},... | collective-permute-start | bytes 30728 | tf_op jit(solution)/shard_map/ppermute | solution.py:578
  14.3 1.7 %collective-permute-start.4 = (f32[8,1,1280]{2,1,0:T(1,128)S(1)}, f32[8,1,1280]{2,1,0:T(1,128)S(1)}, u32[]{:S(2)}, u32[]{:S(2)}) collective-permute-start(f32[8,1,1280]{2,1,0:T(1,128)S(1)} %shard_map.97.gathered_ref), channel_id=1, source_target_pairs={{0,1},{1,0},{2,3},{3,2},{4,5},{5,4},{6,7},{7,6},{8,9},{9,8},{10,11... | collective-permute-start | bytes 122888 | tf_op jit(solution)/shard_map/ppermute | solution.py:555
  17.6 2.1 %collective-permute-start.5 = (f32[3,1024]{1,0:T(4,128)S(1)}, f32[3,1024]{1,0:T(4,128)S(1)}, u32[]{:S(2)}, u32[]{:S(2)}) collective-permute-start(f32[3,1024]{1,0:T(4,128)S(1)} %get-tuple-element.34.field_ref.coil_ref), channel_id=1, source_target_pairs={{0,1},{1,0},{2,3},{3,2},{4,5},{5,4},{6,7},{7,6},{8,9},{9,8},{10,11... | collective-permute-start | bytes 36872 | tf_op jit(solution)/shard_map/ppermute | solution.py:555
  21.3 1.4 %collective-permute-start.6 = (f32[3,1024]{1,0:T(4,128)S(1)}, f32[3,1024]{1,0:T(4,128)S(1)}, u32[]{:S(2)}, u32[]{:S(2)}) collective-permute-start(f32[3,1024]{1,0:T(4,128)S(1)} %get-tuple-element.37.field_ref), channel_id=1, source_target_pairs={{0,1},{1,0},{2,3},{3,2},{4,5},{5,4},{6,7},{7,6},{8,9},{9,8},{10,11... | collective-permute-start | bytes 36872 | tf_op jit(solution)/shard_map/ppermute | solution.py:555
  23.5 1.4 %collective-permute-start.7 = (f32[3,1024]{1,0:T(4,128)S(1)}, f32[3,1024]{1,0:T(4,128)S(1)}, u32[]{:S(2)}, u32[]{:S(2)}) collective-permute-start(f32[3,1024]{1,0:T(4,128)S(1)} %get-tuple-element.49.field_ref), channel_id=1, source_target_pairs={{0,1},{1,0},{2,3},{3,2},{4,5},{5,4},{6,7},{7,6},{8,9},{9,8},{10,11... | collective-permute-start | bytes 36872 | tf_op jit(solution)/shard_map/ppermute | solution.py:555

commit v7 on v6

--- a/solution.py
+++ b/solution.py
@@ -165,13 +165,18 @@
 
 def split_rows(rows, split_ref):
     count = rows.shape[0]
-    for place, part in enumerate(bf16_parts(rows, 3)):
-        split_ref[place * count : (place + 1) * count, :] = part
+    parts = bf16_parts(rows, 3)
+    if count % 16 == 0:
+        for place, part in enumerate(parts):
+            split_ref[place * count : (place + 1) * count, :] = part
+    else:
+        parts = [part.astype(jnp.float32) for part in parts] + [jnp.zeros_like(rows)]
+        split_ref[...] = jnp.concatenate(parts, 0).astype(jnp.bfloat16)
 
 
 def joined(product):
-    count = product.shape[0] // 3
-    return product[:count] + product[count : 2 * count] + product[2 * count :]
+    count = product.shape[0] // 24 * 8
+    return product[:count] + product[count : 2 * count] + product[2 * count : 3 * count]
 
 
 def pick(table_ref, index):
@@ -271,7 +276,7 @@
 
 def coil_rows(segments):
     mx, my, mz, cx, cy, cz = [segments[k : k + 1] for k in range(6)]
-    blank = jnp.zeros((10, segments.shape[1]), jnp.float32)
+    blank = jnp.zeros((2, segments.shape[1]), jnp.float32)
     crossed = [cy * mz - cz * my, cz * mx - cx * mz, cx * my - cy * mx]
     return jnp.concatenate([cx, cy, cz] + crossed + [blank], 0)
 
@@ -450,19 +455,27 @@
     finish(near_row_ref, coil_ref, sums_ref[...] + sums, out_ref)
 
 
-def near_sweep_stage(row_ref, field_ref, first_ref, second_ref, *refs):
-    segment_refs, (sums_ref, segment_ref, split_ref) = refs[:-3], refs[-3:]
+def segment_sums(row_ref, factor_ref, rows_ref, width):
+    targets = square_factor(row_ref[8:16, :width])
+    parts = power_parts(squares(factor_ref[...], targets), 3)
+    return joined(times(rows_ref[...], parts))
+
+
+def near_sweep_stage(
+    row_ref,
+    field_ref,
+    first_ref,
+    second_ref,
+    factor_ref,
+    rows_ref,
+    sums_ref,
+    segment_sums_ref,
+    split_ref,
+):
     source_rows(row_ref, field_ref[...], split_ref)
     sums_ref[...] = apply(split_ref, [first_ref, second_ref])
-    factor_refs, split_refs = segment_refs[:2], segment_refs[2:]
-    own = row_ref[8:16, : segment_ref.shape[1]]
-    targets = square_factor(own)
-    sums = 0.0
-    for factor_ref, rows_ref in zip(factor_refs, split_refs):
-        parts = power_parts(squares(factor_ref[...], targets), 3)
-        sums = sums + joined(times(rows_ref[...], parts))
-    total = 2 * row_ref.shape[1]
-    segment_ref[...] = coil_field(sums, [own[k : k + 1] for k in range(3)], total)
+    width = segment_sums_ref.shape[1]
+    segment_sums_ref[...] = segment_sums(row_ref, factor_ref, rows_ref, width)
 
 
 def far_sweep_stage(
@@ -492,13 +505,21 @@
     row_ref,
     source_ref,
     field_ref,
+    factor_ref,
+    rows_ref,
+    segment_sums_ref,
     sums_ref,
+    segment_ref,
     split_ref,
 ):
     source_rows(row_ref, field_ref[...], split_ref)
-    targets = square_factor(row_ref[8:16, : sums_ref.shape[1]])
-    parts = power_parts(squares(source_ref[...], targets), 5)
+    width = sums_ref.shape[1]
+    own = row_ref[8:16, :width]
+    parts = power_parts(squares(source_ref[...], square_factor(own)), 5)
     sums_ref[...] = joined(times(split_ref[...], parts))
+    sums = segment_sums_ref[...] + segment_sums(row_ref, factor_ref, rows_ref, width)
+    total = 2 * row_ref.shape[1]
+    segment_ref[...] = coil_field(sums, [own[k : k + 1] for k in range(3)], total)
 
 
 def far_force_stage(
@@ -588,13 +609,13 @@
     far = swap(near)
     split_scratch = [pltpu.VMEM((48, half), bf16)]
     factor = shape(half, 64, kind=bf16)
-    split = shape(48, half, kind=bf16)
+    split = shape(32, half, kind=bf16)
     matrix = shape(half, half, kind=bf16)
     narrow = shape(half, width, kind=bf16)
     sums, field, row = shape(16, half), shape(3, half), shape(16, half)
     near_row, shift, near_segments, near_sources, targets, near_split, near_sums = call(
         near_coil_stage,
-        (row, shape(8, 128), factor, factor, shape(64, half, kind=bf16), split, sums),
+        (row, shape(8, 128), factor, factor, shape(64, half, kind=bf16), split, shape(8, half)),
         [],
         near,
     )
@@ -632,17 +653,15 @@
     )
     for sweep in range(1, ITERS):
         other = swap(own)
-        near_sums, segments = call(
+        near_sums, segment_part = call(
             near_sweep_stage,
-            (sums, shape(3, width)),
+            (sums, shape(8, width)),
             split_scratch,
             near_row,
             own,
             *near_parts,
             near_segments,
-            far_segments,
             near_split,
-            far_split,
         )
         own, *narrow_parts = call(
             far_sweep_stage,
@@ -657,13 +676,16 @@
             *far_parts,
         )
     other = swap(own)
-    near_sums = call(
+    near_sums, segments = call(
         near_force_stage,
-        shape(16, width),
+        (shape(16, width), shape(3, width)),
         split_scratch,
         near_row,
         near_sources,
         own,
+        far_segments,
+        far_split,
+        segment_part,
     )
     lorentz, moment = call(
         far_force_stage,

time: 25.9 us -> 25.6 us (0.988)
  no operation moved by 1% of the time
where the time goes in v7:
time: 25.6 us; the launch traced here: 25.4 us
  Pallas kernels  10.6 us (41%)
  starting transfers between devices  8.75 us (34%)
  waiting for transfers between devices  5.35 us (21%)
  between operations  0.71 us (3%)
    pallas_call x11, Pallas kernels, call(): pl.pallas_call(kernel, out_shape=outputs, scratch_shapes=scratch, compile...  10.6 us
    ppermute x4, starting transfers between devices, cross(): lax.ppermute(value, 'seg', [(k, k ^ flip) for k in range(blocks // 2)])  7.59 us
    ppermute x4, waiting for transfers between devices, cross(): lax.ppermute(value, 'seg', [(k, k ^ flip) for k in range(blocks // 2)])  5.06 us
    ppermute x4, starting transfers between devices, swap(): return lax.ppermute(field, 'yoke', [(0, 1), (1, 0)])  1.16 us
  transfers between devices with their start and end apart: 8, of which 5 were waited for; matrix products, arithmetic and copies ran while one was open for 0% of the time, Pallas kernels for 19%

profile of v7, /device:TPU:0, one launch (start us, length us, event | category | flops | bytes accessed | tf_op | source)
XLA Modules:
  0.0 25.4 jit_solution(3743393996094684339)
XLA Ops:
  0.6 1.0 %shard_map.95 = (f32[1,1,1280]{2,1,0:T(1,128)S(1)}, f32[1,128]{1,0:T(1,128)S(1)}) custom-call(f32[3,256]{1,0:T(4,128)} %refs_0_.1, f32[3,256]{1,0:T(4,128)} %refs_1_.1, s32[1,256]{1,0:T(1,128)} %bitcast.5, f32[1,256]{1,0:T(1,128)} %bitcast.6, f32[3,128]{1,0:T(4,128)} %refs_4_.1, f32[1,128]{1,0:T(1,128)} %bitcast.7, s32[1,128]{1,0:T(1,128)} %bitcast.8, ...), custom_call_target="tpu_custom_call" | custom-call | tf_op jit(solution)/shard_map/pallas_call | solution.py:554
  1.6 4.1 %collective-permute-start = (f32[1,1,1280]{2,1,0:T(1,128)S(1)}, f32[1,1,1280]{2,1,0:T(1,128)S(1)}, u32[]{:S(2)}, u32[]{:S(2)}) collective-permute-start(f32[1,1,1280]{2,1,0:T(1,128)S(1)} %get-tuple-element.29.refs_0_), channel_id=1, source_target_pairs={{0,8},{2,10},{4,12},{6,14},{8,0},{10,2},{12,4},{14,6},{1,9},{3,11}... | collective-permute-start | bytes 15368 | tf_op jit(solution)/shard_map/ppermute | solution.py:599
  5.7 1.6 %collective-permute-done.refs_1_ = f32[1,1,1280]{2,1,0:T(1,128)S(1)} collective-permute-done((f32[1,1,1280]{2,1,0:T(1,128)S(1)}, f32[1,1,1280]{2,1,0:T(1,128)S(1)}, u32[]{:S(2)}, u32[]{:S(2)}) %collective-permute-start) | collective-permute-done | bytes 5152 | tf_op jit(solution)/shard_map/ppermute | solution.py:599
  7.3 2.8 %collective-permute-start.3 = (f32[2,1,1280]{2,1,0:T(1,128)S(1)}, f32[2,1,1280]{2,1,0:T(1,128)S(1)}, u32[]{:S(2)}, u32[]{:S(2)}) collective-permute-start(f32[2,1,1280]{2,1,0:T(1,128)S(1)} %shard_map.96.refs_0_), channel_id=1, source_target_pairs={{0,6},{2,4},{4,2},{6,0},{8,14},{10,12},{12,10},{14,8},{1,7},{3,5},... | collective-permute-start | bytes 30728 | tf_op jit(solution)/shard_map/ppermute | solution.py:599
  10.2 0.4 %collective-permute-start.2 = (f32[2,1,1280]{2,1,0:T(1,128)S(1)}, f32[2,1,1280]{2,1,0:T(1,128)S(1)}, u32[]{:S(2)}, u32[]{:S(2)}) collective-permute-start(f32[2,1,1280]{2,1,0:T(1,128)S(1)} %shard_map.96.refs_0_), channel_id=1, source_target_pairs={{0,4},{2,6},{4,0},{6,2},{8,12},{10,14},{12,8},{14,10},{1,5},{3,7},... | collective-permute-start | bytes 30728 | tf_op jit(solution)/shard_map/ppermute | solution.py:599
  10.6 0.2 collective-permute-start.1
  10.8 1.1 %collective-permute-done.3.refs_3_ = f32[2,1,1280]{2,1,0:T(1,128)S(1)} collective-permute-done((f32[2,1,1280]{2,1,0:T(1,128)S(1)}, f32[2,1,1280]{2,1,0:T(1,128)S(1)}, u32[]{:S(2)}, u32[]{:S(2)}) %collective-permute-start.3) | collective-permute-done | bytes 10272 | tf_op jit(solution)/shard_map/ppermute | solution.py:599
  11.9 1.9 %collective-permute-done.2.refs_2_ = f32[2,1,1280]{2,1,0:T(1,128)S(1)} collective-permute-done((f32[2,1,1280]{2,1,0:T(1,128)S(1)}, f32[2,1,1280]{2,1,0:T(1,128)S(1)}, u32[]{:S(2)}, u32[]{:S(2)}) %collective-permute-start.2) | collective-permute-done | bytes 10272 | tf_op jit(solution)/shard_map/ppermute | solution.py:599
  13.8 0.4 %collective-permute-done.1.refs_1_ = f32[2,1,1280]{2,1,0:T(1,128)S(1)} collective-permute-done((f32[2,1,1280]{2,1,0:T(1,128)S(1)}, f32[2,1,1280]{2,1,0:T(1,128)S(1)}, u32[]{:S(2)}, u32[]{:S(2)}) %collective-permute-start.1) | collective-permute-done | bytes 10272 | tf_op jit(solution)/shard_map/ppermute | solution.py:599
  14.3 0.0 collective-permute-start.4
  14.3 1.6 %shard_map.98 = (f32[16,1024]{1,0:T(8,128)S(1)}, f32[8,128]{1,0:T(8,128)S(1)}, bf16[1024,64]{1,0:T(8,128)(2,1)S(1)}, bf16[1024,64]{1,0:T(8,128)(2,1)S(1)}, bf16[...) custom-call(f32[8,1,1280]{2,1,0:T(1,128)S(1)} %shard_map.97.gathered_ref), custom_call_target="tpu_custom_call" | custom-call | tf_op jit(solution)/shard_map/pallas_call | solution.py:554
  15.9 0.0 collective-permute-done.4.gathered_ref
  15.9 1.5 %shard_map.99 = (f32[16,1024]{1,0:T(8,128)S(1)}, bf16[1024,64]{1,0:T(8,128)(2,1)S(1)}, bf16[1024,64]{1,0:T(8,128)(2,1)S(1)}, bf16[32,1024]{1,0:T(8,128)(2,1)S(1)}, f32[3,1024]{1,0:T(4,128)S(1)}) custom-call(f32[8,1,1280]{2,1,0:T(1,128)S(1)} %collective-permute-done.4.gathered_ref, f32[16,1024]{1,0:T(8,128)S(1)} %get-tuple-element.30.near_row_ref.row_ref, ...), custom_call_target="tpu_custom_call" | custom-call | tf_op jit(solution)/shard_map/pallas_call | solution.py:554
  17.5 0.6 %collective-permute-start.5 = (f32[3,1024]{1,0:T(4,128)S(1)}, f32[3,1024]{1,0:T(4,128)S(1)}, u32[]{:S(2)}, u32[]{:S(2)}) collective-permute-start(f32[3,1024]{1,0:T(4,128)S(1)} %get-tuple-element.37.field_ref.coil_ref), channel_id=1, source_target_pairs={{0,1},{1,0},{2,3},{3,2},{4,5},{5,4},{6,7},{7,6},{8,9},{9,8},{10,11... | collective-permute-start | bytes 36872 | tf_op jit(solution)/shard_map/ppermute | solution.py:576
  18.1 1.5 %shard_map.100 = (f32[16,1024]{1,0:T(8,128)S(1)}, bf16[1024,1024]{1,0:T(8,128)(2,1)S(1)}, bf16[1024,1024]{1,0:T(8,128)(2,1)S(1)}) custom-call(f32[16,1024]{1,0:T(8,128)S(1)} %get-tuple-element.30.near_row_ref.row_ref, bf16[1024,64]{1,0:T(8,128)(2,1)S(1)} %get-tuple-element.35.source_ref, bf16[64,1024]{1,0:T(8,128)(2,1)S(1)} %get-tuple-element.32.target_factor_ref.target_ref, ...), custom_call_target="tpu_custom_call" | custom-call | tf_op jit(solution)/shard_map/pallas_call | solution.py:554
  19.6 0.0 collective-permute-done.5.other_ref
  19.6 1.6 %shard_map.101 = (f32[3,1024]{1,0:T(4,128)S(1)}, bf16[1024,1024]{1,0:T(8,128)(2,1)S(1)}, bf16[1024,1024]{1,0:T(8,128)(2,1)S(1)}) custom-call(f32[16,1024]{1,0:T(8,128)S(1)} %get-tuple-element.30.near_row_ref.row_ref, f32[16,1024]{1,0:T(8,128)S(1)} %get-tuple-element.34.row_ref, bf16[1024,64]{1,0:T(8,128)(2,1)S(1)} %get-tuple-element.36.source_ref, ...), custom_call_target="tpu_custom_call" | custom-call | tf_op jit(solution)/shard_map/pallas_call | solution.py:554
  21.2 0.1 collective-permute-start.6
  21.3 1.1 %shard_map.102 = (f32[16,1024]{1,0:T(8,128)S(1)}, f32[8,128]{1,0:T(8,128)S(1)}) custom-call(f32[16,1024]{1,0:T(8,128)S(1)} %get-tuple-element.30.near_row_ref.row_ref, f32[3,1024]{1,0:T(4,128)S(1)} %get-tuple-element.39.field_ref, bf16[1024,1024]{1,0:T(8,128)(2,1)S(1)} %get-tuple-element.40.first_ref, bf16[1024,1024]{1,0:T(8,128)(2,1)S(1)} %get-tuple-element.41.second_ref, ...), custom_call_target="tpu_custom_call" | custom-call | tf_op jit(solution)/shard_map/pallas_call | solution.py:554
  22.4 0.0 collective-permute-done.6.other_ref
  22.4 0.8 %shard_map.103 = (f32[3,1024]{1,0:T(4,128)S(1)}, bf16[1024,128]{1,0:T(8,128)(2,1)S(1)}, bf16[1024,128]{1,0:T(8,128)(2,1)S(1)}) custom-call(f32[16,1024]{1,0:T(8,128)S(1)} %get-tuple-element.30.near_row_ref.row_ref, f32[16,1024]{1,0:T(8,128)S(1)} %get-tuple-element.34.row_ref, bf16[1024,64]{1,0:T(8,128)(2,1)S(1)} %get-tuple-element.36.source_ref, ...), custom_call_target="tpu_custom_call" | custom-call | tf_op jit(solution)/shard_map/pallas_call | solution.py:554
  23.2 0.5 %collective-permute-start.7 = (f32[3,1024]{1,0:T(4,128)S(1)}, f32[3,1024]{1,0:T(4,128)S(1)}, u32[]{:S(2)}, u32[]{:S(2)}) collective-permute-start(f32[3,1024]{1,0:T(4,128)S(1)} %get-tuple-element.47.field_ref), channel_id=1, source_target_pairs={{0,1},{1,0},{2,3},{3,2},{4,5},{5,4},{6,7},{7,6},{8,9},{9,8},{10,11... | collective-permute-start | bytes 36872 | tf_op jit(solution)/shard_map/ppermute | solution.py:576
  23.7 0.6 %shard_map.104 = (f32[16,128]{1,0:T(8,128)S(1)}, f32[3,128]{1,0:T(4,128)S(1)}) custom-call(f32[16,1024]{1,0:T(8,128)S(1)} %get-tuple-element.30.near_row_ref.row_ref, bf16[1024,64]{1,0:T(8,128)(2,1)S(1)} %get-tuple-element.35.source_ref, f32[3,1024]{1,0:T(4,128)S(1)} %get-tuple-element.47.field_ref, bf16[1024,64]{1,0:T(8,128)(2,1)S(1)} %get-tuple-element.48.factor_ref, ...), custom_call_target="tpu_custom_call" | custom-call | tf_op jit(solution)/shard_map/pallas_call | solution.py:554
  24.4 0.2 collective-permute-done.7.other_ref
  24.6 0.8 %shard_map.105 = (f32[3,128]{1,0:T(4,128)}, f32[3,128]{1,0:T(4,128)}) custom-call(f32[16,1024]{1,0:T(8,128)S(1)} %get-tuple-element.30.near_row_ref.row_ref, f32[16,1024]{1,0:T(8,128)S(1)} %get-tuple-element.34.row_ref, f32[3,128]{1,0:T(4,128)S(1)} %get-tuple-element.51.segment_ref, f32[1,128]{1,0:T(1,128)S(1)} %get-tuple-element.52.chi_ref, ...), custom_call_target="tpu_custom_call" | custom-call | tf_op jit(solution)/shard_map/pallas_call | solution.py:554
  (2 shorter events, 0.0 us)
Async XLA Ops:
  1.6 5.7 %collective-permute-start = (f32[1,1,1280]{2,1,0:T(1,128)S(1)}, f32[1,1,1280]{2,1,0:T(1,128)S(1)}, u32[]{:S(2)}, u32[]{:S(2)}) collective-permute-start(f32[1,1,1280]{2,1,0:T(1,128)S(1)} %get-tuple-element.29.refs_0_), channel_id=1, source_target_pairs={{0,8},{2,10},{4,12},{6,14},{8,0},{10,2},{12,4},{14,6},{1,9},{3,11}... | collective-permute-start | bytes 15368 | tf_op jit(solution)/shard_map/ppermute | solution.py:599
  7.3 4.6 %collective-permute-start.3 = (f32[2,1,1280]{2,1,0:T(1,128)S(1)}, f32[2,1,1280]{2,1,0:T(1,128)S(1)}, u32[]{:S(2)}, u32[]{:S(2)}) collective-permute-start(f32[2,1,1280]{2,1,0:T(1,128)S(1)} %shard_map.96.refs_0_), channel_id=1, source_target_pairs={{0,6},{2,4},{4,2},{6,0},{8,14},{10,12},{12,10},{14,8},{1,7},{3,5},... | collective-permute-start | bytes 30728 | tf_op jit(solution)/shard_map/ppermute | solution.py:599
  10.2 3.7 %collective-permute-start.2 = (f32[2,1,1280]{2,1,0:T(1,128)S(1)}, f32[2,1,1280]{2,1,0:T(1,128)S(1)}, u32[]{:S(2)}, u32[]{:S(2)}) collective-permute-start(f32[2,1,1280]{2,1,0:T(1,128)S(1)} %shard_map.96.refs_0_), channel_id=1, source_target_pairs={{0,4},{2,6},{4,0},{6,2},{8,12},{10,14},{12,8},{14,10},{1,5},{3,7},... | collective-permute-start | bytes 30728 | tf_op jit(solution)/shard_map/ppermute | solution.py:599
  10.6 3.7 %collective-permute-start.1 = (f32[2,1,1280]{2,1,0:T(1,128)S(1)}, f32[2,1,1280]{2,1,0:T(1,128)S(1)}, u32[]{:S(2)}, u32[]{:S(2)}) collective-permute-start(f32[2,1,1280]{2,1,0:T(1,128)S(1)} %shard_map.96.refs_0_), channel_id=1, source_target_pairs={{0,2},{2,0},{4,6},{6,4},{8,10},{10,8},{12,14},{14,12},{1,3},{3,1},... | collective-permute-start | bytes 30728 | tf_op jit(solution)/shard_map/ppermute | solution.py:599
  14.3 1.6 %collective-permute-start.4 = (f32[8,1,1280]{2,1,0:T(1,128)S(1)}, f32[8,1,1280]{2,1,0:T(1,128)S(1)}, u32[]{:S(2)}, u32[]{:S(2)}) collective-permute-start(f32[8,1,1280]{2,1,0:T(1,128)S(1)} %shard_map.97.gathered_ref), channel_id=1, source_target_pairs={{0,1},{1,0},{2,3},{3,2},{4,5},{5,4},{6,7},{7,6},{8,9},{9,8},{10,11... | collective-permute-start | bytes 122888 | tf_op jit(solution)/shard_map/ppermute | solution.py:576
  17.5 2.1 %collective-permute-start.5 = (f32[3,1024]{1,0:T(4,128)S(1)}, f32[3,1024]{1,0:T(4,128)S(1)}, u32[]{:S(2)}, u32[]{:S(2)}) collective-permute-start(f32[3,1024]{1,0:T(4,128)S(1)} %get-tuple-element.37.field_ref.coil_ref), channel_id=1, source_target_pairs={{0,1},{1,0},{2,3},{3,2},{4,5},{5,4},{6,7},{7,6},{8,9},{9,8},{10,11... | collective-permute-start | bytes 36872 | tf_op jit(solution)/shard_map/ppermute | solution.py:576
  21.2 1.2 %collective-permute-start.6 = (f32[3,1024]{1,0:T(4,128)S(1)}, f32[3,1024]{1,0:T(4,128)S(1)}, u32[]{:S(2)}, u32[]{:S(2)}) collective-permute-start(f32[3,1024]{1,0:T(4,128)S(1)} %get-tuple-element.39.field_ref), channel_id=1, source_target_pairs={{0,1},{1,0},{2,3},{3,2},{4,5},{5,4},{6,7},{7,6},{8,9},{9,8},{10,11... | collective-permute-start | bytes 36872 | tf_op jit(solution)/shard_map/ppermute | solution.py:576
  23.2 1.3 %collective-permute-start.7 = (f32[3,1024]{1,0:T(4,128)S(1)}, f32[3,1024]{1,0:T(4,128)S(1)}, u32[]{:S(2)}, u32[]{:S(2)}) collective-permute-start(f32[3,1024]{1,0:T(4,128)S(1)} %get-tuple-element.47.field_ref), channel_id=1, source_target_pairs={{0,1},{1,0},{2,3},{3,2},{4,5},{5,4},{6,7},{7,6},{8,9},{9,8},{10,11... | collective-permute-start | bytes 36872 | tf_op jit(solution)/shard_map/ppermute | solution.py:576
